TPU v7x, 32 devices: a whole 2x2x4 slice. The times are simulated.
32 devices in a mesh: fsdp: 2 (over x), ctx: 4 (over y, core), tp: 4 (over z).
Axes of the slice: x: 2, y: 2, z: 4, core: 2. Of those that a mesh axis runs over, the one named last changes fastest.
Arguments:
- tokens: bfloat16 [4, 2048, 1024], P('fsdp', ('ctx', 'tp')), may hold values from -6 to 6
- enc_states: bfloat16 [4, 256, 1024], P('fsdp', ('ctx', 'tp')), may hold values from -6 to 6
- enc_lengths: int32 [4], P('fsdp'), may hold values from 128 to 256, as said below
- cotangent: bfloat16 [4, 2048, 1024], P('fsdp', ('ctx', 'tp')), may hold values from -6 to 6
- gain_self: float32 [1024], replicated, may hold values from 0.25 to 1.75
- shift_self: float32 [1024], replicated, may hold values from -1.5 to 1.5
- w_query: bfloat16 [1024, 1024], P('fsdp', 'tp'), may hold values from -0.09375 to 0.09375
- w_key: bfloat16 [1024, 1024], P('fsdp', 'tp'), may hold values from -0.09375 to 0.09375
- w_value: bfloat16 [1024, 1024], P('fsdp', 'tp'), may hold values from -0.1875 to 0.1875
- w_out: bfloat16 [1024, 1024], P('tp', 'fsdp'), may hold values from -0.75 to 0.75
- gain_cross: float32 [1024], replicated, may hold values from 0.25 to 1.75
- shift_cross: float32 [1024], replicated, may hold values from -1.5 to 1.5
- cross_query: bfloat16 [1024, 1024], P('fsdp', 'tp'), may hold values from -0.09375 to 0.09375
- cross_key: bfloat16 [1024, 1024], P('fsdp', 'tp'), may hold values from -0.09375 to 0.09375
- cross_value: bfloat16 [1024, 1024], P('fsdp', 'tp'), may hold values from -0.1875 to 0.1875
- cross_out: bfloat16 [1024, 1024], P('tp', 'fsdp'), may hold values from -0.75 to 0.75
- gain_ffn: float32 [1024], replicated, may hold values from 0.25 to 1.75
- shift_ffn: float32 [1024], replicated, may hold values from -1.5 to 1.5
- w_inner: bfloat16 [1024, 4096], P('fsdp', 'tp'), may hold values from -0.1875 to 0.1875
- w_outer: bfloat16 [4096, 1024], P('tp', 'fsdp'), may hold values from -0.09375 to 0.09375
Outputs:
- out_tokens: bfloat16 [4, 2048, 1024], P('fsdp', ('ctx', 'tp'))
- grad_tokens: float32 [4, 2048, 1024], P('fsdp', ('ctx', 'tp'))
- grad_enc: float32 [4, 256, 1024], P('fsdp', ('ctx', 'tp'))
- grad_gain_self: float32 [1024], replicated
- grad_shift_self: float32 [1024], replicated
- grad_query: float32 [1024, 1024], P('fsdp', 'tp')
- grad_key: float32 [1024, 1024], P('fsdp', 'tp')
- grad_value: float32 [1024, 1024], P('fsdp', 'tp')
- grad_w_out: float32 [1024, 1024], P('tp', 'fsdp')
- grad_gain_cross: float32 [1024], replicated
- grad_shift_cross: float32 [1024], replicated
- grad_cross_query: float32 [1024, 1024], P('fsdp', 'tp')
- grad_cross_key: float32 [1024, 1024], P('fsdp', 'tp')
- grad_cross_value: float32 [1024, 1024], P('fsdp', 'tp')
- grad_cross_out: float32 [1024, 1024], P('tp', 'fsdp')
- grad_gain_ffn: float32 [1024], replicated
- grad_shift_ffn: float32 [1024], replicated
- grad_inner: float32 [1024, 4096], P('fsdp', 'tp')
- grad_outer: float32 [4096, 1024], P('tp', 'fsdp')
Inputs may be any that keep to these rules, and one draw needn't show every extreme that they name: `enc_lengths`: some sequence has all 256 encoder states valid in every draw.
All inputs are finite; a program needn't handle non-finite values.
Results may differ from a plain program's by a relative error of at most 0.023.
Values may be sent and summed in bfloat16 or wider, within the bound.
No kernel may reach another device: no remote copies, remote signals or barrier semaphores. Data moves between devices by JAX's collectives and lax.ppermute only.
A program may use at most 256 MiB of HBM per device.

v0:
```python
import jax
import jax.numpy as jnp
from jax import lax
from jax.sharding import PartitionSpec as P

HEAD_DIM = 64


def layer_norm(hidden, gain, shift):
    centre = hidden - jnp.mean(hidden, axis=-1, keepdims=True)
    spread = jnp.mean(centre * centre, axis=-1, keepdims=True)
    return centre * lax.rsqrt(spread + 1e-05) * gain + shift


def gelu_tanh(value):
    return 0.5 * value * (1.0 + jnp.tanh(0.7978845608 * (value + 0.044715 * value * value * value)))


def project(rows_in, weight):
    return jnp.einsum("std,de->ste", rows_in, weight, preferred_element_type=jnp.float32)


def project_back(grad_rows, weight):
    return jnp.einsum("ste,de->std", grad_rows, weight, preferred_element_type=jnp.float32)


def weight_grad(rows_in, grad_rows):
    return jnp.einsum("std,ste->de", rows_in, grad_rows, preferred_element_type=jnp.float32)


def split_heads(matrix):
    return matrix.reshape(matrix.shape[0], matrix.shape[1], matrix.shape[2] // HEAD_DIM, HEAD_DIM)


def join_heads(matrix):
    return matrix.reshape(matrix.shape[0], matrix.shape[1], matrix.shape[2] * matrix.shape[3])


def score_rows(queries, keys_in, allowed):
    scores = jnp.einsum(
        "sqhd,skhd->shqk",
        split_heads(queries),
        split_heads(keys_in),
        preferred_element_type=jnp.float32,
    ) * HEAD_DIM ** (-0.5)
    scores = jnp.where(allowed[:, None], scores, -1000000000.0)
    row_top = jnp.max(scores, axis=-1, keepdims=True)
    exponent = jnp.exp(scores - row_top)
    return exponent / jnp.sum(exponent, axis=-1, keepdims=True)


def attend(queries, keys_in, values_in, allowed):
    probs = score_rows(queries, keys_in, allowed)
    mixed = jnp.einsum(
        "shqk,skhd->sqhd",
        probs.astype(jnp.bfloat16),
        split_heads(values_in),
        preferred_element_type=jnp.float32,
    )
    return join_heads(mixed).astype(jnp.bfloat16)


def attend_back(queries, keys_in, values_in, allowed, grad_mixed):
    probs = score_rows(queries, keys_in, allowed)
    grad_heads = split_heads(grad_mixed)
    grad_probs = jnp.einsum(
        "sqhd,skhd->shqk", grad_heads, split_heads(values_in), preferred_element_type=jnp.float32
    )
    grad_values = jnp.einsum(
        "shqk,sqhd->skhd",
        probs.astype(jnp.bfloat16),
        grad_heads,
        preferred_element_type=jnp.float32,
    )
    grad_scores = (
        probs * (grad_probs - jnp.sum(probs * grad_probs, axis=-1, keepdims=True))
    ).astype(jnp.bfloat16)
    scale = HEAD_DIM ** (-0.5)
    grad_queries = (
        jnp.einsum(
            "shqk,skhd->sqhd", grad_scores, split_heads(keys_in), preferred_element_type=jnp.float32
        )
        * scale
    )
    grad_keys = (
        jnp.einsum(
            "shqk,sqhd->skhd", grad_scores, split_heads(queries), preferred_element_type=jnp.float32
        )
        * scale
    )
    return (join_heads(grad_queries), join_heads(grad_keys), join_heads(grad_values))


def gather_rows(value):
    return lax.all_gather(value, "tp", axis=1, tiled=True)


def sum_rows(value):
    return lax.psum_scatter(
        value.astype(jnp.bfloat16), "tp", scatter_dimension=1, tiled=True
    ).astype(jnp.float32)


def sum_keys(first, second):
    total_first, total_second = (
        lax.psum_scatter(first.astype(jnp.bfloat16), "ctx", scatter_dimension=1, tiled=True).astype(
            jnp.float32
        ),
        lax.psum_scatter(
            second.astype(jnp.bfloat16), "ctx", scatter_dimension=1, tiled=True
        ).astype(jnp.float32),
    )
    return (total_first.astype(jnp.bfloat16), total_second.astype(jnp.bfloat16))


def shards(
    tokens,
    enc_states,
    enc_lengths,
    cotangent,
    gain_self,
    shift_self,
    w_query,
    w_key,
    w_value,
    w_out,
    gain_cross,
    shift_cross,
    cross_query,
    cross_key,
    cross_value,
    cross_out,
    gain_ffn,
    shift_ffn,
    w_inner,
    w_outer,
):
    g_query, g_key, g_value, g_cquery, g_ckey, g_cvalue, g_inner, g_out, g_cout, g_outer = (
        lax.all_gather(w_query, "fsdp", axis=0, tiled=True),
        lax.all_gather(w_key, "fsdp", axis=0, tiled=True),
        lax.all_gather(w_value, "fsdp", axis=0, tiled=True),
        lax.all_gather(cross_query, "fsdp", axis=0, tiled=True),
        lax.all_gather(cross_key, "fsdp", axis=0, tiled=True),
        lax.all_gather(cross_value, "fsdp", axis=0, tiled=True),
        lax.all_gather(w_inner, "fsdp", axis=0, tiled=True),
        lax.all_gather(w_out, "fsdp", axis=1, tiled=True),
        lax.all_gather(cross_out, "fsdp", axis=1, tiled=True),
        lax.all_gather(w_outer, "fsdp", axis=1, tiled=True),
    )
    span_rows = tokens.shape[1] * lax.axis_size("tp")
    first_pos = lax.axis_index("ctx") * span_rows
    key_count = span_rows * lax.axis_size("ctx")
    positions = first_pos + jnp.arange(span_rows)
    causal = (positions[:, None] >= jnp.arange(key_count)[None, :])[None]
    enc_count = enc_states.shape[1] * lax.axis_size("ctx") * lax.axis_size("tp")
    reach = jnp.arange(enc_count)[None, None, :] < enc_lengths[:, None, None]
    hidden0 = tokens.astype(jnp.float32)
    rows1 = gather_rows(layer_norm(hidden0, gain_self, shift_self).astype(jnp.bfloat16))
    q_self = project(rows1, g_query).astype(jnp.bfloat16)
    k_self = project(rows1, g_key).astype(jnp.bfloat16)
    v_self = project(rows1, g_value).astype(jnp.bfloat16)
    k_all, v_all = (
        lax.all_gather(k_self, "ctx", axis=1, tiled=True),
        lax.all_gather(v_self, "ctx", axis=1, tiled=True),
    )
    o_self = attend(q_self, k_all, v_all, causal)
    hidden1 = hidden0 + sum_rows(project(o_self, g_out))
    rows2 = gather_rows(layer_norm(hidden1, gain_cross, shift_cross).astype(jnp.bfloat16))
    q_cross = project(rows2, g_cquery).astype(jnp.bfloat16)
    enc_all = lax.all_gather(enc_states, ("ctx", "tp"), axis=1, tiled=True)
    k_cross = project(enc_all, g_ckey).astype(jnp.bfloat16)
    v_cross = project(enc_all, g_cvalue).astype(jnp.bfloat16)
    o_cross = attend(q_cross, k_cross, v_cross, reach)
    hidden2 = hidden1 + sum_rows(project(o_cross, g_cout))
    rows3 = gather_rows(layer_norm(hidden2, gain_ffn, shift_ffn).astype(jnp.bfloat16))
    inner = project(rows3, g_inner)
    active_full, pull_gelu = jax.vjp(gelu_tanh, inner)
    active = active_full.astype(jnp.bfloat16)
    hidden3 = hidden2 + sum_rows(project(active, g_outer))
    out_tokens = hidden3.astype(jnp.bfloat16)
    grad3 = cotangent.astype(jnp.float32)
    dy_ffn = gather_rows(grad3.astype(jnp.bfloat16))
    d_active = project_back(dy_ffn, g_outer)
    d_inner = pull_gelu(d_active)[0].astype(jnp.bfloat16)
    grad_outer = weight_grad(active, dy_ffn)
    grad_inner = weight_grad(rows3, d_inner)
    d_normed3 = sum_rows(project_back(d_inner, g_inner))
    pull_ffn = jax.vjp(layer_norm, hidden2, gain_ffn, shift_ffn)[1]
    back_ffn, grad_gain_ffn, grad_shift_ffn = pull_ffn(d_normed3)
    grad2 = grad3 + back_ffn
    dy_cross = gather_rows(grad2.astype(jnp.bfloat16))
    do_cross = project_back(dy_cross, g_cout).astype(jnp.bfloat16)
    grad_cout = weight_grad(o_cross, dy_cross)
    dq_cross, dk_cross, dv_cross = attend_back(q_cross, k_cross, v_cross, reach, do_cross)
    dq_cross = dq_cross.astype(jnp.bfloat16)
    dk_cross, dv_cross = sum_keys(dk_cross, dv_cross)
    grad_cquery = weight_grad(rows2, dq_cross)
    enc_part = lax.dynamic_slice_in_dim(
        enc_all, lax.axis_index("ctx") * dk_cross.shape[1], dk_cross.shape[1], 1
    )
    grad_ckey = weight_grad(enc_part, dk_cross)
    grad_cvalue = weight_grad(enc_part, dv_cross)
    grad_enc = sum_rows(project_back(dk_cross, g_ckey) + project_back(dv_cross, g_cvalue))
    d_normed2 = sum_rows(project_back(dq_cross, g_cquery))
    pull_cross = jax.vjp(layer_norm, hidden1, gain_cross, shift_cross)[1]
    back_cross, grad_gain_cross, grad_shift_cross = pull_cross(d_normed2)
    grad1 = grad2 + back_cross
    dy_self = gather_rows(grad1.astype(jnp.bfloat16))
    do_self = project_back(dy_self, g_out).astype(jnp.bfloat16)
    grad_out = weight_grad(o_self, dy_self)
    dq_self, dk_self, dv_self = attend_back(q_self, k_all, v_all, causal, do_self)
    dq_self = dq_self.astype(jnp.bfloat16)
    dk_self, dv_self = sum_keys(dk_self, dv_self)
    grad_query = weight_grad(rows1, dq_self)
    grad_key = weight_grad(rows1, dk_self)
    grad_value = weight_grad(rows1, dv_self)
    d_normed1 = sum_rows(
        project_back(dq_self, g_query)
        + project_back(dk_self, g_key)
        + project_back(dv_self, g_value)
    )
    pull_self = jax.vjp(layer_norm, hidden0, gain_self, shift_self)[1]
    back_self, grad_gain_self, grad_shift_self = pull_self(d_normed1)
    grad_tokens = grad1 + back_self
    (
        grad_gain_self,
        grad_shift_self,
        grad_gain_cross,
        grad_shift_cross,
        grad_gain_ffn,
        grad_shift_ffn,
    ) = lax.psum(
        (
            grad_gain_self,
            grad_shift_self,
            grad_gain_cross,
            grad_shift_cross,
            grad_gain_ffn,
            grad_shift_ffn,
        ),
        ("fsdp", "ctx", "tp"),
    )
    s_query, s_key, s_value, s_cquery, s_ckey, s_cvalue, s_inner, s_out, s_cout, s_outer = (
        lax.psum_scatter(
            grad_query.astype(jnp.bfloat16), "fsdp", scatter_dimension=0, tiled=True
        ).astype(jnp.float32),
        lax.psum_scatter(
            grad_key.astype(jnp.bfloat16), "fsdp", scatter_dimension=0, tiled=True
        ).astype(jnp.float32),
        lax.psum_scatter(
            grad_value.astype(jnp.bfloat16), "fsdp", scatter_dimension=0, tiled=True
        ).astype(jnp.float32),
        lax.psum_scatter(
            grad_cquery.astype(jnp.bfloat16), "fsdp", scatter_dimension=0, tiled=True
        ).astype(jnp.float32),
        lax.psum_scatter(
            grad_ckey.astype(jnp.bfloat16), "fsdp", scatter_dimension=0, tiled=True
        ).astype(jnp.float32),
        lax.psum_scatter(
            grad_cvalue.astype(jnp.bfloat16), "fsdp", scatter_dimension=0, tiled=True
        ).astype(jnp.float32),
        lax.psum_scatter(
            grad_inner.astype(jnp.bfloat16), "fsdp", scatter_dimension=0, tiled=True
        ).astype(jnp.float32),
        lax.psum_scatter(
            grad_out.astype(jnp.bfloat16), "fsdp", scatter_dimension=1, tiled=True
        ).astype(jnp.float32),
        lax.psum_scatter(
            grad_cout.astype(jnp.bfloat16), "fsdp", scatter_dimension=1, tiled=True
        ).astype(jnp.float32),
        lax.psum_scatter(
            grad_outer.astype(jnp.bfloat16), "fsdp", scatter_dimension=1, tiled=True
        ).astype(jnp.float32),
    )
    s_query, s_key, s_value, s_cquery, s_ckey, s_cvalue, s_inner, s_out, s_cout, s_outer = (
        lax.psum(s_query.astype(jnp.bfloat16), "ctx").astype(jnp.float32),
        lax.psum(s_key.astype(jnp.bfloat16), "ctx").astype(jnp.float32),
        lax.psum(s_value.astype(jnp.bfloat16), "ctx").astype(jnp.float32),
        lax.psum(s_cquery.astype(jnp.bfloat16), "ctx").astype(jnp.float32),
        lax.psum(s_ckey.astype(jnp.bfloat16), "ctx").astype(jnp.float32),
        lax.psum(s_cvalue.astype(jnp.bfloat16), "ctx").astype(jnp.float32),
        lax.psum(s_inner.astype(jnp.bfloat16), "ctx").astype(jnp.float32),
        lax.psum(s_out.astype(jnp.bfloat16), "ctx").astype(jnp.float32),
        lax.psum(s_cout.astype(jnp.bfloat16), "ctx").astype(jnp.float32),
        lax.psum(s_outer.astype(jnp.bfloat16), "ctx").astype(jnp.float32),
    )
    return (
        out_tokens,
        grad_tokens,
        grad_enc,
        grad_gain_self,
        grad_shift_self,
        s_query,
        s_key,
        s_value,
        s_out,
        grad_gain_cross,
        grad_shift_cross,
        s_cquery,
        s_ckey,
        s_cvalue,
        s_cout,
        grad_gain_ffn,
        grad_shift_ffn,
        s_inner,
        s_outer,
    )


def solution(mesh):
    in_specs = (
        P("fsdp", ("ctx", "tp"), None),
        P("fsdp", ("ctx", "tp"), None),
        P("fsdp"),
        P("fsdp", ("ctx", "tp"), None),
        P(),
        P(),
        P("fsdp", "tp"),
        P("fsdp", "tp"),
        P("fsdp", "tp"),
        P("tp", "fsdp"),
        P(),
        P(),
        P("fsdp", "tp"),
        P("fsdp", "tp"),
        P("fsdp", "tp"),
        P("tp", "fsdp"),
        P(),
        P(),
        P("fsdp", "tp"),
        P("tp", "fsdp"),
    )
    out_specs = (
        P("fsdp", ("ctx", "tp"), None),
        P("fsdp", ("ctx", "tp"), None),
        P("fsdp", ("ctx", "tp"), None),
        P(),
        P(),
        P("fsdp", "tp"),
        P("fsdp", "tp"),
        P("fsdp", "tp"),
        P("tp", "fsdp"),
        P(),
        P(),
        P("fsdp", "tp"),
        P("fsdp", "tp"),
        P("fsdp", "tp"),
        P("tp", "fsdp"),
        P(),
        P(),
        P("fsdp", "tp"),
        P("tp", "fsdp"),
    )
    return jax.shard_map(shards, mesh=mesh, in_specs=in_specs, out_specs=out_specs, check_vma=False)
```

profile of v0, /device:TPU:0, one launch (start us, length us, event | category | flops | bytes accessed | tf_op | source)
XLA Modules:
  0.0 1250.9 jit_solution(2573071129623997982)
XLA Ops:
  23.2 38.5 %all-gather.12.cloned.1.call-done = bf16[2,512,1024]{2,1,0:T(8,128)(2,1)} async-done(((bf16[2,128,1024]{2,1,0:T(8,128)(2,1)}), bf16[2,512,1024]{2,1,0:T(8,128)(2,1)}) %all-gather.12.cloned.1.call-update) | async-done | bytes 2097168 | tf_op jit(solution)/shard_map/all_gather | solution.py:95
  99.1 17.6 %fusion.114 = (f32[2,4,512]{2,1,0:T(4,128)S(1)}, f32[2,4,512,2048]{3,2,1,0:T(8,128)}) fusion(pred[512,2048]{1,0:T(8,128)(4,1)} %iota_compare_fusion, bf16[2,512,4,64]{1,3,2,0:T(8,128)(2,1)S(1)} %bitcast.197, bf16[2,2048,4,64]{1,3,2,0:T(8,128)(2,1)S(1)} %bitcast.186), kind=kOutput, calls=%fused_computation.187 | convolution fusion | flops 1107298304 | bytes 37240832 | tf_op jit(solution)/shard_map/sub | solution.py:48
  138.5 44.3 %reduce-scatter.22.cloned.1.call-done = bf16[2,128,1024]{2,1,0:T(8,128)(2,1)} async-done(((bf16[2,512,1024]{2,1,0:T(8,128)(2,1)}), bf16[2,128,1024]{2,1,0:T(8,128)(2,1)}) %reduce-scatter.22.cloned.1.call-update) | async-done | bytes 524304 | tf_op jit(solution)/shard_map/reduce_scatter | solution.py:99
  223.3 25.0 %all-gather.20.cloned.1.call-done = bf16[2,512,1024]{2,1,0:T(8,128)(2,1)} async-done(((bf16[2,128,1024]{2,1,0:T(8,128)(2,1)}), bf16[2,512,1024]{2,1,0:T(8,128)(2,1)}) %all-gather.20.cloned.1.call-update) | async-done | bytes 2097168 | tf_op jit(solution)/shard_map/all_gather | solution.py:95
  260.7 41.6 %reduce-scatter.24.cloned.1.call-done = bf16[2,128,1024]{2,1,0:T(8,128)(2,1)} async-done(((bf16[2,512,1024]{2,1,0:T(8,128)(2,1)}), bf16[2,128,1024]{2,1,0:T(8,128)(2,1)}) %reduce-scatter.24.cloned.1.call-update) | async-done | bytes 524304 | tf_op jit(solution)/shard_map/reduce_scatter | solution.py:99
  306.4 29.7 %all-gather.24.cloned.1.call-done = bf16[1024,1024]{1,0:T(8,128)(2,1)} async-done(((bf16[512,1024]{1,0:T(8,128)(2,1)}), bf16[1024,1024]{1,0:T(8,128)(2,1)}) %all-gather.24.cloned.1.call-update) | async-done | bytes 2097168 | tf_op jit(solution)/shard_map/all_gather | solution.py:145
  336.0 47.8 %all-gather.22.cloned.1.call-done = bf16[2,512,1024]{2,1,0:T(8,128)(2,1)} async-done(((bf16[2,128,1024]{2,1,0:T(8,128)(2,1)}), bf16[2,512,1024]{2,1,0:T(8,128)(2,1)}) %all-gather.22.cloned.1.call-update) | async-done | bytes 2097168 | tf_op jit(solution)/shard_map/all_gather | solution.py:95
  390.3 26.8 %all-gather.26.cloned.1.call-done = bf16[1024,1024]{1,0:T(8,128)(2,1)} async-done(((bf16[1024,512]{1,0:T(8,128)(2,1)}), bf16[1024,1024]{1,0:T(8,128)(2,1)}) %all-gather.26.cloned.1.call-update) | async-done | bytes 2097168 | tf_op jit(solution)/shard_map/all_gather | solution.py:148
  417.2 47.0 %all-gather.28.cloned.1.call-done = bf16[2,512,1024]{2,1,0:T(8,128)(2,1)} async-done(((bf16[2,128,1024]{2,1,0:T(8,128)(2,1)}), bf16[2,512,1024]{2,1,0:T(8,128)(2,1)}) %all-gather.28.cloned.1.call-update) | async-done | bytes 2097168 | tf_op jit(solution)/shard_map/all_gather | solution.py:95
  477.5 42.8 %reduce-scatter.28.cloned.1.call-done = bf16[2,128,1024]{2,1,0:T(8,128)(2,1)} async-done(((bf16[2,512,1024]{2,1,0:T(8,128)(2,1)}), bf16[2,128,1024]{2,1,0:T(8,128)(2,1)}) %reduce-scatter.28.cloned.1.call-update) | async-done | bytes 524304 | tf_op jit(solution)/shard_map/reduce_scatter | solution.py:99
  526.7 45.4 %all-gather.30.cloned.1.call-done = bf16[2,512,1024]{2,1,0:T(8,128)(2,1)} async-done(((bf16[2,128,1024]{2,1,0:T(8,128)(2,1)}), bf16[2,512,1024]{2,1,0:T(8,128)(2,1)}) %all-gather.30.cloned.1.call-update) | async-done | bytes 2097168 | tf_op jit(solution)/shard_map/all_gather | solution.py:95
  591.4 35.2 %reduce-scatter.30.cloned.1.call-done = bf16[2,128,1024]{2,1,0:T(8,128)(2,1)} async-done(((bf16[2,512,1024]{2,1,0:T(8,128)(2,1)}), bf16[2,128,1024]{2,1,0:T(8,128)(2,1)}) %reduce-scatter.30.cloned.1.call-update) | async-done | bytes 524304 | tf_op jit(solution)/shard_map/reduce_scatter | solution.py:99
  629.7 42.3 %reduce-scatter.26.cloned.1.call-done = bf16[2,128,1024]{2,1,0:T(8,128)(2,1)} async-done(((bf16[2,512,1024]{2,1,0:T(8,128)(2,1)}), bf16[2,128,1024]{2,1,0:T(8,128)(2,1)}) %reduce-scatter.26.cloned.1.call-update) | async-done | bytes 524304 | tf_op jit(solution)/shard_map/reduce_scatter | solution.py:99
  682.4 38.3 %all-gather.32.cloned.1.call-done = bf16[2,512,1024]{2,1,0:T(8,128)(2,1)} async-done(((bf16[2,128,1024]{2,1,0:T(8,128)(2,1)}), bf16[2,512,1024]{2,1,0:T(8,128)(2,1)}) %all-gather.32.cloned.1.call-update) | async-done | bytes 2097168 | tf_op jit(solution)/shard_map/all_gather | solution.py:95
  723.1 21.4 %multiply_reduce_fusion = (f32[2,4,512]{2,1,0:T(4,128)S(1)}, f32[2,4,512,2048]{3,2,1,0:T(8,128)}) fusion(f32[2,4,512,2048]{3,2,1,0:T(8,128)} %get-tuple-element.53, f32[2,4,512]{2,1,0:T(4,128)S(1)} %get-tuple-element.52, bf16[2,512,4,64]{1,3,2,0:T(8,128)(2,1)S(1)} %bitcast.210, bf16[2,2048,4,64]{1,3,2,0:T(8,128)(2,1)S(1)} %bitcast.192), kind=kOutput, calls=%fused_computation.3 | convolution fusion | flops 1098903552 | bytes 69763072 | tf_op jit(solution)/shard_map/sqhd,skhd->shqk/dot_general | solution.py:66
  760.2 28.9 %multiply_convert_fusion = bf16[2,4,512,2048]{3,2,1,0:T(8,128)(2,1)} fusion(f32[2,4,512,2048]{3,2,1,0:T(8,128)} %get-tuple-element.59, f32[2,4,512]{2,1,0:T(4,128)S(1)} %get-tuple-element.58, f32[2,4,512,2048]{3,2,1,0:T(8,128)} %get-tuple-element.53, f32[2,4,512]{2,1,0:T(4,128)S(1)} %get-tuple-element.52), kind=kLoop, calls=%fused_computation.2 | loop fusion | flops 33554432 | bytes 83918848 | tf_op jit(solution)/shard_map/convert_element_type | solution.py:77
  850.3 18.1 %reduce-scatter.60.cloned.1.call-done = bf16[512,1024]{1,0:T(8,128)(2,1)} async-done(((bf16[1024,1024]{1,0:T(8,128)(2,1)}), bf16[512,1024]{1,0:T(8,128)(2,1)}) %reduce-scatter.60.cloned.1.call-update) | async-done | bytes 1048592 | tf_op jit(solution)/shard_map/reduce_scatter | solution.py:262
  868.4 34.1 %reduce-scatter.62.cloned.1.call-done = bf16[1024,512]{1,0:T(8,128)(2,1)} async-done(((bf16[1024,1024]{1,0:T(8,128)(2,1)}), bf16[1024,512]{1,0:T(8,128)(2,1)}) %reduce-scatter.62.cloned.1.call-update) | async-done | bytes 1048592 | tf_op jit(solution)/shard_map/reduce_scatter | solution.py:271
  987.4 17.4 %reduce-scatter.44.cloned.1.call-done = bf16[512,256]{1,0:T(8,128)(2,1)} async-done(((bf16[1024,256]{1,0:T(8,128)(2,1)}), bf16[512,256]{1,0:T(8,128)(2,1)}) %reduce-scatter.44.cloned.1.call-update) | async-done | bytes 262160 | tf_op jit(solution)/shard_map/reduce_scatter | solution.py:244
  1022.1 17.4 %reduce-scatter.46.cloned.1.call-done = bf16[512,256]{1,0:T(8,128)(2,1)} async-done(((bf16[1024,256]{1,0:T(8,128)(2,1)}), bf16[512,256]{1,0:T(8,128)(2,1)}) %reduce-scatter.46.cloned.1.call-update) | async-done | bytes 262160 | tf_op jit(solution)/shard_map/reduce_scatter | solution.py:247
  1043.7 18.4 %reduce-scatter.42.cloned.1.call-done = bf16[2,16,1024]{2,1,0:T(8,128)(2,1)} async-done(((bf16[2,64,1024]{2,1,0:T(8,128)(2,1)}), bf16[2,16,1024]{2,1,0:T(8,128)(2,1)}) %reduce-scatter.42.cloned.1.call-update) | async-done | bytes 65552 | tf_op jit(solution)/shard_map/reduce_scatter | solution.py:99
  1063.5 87.1 %all-reduce.4.cloned.1.call-done = (bf16[512,256]{1,0:T(8,128)(2,1)}, bf16[512,256]{1,0:T(8,128)(2,1)}, bf16[512,256]{1,0:T(8,128)(2,1)}, bf16[256,512]{1,0:T(8,...) async-done(((bf16[512,256]{1,0:T(8,128)(2,1)}, ...) | async-done | bytes 4194320 | tf_op jit(solution)/shard_map/psum | solution.py:276
  1166.5 30.5 %reduce-scatter.36.cloned.1.call-done = bf16[2,128,1024]{2,1,0:T(8,128)(2,1)} async-done(((bf16[2,512,1024]{2,1,0:T(8,128)(2,1)}), bf16[2,128,1024]{2,1,0:T(8,128)(2,1)}) %reduce-scatter.36.cloned.1.call-update) | async-done | bytes 524304 | tf_op jit(solution)/shard_map/reduce_scatter | solution.py:99
  1200.2 40.2 %all-reduce = (f32[1024]{0:T(1024)}, f32[1024]{0:T(1024)}, f32[1024]{0:T(1024)}, f32[1024]{0:T(1024)}, f32[1024]{0:T(1024)}, /*index=5*/f32[1024]{0:T(1024)}) all-reduce(f32[1024]{0:T(1024)S(1)} %get-tuple-element.23, f32[1024]{0:T(1024)S(1)} %get-tuple-element.29, ...), channel_id=1, replica_groups=mesh['fsdp'=2,'ctx'=4,'tp'=4] {'fsdp','ctx','tp'}, use_global_device_ids=true, to_apply=%region_30.31 | all-reduce | flops 6144 | bytes 49152 | tf_op jit(solution)/shard_map/psum | solution.py:232
  (316 shorter events, 397.4 us)
Async XLA Ops:
  138.4 109.8 %all-gather.20.cloned.1.call-start = ((), (), s32[]{:S(2)}) async-start(), calls=%async_computation.26 | async-start | bytes 2621440 | tf_op jit(solution)/shard_map/all_gather | solution.py:95
  187.6 114.7 %reduce-scatter.24.cloned.1.call-start = ((), (), s32[]{:S(2)}) async-start(), calls=%async_computation.27 | async-start | bytes 2621440 | tf_op jit(solution)/shard_map/reduce_scatter | solution.py:99
  260.6 123.2 %all-gather.22.cloned.1.call-start = ((), (), s32[]{:S(2)}) async-start(), calls=%async_computation.28 | async-start | bytes 2621440 | tf_op jit(solution)/shard_map/all_gather | solution.py:95
  305.0 112.2 %all-gather.26.cloned.1.call-start = ((), (), s32[]{:S(2)}) async-start(), calls=%async_computation.30 | async-start | bytes 3145728 | tf_op jit(solution)/shard_map/all_gather | solution.py:148
  305.7 158.5 %all-gather.28.cloned.1.call-start = ((), (), s32[]{:S(2)}) async-start(), calls=%async_computation.32 | async-start | bytes 2621440 | tf_op jit(solution)/shard_map/all_gather | solution.py:95
  306.3 213.9 %reduce-scatter.28.cloned.1.call-start = ((), (), s32[]{:S(2)}) async-start(), calls=%async_computation.33 | async-start | bytes 2621440 | tf_op jit(solution)/shard_map/reduce_scatter | solution.py:99
  477.4 94.7 %all-gather.30.cloned.1.call-start = ((), (), s32[]{:S(2)}) async-start(), calls=%async_computation.34 | async-start | bytes 2621440 | tf_op jit(solution)/shard_map/all_gather | solution.py:95
  526.7 99.9 %reduce-scatter.30.cloned.1.call-start = ((), (), s32[]{:S(2)}) async-start(), calls=%async_computation.35 | async-start | bytes 2621440 | tf_op jit(solution)/shard_map/reduce_scatter | solution.py:99
  591.3 129.4 %all-gather.32.cloned.1.call-start = ((), (), s32[]{:S(2)}) async-start(), calls=%async_computation.36 | async-start | bytes 2621440 | tf_op jit(solution)/shard_map/all_gather | solution.py:95
  675.5 145.0 %reduce-scatter.40.cloned.1.call-start = ((), (), s32[]{:S(2)}) async-start(), calls=%async_computation.41 | async-start | bytes 327680 | tf_op jit(solution)/shard_map/reduce_scatter | solution.py:109
  679.6 143.2 %reduce-scatter.38.cloned.1.call-start = ((), (), s32[]{:S(2)}) async-start(), calls=%async_computation.40 | async-start | bytes 327680 | tf_op jit(solution)/shard_map/reduce_scatter | solution.py:106
  682.4 160.5 %reduce-scatter.34.cloned.1.call-start = ((), (), s32[]{:S(2)}) async-start(), calls=%async_computation.38 | async-start | bytes 2621440 | tf_op jit(solution)/shard_map/reduce_scatter | solution.py:109
  806.5 96.1 %reduce-scatter.62.cloned.1.call-start = ((), (), s32[]{:S(2)}) async-start(), calls=%async_computation.52 | async-start | bytes 3145728 | tf_op jit(solution)/shard_map/reduce_scatter | solution.py:271
  813.9 105.4 %reduce-scatter.58.cloned.1.call-start = ((), (), s32[]{:S(2)}) async-start(), calls=%async_computation.50 | async-start | bytes 786432 | tf_op jit(solution)/shard_map/reduce_scatter | solution.py:268
  817.1 119.5 %reduce-scatter.52.cloned.1.call-start = ((), (), s32[]{:S(2)}) async-start(), calls=%async_computation.47 | async-start | bytes 786432 | tf_op jit(solution)/shard_map/reduce_scatter | solution.py:253
  820.4 132.9 %reduce-scatter.56.cloned.1.call-start = ((), (), s32[]{:S(2)}) async-start(), calls=%async_computation.49 | async-start | bytes 786432 | tf_op jit(solution)/shard_map/reduce_scatter | solution.py:259
  822.7 147.3 %reduce-scatter.54.cloned.1.call-start = ((), (), s32[]{:S(2)}) async-start(), calls=%async_computation.48 | async-start | bytes 786432 | tf_op jit(solution)/shard_map/reduce_scatter | solution.py:256
  824.9 162.4 %reduce-scatter.50.cloned.1.call-start = ((), (), s32[]{:S(2)}) async-start(), calls=%async_computation.46 | async-start | bytes 786432 | tf_op jit(solution)/shard_map/reduce_scatter | solution.py:265
  828.1 176.6 %reduce-scatter.44.cloned.1.call-start = ((), (), s32[]{:S(2)}) async-start(), calls=%async_computation.43 | async-start | bytes 786432 | tf_op jit(solution)/shard_map/reduce_scatter | solution.py:244
  842.8 179.3 %reduce-scatter.48.cloned.1.call-start = ((), (), s32[]{:S(2)}) async-start(), calls=%async_computation.45 | async-start | bytes 786432 | tf_op jit(solution)/shard_map/reduce_scatter | solution.py:250
  845.6 193.9 %reduce-scatter.46.cloned.1.call-start = ((), (), s32[]{:S(2)}) async-start(), calls=%async_computation.44 | async-start | bytes 786432 | tf_op jit(solution)/shard_map/reduce_scatter | solution.py:247
  849.0 213.1 %reduce-scatter.42.cloned.1.call-start = ((), (), s32[]{:S(2)}) async-start(), calls=%async_computation.42 | async-start | bytes 327680 | tf_op jit(solution)/shard_map/reduce_scatter | solution.py:99
  850.3 300.4 %all-reduce.4.cloned.1.call-start = ((), (), s32[]{:S(2)}) async-start(), calls=%async_computation.53 | async-start | bytes 8388608 | tf_op jit(solution)/shard_map/psum | solution.py:276
  1039.6 157.5 %reduce-scatter.36.cloned.1.call-start = ((), (), s32[]{:S(2)}) async-start(), calls=%async_computation.39 | async-start | bytes 2621440 | tf_op jit(solution)/shard_map/reduce_scatter | solution.py:99
  (76 other events, 2607.7 us)
Sparse Core Ops, SparseCore 0:
  13.1 48.6 all-gather.11
  65.0 21.2 all-gather.15
  92.0 22.0 all-gather.13
  138.0 44.8 reduce-scatter.21
  477.5 42.6 reduce-scatter.27
  526.8 45.2 all-gather.29
  675.6 45.1 all-gather.31
  723.3 18.7 reduce-scatter.39
  745.1 20.0 reduce-scatter.37
  768.3 31.4 reduce-scatter.33
  802.9 31.4 reduce-scatter.31
  836.6 31.8 reduce-scatter.59
  870.7 31.8 reduce-scatter.61
  904.7 14.5 reduce-scatter.57
  921.9 14.5 reduce-scatter.51
  938.8 14.5 reduce-scatter.55
  955.4 14.5 reduce-scatter.53
  972.8 14.5 reduce-scatter.49
  990.2 14.5 reduce-scatter.43
  1007.5 14.5 reduce-scatter.47
  1024.9 14.5 reduce-scatter.45
  1042.4 19.5 reduce-scatter.41
  1065.1 85.4 all-reduce.3
  1152.9 44.0 reduce-scatter.35
Sparse Core Ops, SparseCore 1:
  140.6 61.0 all-gather.17
  203.7 44.5 all-gather.19
  260.0 42.3 reduce-scatter.23
  303.9 32.1 all-gather.23
  338.2 45.5 all-gather.21
  385.4 31.7 all-gather.25
  418.6 45.5 all-gather.27
  584.3 42.2 reduce-scatter.29
  629.3 42.7 reduce-scatter.25
where the time goes:
time: 1260 us; the launch traced here: 1250 us
  waiting for transfers between devices  833 us (66%)
  matrix products  195 us (15%)
  blocking collectives  104 us (8%)
  other arithmetic  79.6 us (6%)
  local copies, waits for them, and re-layouts  18.7 us (1%)
  between operations  17.5 us (1%)
    reduce_scatter x7, waiting for transfers between devices, sum_rows(): lax.psum_scatter(value.astype(jnp.bfloat16), 'tp', scatter_dimension=1, t...  255 us
    all_gather x6, waiting for transfers between devices, gather_rows(): return lax.all_gather(value, 'tp', axis=1, tiled=True)  242 us
    psum x1, waiting for transfers between devices, shards(): lax.psum(s_query.astype(jnp.bfloat16), 'ctx').astype(jnp.float32)  87.1 us
    psum x1, blocking collectives, shards(): lax.psum((grad_gain_self, grad_shift_self, grad_gain_cross, grad_shift_cr...  40.2 us
    dot_general x10, matrix products, weight_grad(): jnp.einsum('std,ste->de', rows_in, grad_rows, preferred_element_type=jnp....  36.3 us
    reduce_scatter x1, waiting for transfers between devices, shards(): lax.psum_scatter(grad_outer.astype(jnp.bfloat16), 'fsdp', scatter_dimensi...  34.1 us
    dot_general x10, matrix products, project(): jnp.einsum('std,de->ste', rows_in, weight, preferred_element_type=jnp.flo...  33.9 us
    convert_element_type x2, other arithmetic, attend_back(): grad_scores = (probs * (grad_probs - jnp.sum(probs * grad_probs, axis=-1,...  30.1 us
  transfers between devices with their start and end apart: 33, of which 26 were waited for; matrix products, arithmetic and copies ran while one was open for 17% of the time, Pallas kernels for 0%

commit v1 on v0

v1 whole, which is shorter than its diff:
```python
import functools

import jax
import jax.numpy as jnp
from jax import lax
from jax.experimental import pallas as pl
from jax.experimental.pallas import tpu as pltpu
from jax.sharding import PartitionSpec as P

HEAD_DIM = 64
SCALE = HEAD_DIM ** (-0.5)
BLOCK = 512
MASKED = -1e30
F32 = jnp.float32
BF16 = jnp.bfloat16
ROWS_ROWS = (((1,), (1,)), ((), ()))
ROWS_COLS = (((1,), (0,)), ((), ()))
COLS_COLS = (((0,), (0,)), ((), ()))


def dot(left, right, dims, precision=None):
    return lax.dot_general(left, right, dims, preferred_element_type=F32, precision=precision)


def self_kernel(block, order, qkv, out, lse, q_s, k_s, v_s):
    parts, rows, width = qkv.shape[0], qkv.shape[1], q_s.shape[1]
    for p in range(parts):
        r, at = order[p], slice(p * rows, (p + 1) * rows)
        q_s[at, :] = qkv[r, :, 0:width]
        k_s[at, :] = qkv[r, :, width : 2 * width]
        v_s[at, :] = qkv[r, :, 2 * width : 3 * width]
    lane = lax.broadcasted_iota(jnp.int32, (1, width), 1)
    row = lax.broadcasted_iota(jnp.int32, (block, block), 0)
    col = lax.broadcasted_iota(jnp.int32, (block, block), 1)
    for i in range(parts * rows // block):
        first, at = i * block, slice(i * block, (i + 1) * block)
        q = q_s[at, :]
        mixed = []
        for h in range(2):
            qh = jnp.where((lane < width // 2) == (h == 0), q, jnp.zeros_like(q))
            near = jnp.where(row >= col, dot(qh, k_s[at, :], ROWS_ROWS) * SCALE, MASKED)
            top = jnp.max(near, axis=1, keepdims=True)
            if first:
                far = dot(qh, k_s[0:first, :], ROWS_ROWS) * SCALE
                top = jnp.maximum(top, jnp.max(far, axis=1, keepdims=True))
                far = jnp.exp(far - top)
            near = jnp.exp(near - top)
            total = jnp.sum(near, axis=1, keepdims=True)
            acc = dot(near.astype(BF16), v_s[at, :], ROWS_COLS)
            if first:
                total = total + jnp.sum(far, axis=1, keepdims=True)
                acc = acc + dot(far.astype(BF16), v_s[0:first, :], ROWS_COLS)
            mixed.append(acc / total)
            flat = jnp.broadcast_to(top + jnp.log(total), (block, 128)).T
            lse[h : h + 1, at] = flat[0:1, :]
        both = jnp.where(lane < width // 2, mixed[0], mixed[1]).astype(BF16)
        for t in range(block // rows):
            out[order[i * (block // rows) + t]] = both[t * rows : (t + 1) * rows, :]


def self_attend(qkv, order):
    parts, rows, width = qkv.shape
    width //= 3
    length = parts * rows
    vmem = pl.BlockSpec(memory_space=pltpu.VMEM)
    return pl.pallas_call(
        functools.partial(self_kernel, BLOCK),
        out_shape=(
            jax.ShapeDtypeStruct((parts, rows, width), BF16),
            jax.ShapeDtypeStruct((2, length), F32),
        ),
        in_specs=[pl.BlockSpec(memory_space=pltpu.SMEM), vmem],
        out_specs=(vmem, vmem),
        scratch_shapes=[pltpu.VMEM((length, width), BF16)] * 3,
        compiler_params=pltpu.CompilerParams(vmem_limit_bytes=48 << 20),
        cost_estimate=pl.CostEstimate(
            flops=4 * length * length * width,
            bytes_accessed=8 * length * width,
            transcendentals=length * length,
        ),
        name="self_attend",
    )(order, qkv)


def self_back_kernel(block, order, qkv, out, lse, grad, grad_qkv, q_s, k_s, v_s, g_s, sum_s, dq_s):
    parts, rows, width = qkv.shape[0], qkv.shape[1], q_s.shape[1]
    length = parts * rows
    lane = lax.broadcasted_iota(jnp.int32, (1, width), 1)
    lane8 = lax.broadcasted_iota(jnp.int32, (8, width), 1)
    row8 = lax.broadcasted_iota(jnp.int32, (8, width), 0)
    pick = jnp.where(lane8 // (width // 2) == row8, 1.0, 0.0).astype(F32)
    for p in range(parts):
        r, at = order[p], slice(p * rows, (p + 1) * rows)
        q_s[at, :] = qkv[r, :, 0:width]
        k_s[at, :] = qkv[r, :, width : 2 * width]
        v_s[at, :] = qkv[r, :, 2 * width : 3 * width]
        g_s[at, :] = grad[r]
        sum_s[:, at] = dot(
            pick, grad[r].astype(F32) * out[r].astype(F32), ROWS_ROWS, lax.Precision.HIGHEST
        )
    row = lax.broadcasted_iota(jnp.int32, (block, block), 0)
    col = lax.broadcasted_iota(jnp.int32, (block, block), 1)
    dq_s[...] = jnp.zeros_like(dq_s)
    for j in range(length // block):
        kj, vj = k_s[j * block : (j + 1) * block, :], v_s[j * block : (j + 1) * block, :]
        dks, dvs = [], []
        for h in range(2):
            mine = (lane < width // 2) == (h == 0)
            kh = jnp.where(mine, kj, jnp.zeros_like(kj))
            vh = jnp.where(mine, vj, jnp.zeros_like(vj))
            dk = dv = None
            for i in range(j, length // block):
                at = slice(i * block, (i + 1) * block)
                q, g = q_s[at, :], g_s[at, :]
                scores = dot(kh, q, ROWS_ROWS) * SCALE - lse[h : h + 1, at]
                if i == j:
                    scores = jnp.where(col >= row, scores, MASKED)
                probs = jnp.exp(scores)
                ds = probs * (dot(vh, g, ROWS_ROWS) - sum_s[h : h + 1, at])
                ds = ds.astype(BF16)
                more_v, more_k = (
                    dot(probs.astype(BF16), g, ROWS_COLS),
                    dot(ds, q, ROWS_COLS),
                )
                dk, dv = (more_k, more_v) if dk is None else (dk + more_k, dv + more_v)
                dq_s[at, :] += dot(ds, kh, COLS_COLS)
            dks.append(dk)
            dvs.append(dv)
        dk = (jnp.where(lane < width // 2, dks[0], dks[1]) * SCALE).astype(BF16)
        dv = jnp.where(lane < width // 2, dvs[0], dvs[1]).astype(BF16)
        for t in range(block // rows):
            r, at = order[j * (block // rows) + t], slice(t * rows, (t + 1) * rows)
            grad_qkv[r, :, width : 2 * width] = dk[at]
            grad_qkv[r, :, 2 * width : 3 * width] = dv[at]
    for p in range(parts):
        grad_qkv[order[p], :, 0:width] = (dq_s[p * rows : (p + 1) * rows, :] * SCALE).astype(BF16)


def self_attend_back(qkv, out, lse, grad, order):
    parts, rows, width = qkv.shape
    width //= 3
    length = parts * rows
    vmem = pl.BlockSpec(memory_space=pltpu.VMEM)
    return pl.pallas_call(
        functools.partial(self_back_kernel, BLOCK),
        out_shape=jax.ShapeDtypeStruct(qkv.shape, BF16),
        in_specs=[pl.BlockSpec(memory_space=pltpu.SMEM), vmem, vmem, vmem, vmem],
        out_specs=vmem,
        scratch_shapes=[pltpu.VMEM((length, width), BF16)] * 4
        + [pltpu.VMEM((8, length), F32), pltpu.VMEM((length, width), F32)],
        compiler_params=pltpu.CompilerParams(vmem_limit_bytes=48 << 20),
        cost_estimate=pl.CostEstimate(
            flops=10 * length * length * width,
            bytes_accessed=16 * length * width,
            transcendentals=length * length,
        ),
        name="self_attend_back",
    )(order, qkv, out, lse, grad)


def cross_kernel(lengths, q_ref, k_ref, v_ref, out, lse):
    seqs, rows, width = q_ref.shape
    keys = k_ref.shape[1]
    lane = lax.broadcasted_iota(jnp.int32, (1, 128), 1)
    col = lax.broadcasted_iota(jnp.int32, (rows, keys), 1)
    for s in range(seqs):
        valid = col < lengths[s]
        for pair in range(width // 128):
            at = slice(pair * 128, (pair + 1) * 128)
            q, k, v = q_ref[s, :, at], k_ref[s, :, at], v_ref[s, :, at]
            mixed = []
            for h in range(2):
                qh = jnp.where((lane < 64) == (h == 0), q, jnp.zeros_like(q))
                scores = jnp.where(valid, dot(qh, k, ROWS_ROWS) * SCALE, MASKED)
                top = jnp.max(scores, axis=1, keepdims=True)
                probs = jnp.exp(scores - top)
                total = jnp.sum(probs, axis=1, keepdims=True)
                mixed.append(dot(probs.astype(BF16), v, ROWS_COLS) / total)
                flat = jnp.broadcast_to(top + jnp.log(total), (rows, 128)).T
                place = s * (width // 64) + pair * 2 + h
                lse[place : place + 1, :] = flat[0:1, :]
            out[s, :, at] = jnp.where(lane < 64, mixed[0], mixed[1]).astype(BF16)


def cross_attend(queries, keys_in, values_in, lengths):
    seqs, rows, width = queries.shape
    keys = keys_in.shape[1]
    vmem = pl.BlockSpec(memory_space=pltpu.VMEM)
    return pl.pallas_call(
        cross_kernel,
        out_shape=(
            jax.ShapeDtypeStruct(queries.shape, BF16),
            jax.ShapeDtypeStruct((seqs * width // 64, rows), F32),
        ),
        in_specs=[pl.BlockSpec(memory_space=pltpu.SMEM), vmem, vmem, vmem],
        out_specs=(vmem, vmem),
        compiler_params=pltpu.CompilerParams(vmem_limit_bytes=48 << 20),
        cost_estimate=pl.CostEstimate(
            flops=8 * seqs * rows * keys * width,
            bytes_accessed=4 * seqs * (rows + keys) * width,
            transcendentals=seqs * rows * keys * width // 64,
        ),
        name="cross_attend",
    )(lengths, queries, keys_in, values_in)


def cross_back_kernel(lengths, q_ref, k_ref, v_ref, lse, g_ref, dq_ref, dk_ref, dv_ref):
    seqs, rows, width = q_ref.shape
    keys = k_ref.shape[1]
    lane = lax.broadcasted_iota(jnp.int32, (1, 128), 1)
    row = lax.broadcasted_iota(jnp.int32, (keys, rows), 0)
    for s in range(seqs):
        valid = row < lengths[s]
        for pair in range(width // 128):
            at = slice(pair * 128, (pair + 1) * 128)
            q, k, v, g = q_ref[s, :, at], k_ref[s, :, at], v_ref[s, :, at], g_ref[s, :, at]
            dks, dvs, dq = [], [], None
            for h in range(2):
                mine = (lane < 64) == (h == 0)
                kh = jnp.where(mine, k, jnp.zeros_like(k))
                vh = jnp.where(mine, v, jnp.zeros_like(v))
                place = s * (width // 64) + pair * 2 + h
                scores = dot(kh, q, ROWS_ROWS) * SCALE - lse[place : place + 1, :]
                probs = jnp.exp(jnp.where(valid, scores, MASKED))
                dp = dot(vh, g, ROWS_ROWS)
                ds = (probs * (dp - jnp.sum(probs * dp, axis=0, keepdims=True))).astype(BF16)
                dvs.append(dot(probs.astype(BF16), g, ROWS_COLS))
                dks.append(dot(ds, q, ROWS_COLS))
                more = dot(ds, kh, COLS_COLS)
                dq = more if dq is None else dq + more
            dq_ref[s, :, at] = (dq * SCALE).astype(BF16)
            dk_ref[s, :, at] = (jnp.where(lane < 64, dks[0], dks[1]) * SCALE).astype(BF16)
            dv_ref[s, :, at] = jnp.where(lane < 64, dvs[0], dvs[1]).astype(BF16)


def cross_attend_back(queries, keys_in, values_in, lse, grad, lengths):
    seqs, rows, width = queries.shape
    keys = keys_in.shape[1]
    vmem = pl.BlockSpec(memory_space=pltpu.VMEM)
    return pl.pallas_call(
        cross_back_kernel,
        out_shape=(
            jax.ShapeDtypeStruct(queries.shape, BF16),
            jax.ShapeDtypeStruct(keys_in.shape, BF16),
            jax.ShapeDtypeStruct(keys_in.shape, BF16),
        ),
        in_specs=[pl.BlockSpec(memory_space=pltpu.SMEM)] + [vmem] * 5,
        out_specs=(vmem, vmem, vmem),
        compiler_params=pltpu.CompilerParams(vmem_limit_bytes=48 << 20),
        cost_estimate=pl.CostEstimate(
            flops=20 * seqs * rows * keys * width,
            bytes_accessed=8 * seqs * (rows + keys) * width,
            transcendentals=seqs * rows * keys * width // 64,
        ),
        name="cross_attend_back",
    )(lengths, queries, keys_in, values_in, lse, grad)


def swap_core(value):
    size = lax.axis_size("ctx")
    return lax.ppermute(value, "ctx", [(i, i ^ 1) for i in range(size)])


def swap_y(value):
    size = lax.axis_size("ctx")
    return lax.ppermute(value, "ctx", [(i, i ^ 2) for i in range(size)])


def from_tp(value, step):
    size = lax.axis_size("tp")
    return lax.ppermute(value, "tp", [((i + step) % size, i) for i in range(size)])


def gather_tp(value):
    return jnp.stack([value] + [from_tp(value, e) for e in range(1, lax.axis_size("tp"))])


def in_order(pieces, place):
    size = pieces.shape[0]
    return lax.dynamic_slice_in_dim(
        jnp.concatenate([pieces, pieces]), (size - place) % size, size, 0
    )


def gather_model(value):
    if lax.axis_size("fsdp") != 2:
        return lax.all_gather(value, "fsdp", axis=value.ndim - 1, tiled=True)
    other = lax.ppermute(value, "fsdp", [(0, 1), (1, 0)])
    return jnp.where(
        lax.axis_index("fsdp") == 0,
        jnp.concatenate([value, other], axis=-1),
        jnp.concatenate([other, value], axis=-1),
    )


def sum_model(value):
    if lax.axis_size("fsdp") != 2:
        return lax.psum_scatter(
            value.astype(BF16), "fsdp", scatter_dimension=value.ndim - 1, tiled=True
        ).astype(F32)
    width, mine = value.shape[-1] // 2, lax.axis_index("fsdp")
    keep = lax.dynamic_slice_in_dim(value, mine * width, width, value.ndim - 1)
    send = lax.dynamic_slice_in_dim(value, (1 - mine) * width, width, value.ndim - 1)
    return keep.astype(F32) + lax.ppermute(
        send.astype(BF16), "fsdp", [(0, 1), (1, 0)]
    ).astype(F32)


def sum_tp(pieces):
    size = pieces.shape[0]
    total = pieces[0].astype(F32)
    for e in range(1, size):
        total = total + from_tp(pieces[size - e].astype(BF16), e).astype(F32)
    return total


def pick(value, index, axis):
    return lax.dynamic_index_in_dim(value, index, axis, keepdims=False)


def layer_norm(hidden, gain, shift):
    centre = hidden - jnp.mean(hidden, axis=-1, keepdims=True)
    spread = jnp.mean(centre * centre, axis=-1, keepdims=True)
    return (centre * lax.rsqrt(spread + 1e-05) * gain + shift).astype(BF16)


def layer_norm_back(hidden, gain, grad):
    centre = hidden - jnp.mean(hidden, axis=-1, keepdims=True)
    rate = lax.rsqrt(jnp.mean(centre * centre, axis=-1, keepdims=True) + 1e-05)
    unit, scaled = centre * rate, grad * gain
    back = rate * (
        scaled
        - jnp.mean(scaled, axis=-1, keepdims=True)
        - unit * jnp.mean(scaled * unit, axis=-1, keepdims=True)
    )
    return back, jnp.sum(grad * unit, axis=(0, 1)), jnp.sum(grad, axis=(0, 1))


def gelu_tanh(value):
    return 0.5 * value * (1.0 + jnp.tanh(0.7978845608 * (value + 0.044715 * value * value * value)))


def onto(rows_in, weight):
    return lax.dot_general(
        rows_in, weight, (((rows_in.ndim - 1,), (1,)), ((), ())), preferred_element_type=F32
    )


def back_onto(rows_in, weight):
    return lax.dot_general(
        rows_in, weight, (((rows_in.ndim - 1,), (0,)), ((), ())), preferred_element_type=F32
    )


def weight_grad(grad_rows, rows_in):
    dims = tuple(range(rows_in.ndim - 1))
    return lax.dot_general(
        grad_rows, rows_in, ((dims, dims), ((), ())), preferred_element_type=F32
    )


def chip_rows(value):
    return jnp.stack([value, swap_core(value)], axis=1).reshape(
        value.shape[0], 2 * value.shape[1], value.shape[2]
    )


def sum_chip(value):
    seqs, rows, width = value.shape
    value = value.reshape(seqs, 2, rows // 2, width)
    return value[:, 0] + swap_core(value[:, 1].astype(BF16)).astype(F32)


def ctx_rows(value):
    near = jnp.stack([value, swap_core(value)])
    far = swap_y(value)
    far = jnp.stack([far, swap_core(far)])
    return jnp.concatenate([near, far]).reshape(-1, value.shape[-1])


def sum_ctx(value, shape):
    value = value.reshape((4,) + shape)
    got = swap_core(value[1::2].astype(BF16)).astype(F32)
    far = value[2] + got[1]
    return value[0] + got[0] + swap_y(far.astype(BF16)).astype(F32)


def shards(
    tokens,
    enc_states,
    enc_lengths,
    cotangent,
    gain_self,
    shift_self,
    w_query,
    w_key,
    w_value,
    w_out,
    gain_cross,
    shift_cross,
    cross_query,
    cross_key,
    cross_value,
    cross_out,
    gain_ffn,
    shift_ffn,
    w_inner,
    w_outer,
):
    seqs, rows, model = tokens.shape
    tp, ctx = lax.axis_size("tp"), lax.axis_size("ctx")
    z, c = lax.axis_index("tp"), lax.axis_index("ctx")
    y, k = c // 2, c % 2
    span = tp // 2
    half, low = z // span, z % span
    local = w_query.shape[0]
    hid = w_inner.shape[1] // ctx

    def core_half(weight):
        return pick(weight.reshape(2, 2, HEAD_DIM, local), k, 1).reshape(2 * HEAD_DIM, local)

    def own_head(weight):
        return lax.dynamic_slice_in_dim(weight, c * HEAD_DIM, HEAD_DIM, 0)

    hidden0 = tokens.astype(F32)
    n1 = layer_norm(hidden0, gain_self, shift_self)
    mine = pick(n1, half, 0)
    near = [mine] + [
        from_tp(pick(n1, ((z - e) % tp) // span, 0), e) for e in range(1, tp)
    ]
    far = [swap_y(piece) for piece in near]
    near, far = jnp.stack(near), jnp.stack(far)
    n1_all = [near, far, swap_core(near), swap_core(far)]

    own_qkv = jnp.stack([own_head(w.T) for w in (w_query, w_key, w_value)])
    other_qkv = from_tp(own_qkv, span)
    h_qkv = jnp.where(
        z < span, jnp.stack([own_qkv, other_qkv], 1), jnp.stack([other_qkv, own_qkv], 1)
    )
    h_qkv = gather_model(h_qkv.reshape(-1, local))

    h_out = in_order(gather_tp(core_half(w_out)), z)
    h_out = (
        h_out.reshape(2, span, 2, HEAD_DIM, local).transpose(1, 2, 0, 3, 4).reshape(-1, local)
    )
    h_out = gather_model(h_out)

    h_ckv = gather_model(jnp.concatenate([core_half(cross_key.T), core_half(cross_value.T)]))
    h_cq, h_cout = gather_model(
        gather_tp(jnp.stack([core_half(cross_query.T), core_half(cross_out)]))
        .transpose(1, 0, 2, 3)
        .reshape(2, -1, local)
    )
    quarter = jnp.stack(
        [
            lax.dynamic_slice_in_dim(w_inner, c * hid, hid, 1).T,
            lax.dynamic_slice_in_dim(w_outer, c * hid, hid, 0),
        ]
    )
    h_inner, h_outer = gather_model(
        gather_tp(quarter).transpose(1, 0, 2, 3).reshape(2, -1, local)
    )

    place = jnp.arange(ctx * tp)
    p_c, p_z = place // tp, place % tp
    order = (((p_c % 2) ^ k) * 2 + ((p_c // 2) ^ y)) * tp + (p_z - z) % tp
    order = order.astype(jnp.int32)
    qkv = jnp.concatenate([onto(part, h_qkv).astype(BF16) for part in n1_all])
    o_self, lse_self = self_attend(qkv, order)

    o_parts = o_self.reshape(2, 2, tp, rows, 2 * HEAD_DIM)
    came = jnp.stack(
        [o_parts[:, :, 0]] + [from_tp(o_parts[:, :, tp - e], e) for e in range(1, tp)]
    )
    here, there = came[:, :, 0], swap_y(came[:, :, 1])
    came = jnp.where(y == 0, jnp.stack([here, there], 1), jnp.stack([there, here], 1))
    came = in_order(came, z)
    o_chip = (
        came.reshape(seqs, span, 2, 2, rows, 2 * HEAD_DIM)
        .transpose(0, 3, 4, 1, 2, 5)
        .reshape(seqs, 2 * rows, -1)
    )
    hidden1 = hidden0 + sum_chip(back_onto(o_chip, h_out))

    enc_all = lax.all_gather(enc_states, ("ctx", "tp"), axis=1, tiled=True)
    kv = gather_tp(onto(enc_all, h_ckv).astype(BF16))
    kv = kv.reshape(tp, seqs, -1, 2, 2 * HEAD_DIM).transpose(3, 1, 2, 0, 4)
    k_cross, v_cross = kv.reshape(2, seqs, -1, tp * 2 * HEAD_DIM)
    n2 = chip_rows(layer_norm(hidden1, gain_cross, shift_cross))
    q_cross = onto(n2, h_cq).astype(BF16)
    o_cross, lse_cross = cross_attend(q_cross, k_cross, v_cross, enc_lengths)
    hidden2 = hidden1 + sum_chip(back_onto(o_cross, h_cout))

    grad3 = cotangent.astype(F32)
    dy_ffn = ctx_rows(cotangent)
    n3 = ctx_rows(layer_norm(hidden2, gain_ffn, shift_ffn))
    inner = onto(n3, h_inner)
    active, pull_gelu = jax.vjp(gelu_tanh, inner)
    active = active.astype(BF16)
    d_inner = pull_gelu(onto(dy_ffn, h_outer))[0].astype(BF16)
    d_n3 = sum_ctx(back_onto(d_inner, h_inner), tokens.shape)
    out_tokens = (hidden2 + sum_ctx(back_onto(active, h_outer), tokens.shape)).astype(BF16)

    g_ffn = jnp.stack([weight_grad(d_inner, n3), weight_grad(active, dy_ffn)])
    g_ffn = sum_model(g_ffn.reshape(2, tp, hid, model))
    g_ffn = sum_tp(g_ffn.transpose(1, 0, 2, 3)).astype(BF16)
    g_ffn = lax.all_gather(g_ffn, "ctx", axis=1, tiled=True)
    grad_inner, grad_outer = g_ffn[0].T.astype(F32), g_ffn[1].astype(F32)

    back_ffn, grad_gain_ffn, grad_shift_ffn = layer_norm_back(hidden2, gain_ffn, d_n3)
    grad2 = grad3 + back_ffn

    dy_cross = chip_rows(grad2.astype(BF16))
    do_cross = onto(dy_cross, h_cout).astype(BF16)
    dq_cross, dk_cross, dv_cross = cross_attend_back(
        q_cross, k_cross, v_cross, lse_cross, do_cross, enc_lengths
    )
    d_n2 = sum_chip(back_onto(dq_cross, h_cq))
    back_cross, grad_gain_cross, grad_shift_cross = layer_norm_back(hidden1, gain_cross, d_n2)
    grad1 = grad2 + back_cross

    d_kv = jnp.concatenate(
        [v.reshape(seqs, -1, tp, 2, HEAD_DIM) for v in (dk_cross, dv_cross)], axis=-1
    )
    d_kv = pick(d_kv, y, 3).astype(F32) + swap_y(pick(d_kv, 1 - y, 3)).astype(F32)
    d_kv = sum_tp(d_kv.transpose(2, 0, 1, 3)).astype(BF16)
    own_ckv = pick(h_ckv.reshape(2, 2, HEAD_DIM, model), y, 1).reshape(-1, model)
    grad_enc = lax.psum_scatter(
        back_onto(d_kv, own_ckv).astype(BF16), ("ctx", "tp"), scatter_dimension=1, tiled=True
    ).astype(F32)
    g_ckv = sum_model(weight_grad(d_kv, enc_all))

    g_cross = jnp.stack([weight_grad(dq_cross, n2), weight_grad(o_cross, dy_cross)])
    g_cross = g_cross.reshape(2, tp, 2, HEAD_DIM, model)
    g_cross = pick(g_cross, y, 2) + swap_y(pick(g_cross, 1 - y, 2).astype(BF16)).astype(F32)
    g_cross = sum_tp(sum_model(g_cross).transpose(1, 0, 2, 3))
    g_cross = jnp.concatenate([g_ckv.reshape(2, HEAD_DIM, local), g_cross]).astype(BF16)
    g_cross = lax.all_gather(g_cross, "ctx", axis=1, tiled=True).astype(F32)

    dy_self = chip_rows(grad1.astype(BF16))
    do_chip = onto(dy_self, h_out).astype(BF16)
    do_parts = in_order(
        do_chip.reshape(seqs, 2, rows, span, 2, 2 * HEAD_DIM)
        .transpose(0, 3, 4, 1, 2, 5)
        .reshape(tp, 2, 2, rows, 2 * HEAD_DIM),
        tp - z,
    )
    do_parts = jnp.stack(
        [pick(do_parts, y, 1), swap_y(pick(do_parts, 1 - y, 1))], 1
    )
    do_self = jnp.stack(
        [do_parts[0]] + [from_tp(do_parts[tp - e], e) for e in range(1, tp)]
    )
    do_self = do_self.transpose(2, 1, 0, 3, 4).reshape(o_self.shape)
    d_qkv = self_attend_back(qkv, o_self, lse_self, do_self, order)
    d_parts = d_qkv.reshape(4, tp, rows, -1)
    d_n1 = [back_onto(d_parts[g], h_qkv) for g in range(4)]
    d_near, d_far = (
        d_n1[g] + swap_core(d_n1[g + 2].astype(BF16)).astype(F32) for g in range(2)
    )
    d_mine = [
        d_near[e] + swap_y(d_far[e].astype(BF16)).astype(F32) for e in range(tp)
    ]
    came = [d_mine[0]] + [
        from_tp(d_mine[tp - e].astype(BF16), e).astype(F32) for e in range(1, tp)
    ]
    d_n1 = jnp.stack(
        [
            sum(jnp.where(((z + e) % tp) // span == s, came[e], 0.0) for e in range(tp))
            for s in range(seqs)
        ]
    )
    back_self, grad_gain_self, grad_shift_self = layer_norm_back(hidden0, gain_self, d_n1)
    grad_tokens = grad1 + back_self

    g_out = weight_grad(o_chip, dy_self)
    g_out = g_out.reshape(span, 2, 2, HEAD_DIM, model).transpose(1, 2, 0, 3, 4)
    g_out = g_out.reshape(2, tp, HEAD_DIM, model)
    g_out = pick(g_out, y, 0) + swap_y(pick(g_out, 1 - y, 0).astype(BF16)).astype(F32)
    g_out = sum_tp(in_order(sum_model(g_out), tp - z))

    g_qkv = sum(weight_grad(d_parts[g], n1_all[g]) for g in range(4))
    g_qkv = sum_model(g_qkv).reshape(3, 2, HEAD_DIM, local)
    upper = (z >= span).astype(jnp.int32)
    g_qkv = pick(g_qkv, upper, 1) + from_tp(pick(g_qkv, 1 - upper, 1).astype(BF16), span).astype(
        F32
    )
    g_self = jnp.concatenate([g_qkv, g_out[None]]).astype(BF16)
    g_self = lax.all_gather(g_self, "ctx", axis=1, tiled=True).astype(F32)

    sums = lax.psum(
        (grad_gain_cross, grad_shift_cross, grad_gain_ffn, grad_shift_ffn), ("fsdp", "ctx", "tp")
    )
    grad_gain_self, grad_shift_self = lax.psum(
        (grad_gain_self, grad_shift_self), ("fsdp", "ctx", "tp")
    )
    return (
        out_tokens,
        grad_tokens,
        grad_enc,
        grad_gain_self,
        grad_shift_self,
        g_self[0].T,
        g_self[1].T,
        g_self[2].T,
        g_self[3],
        sums[0],
        sums[1],
        g_cross[2].T,
        g_cross[0].T,
        g_cross[1].T,
        g_cross[3],
        sums[2],
        sums[3],
        grad_inner,
        grad_outer,
    )


def solution(mesh):
    in_specs = (
        P("fsdp", ("ctx", "tp"), None),
        P("fsdp", ("ctx", "tp"), None),
        P("fsdp"),
        P("fsdp", ("ctx", "tp"), None),
        P(),
        P(),
        P("fsdp", "tp"),
        P("fsdp", "tp"),
        P("fsdp", "tp"),
        P("tp", "fsdp"),
        P(),
        P(),
        P("fsdp", "tp"),
        P("fsdp", "tp"),
        P("fsdp", "tp"),
        P("tp", "fsdp"),
        P(),
        P(),
        P("fsdp", "tp"),
        P("tp", "fsdp"),
    )
    out_specs = (
        P("fsdp", ("ctx", "tp"), None),
        P("fsdp", ("ctx", "tp"), None),
        P("fsdp", ("ctx", "tp"), None),
        P(),
        P(),
        P("fsdp", "tp"),
        P("fsdp", "tp"),
        P("fsdp", "tp"),
        P("tp", "fsdp"),
        P(),
        P(),
        P("fsdp", "tp"),
        P("fsdp", "tp"),
        P("fsdp", "tp"),
        P("tp", "fsdp"),
        P(),
        P(),
        P("fsdp", "tp"),
        P("tp", "fsdp"),
    )
    return jax.shard_map(shards, mesh=mesh, in_specs=in_specs, out_specs=out_specs, check_vma=False)
```

time: 1260 us -> 616 us (0.49)
  waiting for transfers between devices: 833 us -> 159 us
  matrix products: 195 us -> 58.9 us
  starting transfers between devices: 2.36 us -> 138 us
  local copies, waits for them, and re-layouts: 18.7 us -> 82.1 us
  blocking collectives: 104 us -> 44.7 us
  Pallas kernels: 0 us -> 35.2 us
    reduce_scatter x21 -> x1, waiting for transfers between devices: 444 us -> 0.01 us  [shards(): lax.psum_scatter(back_onto(d_kv, own_ckv).astype(BF16), ('ctx', 'tp'), sc...]
    all_gather x10 -> x3, waiting for transfers between devices: 299 us -> 0.01 us  [the longest x1 0.01 us: shards(): g_cross = lax.all_gather(g_cross, 'ctx', axis=1, tiled=True).astype(F32)]
    ppermute x0 -> x81, waiting for transfers between devices: none -> 159 us  [the longest x38 92.2 us: from_tp(): lax.ppermute(value, 'tp', [((i + step) % size, i) for i in range(size)])]
    ppermute x0 -> x81, starting transfers between devices: none -> 137 us  [the longest x38 110 us: from_tp(): lax.ppermute(value, 'tp', [((i + step) % size, i) for i in range(size)])]
    dot_general x40 -> x30, matrix products: 174 us -> 58.9 us  [the longest x10 24.3 us: onto(): lax.dot_general(rows_in, weight, (((rows_in.ndim - 1,), (1,)), ((), ())),...]
    psum x1 -> x0, waiting for transfers between devices: 87.1 us -> none  [shards(): lax.psum(s_query.astype(jnp.bfloat16), 'ctx').astype(jnp.float32)]
    all_gather x8 -> x0, blocking collectives: 64.1 us -> none  [the longest x1 10.2 us: shards(): lax.all_gather(w_key, 'fsdp', axis=0, tiled=True)]
    convert_element_type x18, other arithmetic: 58.3 us -> 22.7 us  [the longest x1 3.46 us: shards(): dy_self = chip_rows(grad1.astype(BF16))]
  transfers between devices with their start and end apart: 33 -> 86, of which waited for: 26 -> 29; matrix products, arithmetic and copies ran while one was open for 17% -> 28% of each run, Pallas kernels for 0% -> 6%
where the time goes in v1:
time: 616 us; the launch traced here: 611 us
  waiting for transfers between devices  159 us (26%)
  starting transfers between devices  138 us (22%)
  local copies, waits for them, and re-layouts  82.1 us (13%)
  other arithmetic  77 us (12%)
  matrix products  58.9 us (10%)
  blocking collectives  44.7 us (7%)
  Pallas kernels  35.2 us (6%)
  between operations  16.1 us (3%)
    ppermute x38, starting transfers between devices, from_tp(): lax.ppermute(value, 'tp', [((i + step) % size, i) for i in range(size)])  110 us
    ppermute x38, waiting for transfers between devices, from_tp(): lax.ppermute(value, 'tp', [((i + step) % size, i) for i in range(size)])  92.2 us
    psum x1, blocking collectives, shards(): lax.psum((grad_gain_self, grad_shift_self), ('fsdp', 'ctx', 'tp'))  44.7 us
    ppermute x17, waiting for transfers between devices, swap_y(): return lax.ppermute(value, 'ctx', [(i, i ^ 2) for i in range(size)])  32.3 us
    unnamed x221, local copies, waits for them, and re-layouts  31.7 us
    ppermute x5, waiting for transfers between devices, gather_model(): other = lax.ppermute(value, 'fsdp', [(0, 1), (1, 0)])  27.5 us
    dot_general x10, matrix products, onto(): lax.dot_general(rows_in, weight, (((rows_in.ndim - 1,), (1,)), ((), ())),...  24.3 us
    dot_general x10, matrix products, back_onto(): lax.dot_general(rows_in, weight, (((rows_in.ndim - 1,), (0,)), ((), ())),...  22.6 us
  transfers between devices with their start and end apart: 86, of which 29 were waited for; matrix products, arithmetic and copies ran while one was open for 28% of the time, Pallas kernels for 6%

profile of v1, /device:TPU:0, one launch (start us, length us, event | category | flops | bytes accessed | tf_op | source)
XLA Modules:
  0.0 610.9 jit_solution(16132774633977862741)
XLA Ops:
  40.5 7.8 %collective-permute-done.1 = bf16[128,1024]{1,0:T(8,128)(2,1)} collective-permute-done((bf16[128,1024]{1,0:T(8,128)(2,1)}, bf16[128,1024]{1,0:T(8,128)(2,1)}, u32[]{:S(2)}, u32[]{:S(2)}) %collective-permute-start.1) | collective-permute-done | bytes 262176 | tf_op jit(solution)/shard_map/ppermute | solution.py:271
  52.3 5.3 collective-permute-done.3
  65.2 9.2 %collective-permute-done.4 = bf16[384,512]{1,0:T(8,128)(2,1)S(1)} collective-permute-done((bf16[384,512]{1,0:T(8,128)(2,1)S(1)}, bf16[384,512]{1,0:T(8,128)(2,1)S(1)}, u32[]{:S(2)}, u32[]{:S(2)}) %collective-permute-start.4) | collective-permute-done | bytes 393248 | tf_op jit(solution)/shard_map/ppermute | solution.py:288
  80.0 8.9 %self_attend.1 = (bf16[16,128,128]{2,1,0:T(8,128)(2,1)S(1)}, f32[2,2048]{1,0:T(2,128)S(1)}) custom-call(s32[16]{0:T(128)S(1)} %fusion.150.order, bf16[16,128,384]{2,1,0:T(8,128)(2,1)S(1)} %pad_maximum_fusion.2.qkv), custom_call_target="tpu_custom_call" | custom-call | flops 2147483648 | bytes 2097152 | tf_op jit(solution)/shard_map/self_attend/pallas_call | solution.py:66
  105.5 6.0 collective-permute-start.35
  124.4 18.3 %collective-permute-done.25 = bf16[256,512]{1,0:T(8,128)(2,1)S(1)} collective-permute-done((bf16[256,512]{1,0:T(8,128)(2,1)S(1)}, bf16[256,512]{1,0:T(8,128)(2,1)S(1)}, u32[]{:S(2)}, u32[]{:S(2)}) %collective-permute-start.25) | collective-permute-done | bytes 262176 | tf_op jit(solution)/shard_map/ppermute | solution.py:288
  154.1 6.2 %collective-permute-start.26 = (bf16[2,256,256]{1,2,0:T(8,128)(2,1)}, bf16[2,256,256]{1,2,0:T(8,128)(2,1)}, u32[]{:S(2)}, u32[]{:S(2)}) collective-permute-start(bf16[2,256,256]{1,2,0:T(8,128)(2,1)} %bitcast.73), channel_id=1, source_target_pairs={{1,0},{2,1},{3,2},{0,3},{5,4},{6,5},{7,6},{4,7},{9,8},{10,9},{11,1... | collective-permute-start | bytes 786440 | tf_op jit(solution)/shard_map/ppermute | solution.py:271
  215.8 5.4 maximum_select_fusion
  227.7 5.3 copy.208
  238.2 9.3 %multiply_convert_fusion = (bf16[1024,1024]{1,0:T(8,128)(2,1)}, bf16[1024,1024]{1,0:T(8,128)(2,1)}, f32[1024,1024]{0,1:T(8,128)}) fusion(f32[1024,1024]{0,1:T(8,128)} %fusion.34, bf16[1024,1024]{1,0:T(8,128)(2,1)S(1)} %bitcast.661, bf16[2,1024,1024]{2,1,0:T(8,128)(2,1)S(1)} %copy-done.38), kind=kOutput, calls=%fused_computation.43 | convolution fusion | flops 2174746624 | bytes 16777216 | tf_op jit(solution)/shard_map/dot_general | solution.py:344
  247.5 5.4 copy.203
  252.9 8.5 %fusion.199 = (bf16[1024,1024]{1,0:T(8,128)(2,1)S(1)}, f32[1024,1024]{1,0:T(8,128)S(1)}) fusion(bf16[2,1024,1024]{2,1,0:T(8,128)(2,1)} %copy-done.37, f32[1024,1024]{1,0:T(8,128)} %copy.203, f32[1024,1024]{1,0:T(8,128)} %copy.208), kind=kOutput, calls=%fused_computation.415 | convolution fusion | flops 2173698048 | bytes 16777216 | tf_op jit(solution)/shard_map/dot_general | solution.py:350
  293.7 6.1 %cross_attend_back.1 = (bf16[2,256,512]{2,1,0:T(8,128)(2,1)S(1)}, bf16[2,256,512]{2,1,0:T(8,128)(2,1)S(1)}, bf16[2,256,512]{2,1,0:T(8,128)(2,1)S(1)}) custom-call(s32[2]{0:T(128)S(1)} %copy-done.6, bf16[2,256,512]{2,1,0:T(8,128)(2,1)S(1)} %copy-done.8, bf16[2,256,512]{2,1,0:T(8,128)(2,1)S(1)} %unstack.39.k_ref, bf16[2,256,512]{2,1,0:T(8,128)(2,1)S(1)} %unstack.41.v_ref, ...), custom_call_target="tpu_custom_call" | custom-call | flops 1342177280 | bytes 4194304 | tf_op jit(solution)/shard_map/cross_attend_back/pallas_call | solution.py:240
  314.5 6.0 collective-permute-done.60
  321.8 10.1 %collective-permute-start.63 = (bf16[2,256,128]{1,2,0:T(8,128)(2,1)S(1)}, bf16[2,256,128]{1,2,0:T(8,128)(2,1)S(1)}, u32[]{:S(2)}, u32[]{:S(2)}) collective-permute-start(bf16[2,256,128]{1,2,0:T(8,128)(2,1)S(1)} %get-tuple-element.163), channel_id=1, source_target_pairs={{3,0},{0,1},{1,2},{2,3},{7,4},{4,5},{5,6},{6,7},{11,8},{8,9},{9,10... | collective-permute-start | bytes 393224 | tf_op jit(solution)/shard_map/ppermute | solution.py:271
  374.1 17.3 %self_attend_back.1 = bf16[16,128,384]{2,1,0:T(8,128)(2,1)S(1)} custom-call(s32[16]{0:T(128)S(1)} %fusion.150.order, bf16[16,128,384]{2,1,0:T(8,128)(2,1)S(1)} %pad_maximum_fusion.2.qkv, bf16[16,128,128]{2,1,0:T(8,128)(2,1)S(1)} %copy-done.3, f32[2,2048]{1,0:T(2,128)S(1)} %get-tuple-element.30.lse, bf16[16,128,128]{2,1,0:T(8,128)(2,1)S(1)} %bitcast.623), custom_call_target="tpu_custom_call" | custom-call | flops 5368709120 | bytes 4194304 | tf_op jit(solution)/shard_map/self_attend_back/pallas_call | solution.py:144
  424.3 8.4 %collective-permute-done.65 = bf16[3,64,512]{2,1,0:T(8,128)(2,1)S(1)} collective-permute-done((bf16[3,64,512]{2,1,0:T(8,128)(2,1)S(1)}, bf16[3,64,512]{2,1,0:T(8,128)(2,1)S(1)}, u32[]{:S(2)}, u32[]{:S(2)}) %collective-permute-start.65) | collective-permute-done | bytes 196640 | tf_op jit(solution)/shard_map/ppermute | solution.py:271
  445.2 10.7 %collective-permute-done.80 = bf16[2,256,512]{2,1,0:T(8,128)(2,1)S(1)} collective-permute-done((bf16[2,256,512]{2,1,0:T(8,128)(2,1)S(1)}, bf16[2,256,512]{2,1,0:T(8,128)(2,1)S(1)}, u32[]{:S(2)}, u32[]{:S(2)}) %collective-permute-start.80) | collective-permute-done | bytes 524320 | tf_op jit(solution)/shard_map/ppermute | solution.py:271
  455.8 22.0 %collective-permute-done.79 = bf16[2,256,512]{2,1,0:T(8,128)(2,1)S(1)} collective-permute-done((bf16[2,256,512]{2,1,0:T(8,128)(2,1)S(1)}, bf16[2,256,512]{2,1,0:T(8,128)(2,1)S(1)}, u32[]{:S(2)}, u32[]{:S(2)}) %collective-permute-start.79) | collective-permute-done | bytes 524320 | tf_op jit(solution)/shard_map/ppermute | solution.py:271
  489.8 5.6 collective-permute-done.58
  495.4 9.0 %collective-permute-done.56 = bf16[128,1024]{1,0:T(8,128)(2,1)S(1)} collective-permute-done((bf16[128,1024]{1,0:T(8,128)(2,1)S(1)}, bf16[128,1024]{1,0:T(8,128)(2,1)S(1)}, u32[]{:S(2)}, u32[]{:S(2)}) %collective-permute-start.56) | collective-permute-done | bytes 262176 | tf_op jit(solution)/shard_map/ppermute | solution.py:266
  504.8 19.6 %collective-permute-start.59 = (bf16[128,1024]{1,0:T(8,128)(2,1)S(1)}, bf16[128,1024]{1,0:T(8,128)(2,1)S(1)}, u32[]{:S(2)}, u32[]{:S(2)}) collective-permute-start(bf16[128,1024]{1,0:T(8,128)(2,1)S(1)} %get-tuple-element.148), channel_id=1, source_target_pairs={{3,0},{0,1},{1,2},{2,3},{7,4},{4,5},{5,6},{6,7},{11,8},{8,9},{9,10... | collective-permute-start | bytes 786440 | tf_op jit(solution)/shard_map/ppermute | solution.py:271
  531.1 7.3 %collective-permute-done.57 = bf16[128,1024]{1,0:T(8,128)(2,1)S(1)} collective-permute-done((bf16[128,1024]{1,0:T(8,128)(2,1)S(1)}, bf16[128,1024]{1,0:T(8,128)(2,1)S(1)}, u32[]{:S(2)}, u32[]{:S(2)}) %collective-permute-start.57) | collective-permute-done | bytes 262176 | tf_op jit(solution)/shard_map/ppermute | solution.py:271
  541.8 44.7 %all-reduce = (f32[1024]{0:T(1024)}, f32[1024]{0:T(1024)}, f32[1024]{0:T(1024)}, f32[1024]{0:T(1024)}, f32[1024]{0:T(1024)}, /*index=5*/f32[1024]{0:T(1024)}) all-reduce(f32[1024]{0:T(1024)S(1)} %get-tuple-element.96, f32[1024]{0:T(1024)S(1)} %reduce_sum.209, ...), channel_id=1, replica_groups=mesh['fsdp'=2,'ctx'=4,'tp'=4] {'fsdp','ctx','tp'}, use_global_device_ids=true, to_apply=%region_14.15 | all-reduce | flops 6144 | bytes 49152 | tf_op jit(solution)/shard_map/psum | solution.py:594
  (555 shorter events, 332.4 us)
Async XLA Ops:
  7.2 136.2 %all-gather.5.cloned.1.call-start = ((), (), s32[]{:S(2)}) async-start(), calls=%async_computation.1 | async-start | bytes 1114112 | tf_op jit(solution)/shard_map/all_gather | solution.py:485
  23.2 503.6 %reduce-scatter.2.cloned.1.call-start = ((), (), s32[]{:S(2)}) async-start(), calls=%async_computation.2 | async-start | bytes 1114112 | tf_op jit(solution)/shard_map/reduce_scatter | solution.py:528
  57.7 47.8 %collective-permute-start.23 = (bf16[2,128,512]{2,1,0:T(8,128)(2,1)S(1)}, bf16[2,128,512]{2,1,0:T(8,128)(2,1)S(1)}, u32[]{:S(2)}, u32[]{:S(2)}) collective-permute-start(bf16[2,128,512]{2,1,0:T(8,128)(2,1)S(1)} %copy-done.76), channel_id=1, source_target_pairs={{3,0},{0,1},{1,2},{2,3},{7,4},{4,5},{5,6},{6,7},{11,8},{8,9},{9,10... | collective-permute-start | bytes 786440 | tf_op jit(solution)/shard_map/ppermute | solution.py:271
  60.1 51.3 %collective-permute-start.22 = (bf16[2,128,512]{2,1,0:T(8,128)(2,1)S(1)}, bf16[2,128,512]{2,1,0:T(8,128)(2,1)S(1)}, u32[]{:S(2)}, u32[]{:S(2)}) collective-permute-start(bf16[2,128,512]{2,1,0:T(8,128)(2,1)S(1)} %copy-done.76), channel_id=1, source_target_pairs={{2,0},{3,1},{0,2},{1,3},{6,4},{7,5},{4,6},{5,7},{10,8},{11,9},{8,1... | collective-permute-start | bytes 786440 | tf_op jit(solution)/shard_map/ppermute | solution.py:271
  105.5 40.7 %collective-permute-start.35 = (bf16[2,256,512]{2,1,0:T(8,128)(2,1)}, bf16[2,256,512]{2,1,0:T(8,128)(2,1)}, u32[]{:S(2)}, u32[]{:S(2)}) collective-permute-start(bf16[2,256,512]{2,1,0:T(8,128)(2,1)} %get-tuple-element.172), channel_id=1, source_target_pairs={{3,0},{0,1},{1,2},{2,3},{7,4},{4,5},{5,6},{6,7},{11,8},{8,9},{9,10... | collective-permute-start | bytes 1572872 | tf_op jit(solution)/shard_map/ppermute | solution.py:271
  111.5 39.6 %collective-permute-start.34 = (bf16[2,256,512]{2,1,0:T(8,128)(2,1)}, bf16[2,256,512]{2,1,0:T(8,128)(2,1)}, u32[]{:S(2)}, u32[]{:S(2)}) collective-permute-start(bf16[2,256,512]{2,1,0:T(8,128)(2,1)} %get-tuple-element.172), channel_id=1, source_target_pairs={{2,0},{3,1},{0,2},{1,3},{6,4},{7,5},{4,6},{5,7},{10,8},{11,9},{8,1... | collective-permute-start | bytes 1572872 | tf_op jit(solution)/shard_map/ppermute | solution.py:271
  114.9 39.3 %collective-permute-start.33 = (bf16[2,256,512]{2,1,0:T(8,128)(2,1)}, bf16[2,256,512]{2,1,0:T(8,128)(2,1)}, u32[]{:S(2)}, u32[]{:S(2)}) collective-permute-start(bf16[2,256,512]{2,1,0:T(8,128)(2,1)} %get-tuple-element.172), channel_id=1, source_target_pairs={{1,0},{2,1},{3,2},{0,3},{5,4},{6,5},{7,6},{4,7},{9,8},{10,9},{11,1... | collective-permute-start | bytes 1572872 | tf_op jit(solution)/shard_map/ppermute | solution.py:271
  115.1 48.5 %collective-permute-start.24 = (bf16[2,512,512]{2,1,0:T(8,128)(2,1)S(1)}, bf16[2,512,512]{2,1,0:T(8,128)(2,1)}, u32[]{:S(2)}, u32[]{:S(2)}) collective-permute-start(bf16[2,512,512]{2,1,0:T(8,128)(2,1)S(1)} %bitcast.644), channel_id=1, source_target_pairs={{0,16},{16,0},{1,17},{17,1},{2,18},{18,2},{3,19},{19,3},{4,20},{20... | collective-permute-start | bytes 3145736 | tf_op jit(solution)/shard_map/ppermute | solution.py:288
  143.4 43.3 %collective-permute-start.19 = (bf16[2,128,1024]{2,1,0:T(8,128)(2,1)}, bf16[2,128,1024]{2,1,0:T(8,128)(2,1)}, u32[]{:S(2)}, u32[]{:S(2)}) collective-permute-start(bf16[2,128,1024]{2,1,0:T(8,128)(2,1)} %fusion.93), channel_id=1, source_target_pairs={{0,4},{4,0},{8,12},{12,8},{1,5},{5,1},{9,13},{13,9},{2,6},{6,2},{1... | collective-permute-start | bytes 1572872 | tf_op jit(solution)/shard_map/ppermute | solution.py:261
  163.6 39.5 %collective-permute-start.40 = (bf16[2,128,1024]{2,1,0:T(8,128)(2,1)}, bf16[2,128,1024]{2,1,0:T(8,128)(2,1)}, u32[]{:S(2)}, u32[]{:S(2)}) collective-permute-start(bf16[2,128,1024]{2,1,0:T(8,128)(2,1)} %param.23), channel_id=1, source_target_pairs={{0,8},{4,12},{8,0},{12,4},{1,9},{5,13},{9,1},{13,5},{2,10},{6,14},... | collective-permute-start | bytes 1572872 | tf_op jit(solution)/shard_map/ppermute | solution.py:266
  169.1 46.7 %collective-permute-start.36 = (bf16[2,1024,512]{2,1,0:T(8,128)(2,1)}, bf16[2,1024,512]{2,1,0:T(8,128)(2,1)}, u32[]{:S(2)}, u32[]{:S(2)}) collective-permute-start(bf16[2,1024,512]{2,1,0:T(8,128)(2,1)} %bitcast.628), channel_id=1, source_target_pairs={{0,16},{16,0},{1,17},{17,1},{2,18},{18,2},{3,19},{19,3},{4,20},{20... | collective-permute-start | bytes 6291464 | tf_op jit(solution)/shard_map/ppermute | solution.py:288
  278.2 155.4 %collective-permute-start.77 = (bf16[2,4,256,512]{3,2,1,0:T(8,128)(2,1)}, bf16[2,4,256,512]{3,2,1,0:T(8,128)(2,1)}, u32[]{:S(2)}, u32[]{:S(2)}) collective-permute-start(bf16[2,4,256,512]{3,2,1,0:T(8,128)(2,1)} %fusion.13), channel_id=1, source_target_pairs={{0,16},{16,0},{1,17},{17,1},{2,18},{18,2},{3,19},{19,3},{4,20},{20... | collective-permute-start | bytes 6291464 | tf_op jit(solution)/shard_map/ppermute | solution.py:304
  289.2 45.5 %collective-permute-start.38 = (bf16[2,128,1024]{2,1,0:T(8,128)(2,1)}, bf16[2,128,1024]{2,1,0:T(8,128)(2,1)}, u32[]{:S(2)}, u32[]{:S(2)}) collective-permute-start(bf16[2,128,1024]{2,1,0:T(8,128)(2,1)} %fusion.61), channel_id=1, source_target_pairs={{0,8},{4,12},{8,0},{12,4},{1,9},{5,13},{9,1},{13,5},{2,10},{6,14},... | collective-permute-start | bytes 1572872 | tf_op jit(solution)/shard_map/ppermute | solution.py:266
  312.7 41.2 %collective-permute-start.72 = (bf16[2,4,64,1024]{3,2,1,0:T(8,128)(2,1)}, bf16[2,4,64,1024]{3,2,1,0:T(8,128)(2,1)}, u32[]{:S(2)}, u32[]{:S(2)}) collective-permute-start(bf16[2,4,64,1024]{3,2,1,0:T(8,128)(2,1)} %fusion.49), channel_id=1, source_target_pairs={{0,8},{4,12},{8,0},{12,4},{1,9},{5,13},{9,1},{13,5},{2,10},{6,14},... | collective-permute-start | bytes 3145736 | tf_op jit(solution)/shard_map/ppermute | solution.py:266
  343.6 244.3 %all-gather.9.cloned.1.call-start = ((), (), s32[]{:S(2)}) async-start(), calls=%async_computation.4 | async-start | bytes 1310720 | tf_op jit(solution)/shard_map/all_gather | solution.py:538
  355.9 40.1 %collective-permute-start.73 = (bf16[2,4,64,512]{3,2,1,0:T(8,128)(2,1)S(1)}, bf16[2,4,64,512]{3,2,1,0:T(8,128)(2,1)S(1)}, u32[]{:S(2)}, u32[]{:S(2)}) collective-permute-start(bf16[2,4,64,512]{3,2,1,0:T(8,128)(2,1)S(1)} %dynamic-slice_convert_fusion), channel_id=1, source_target_pairs={{0,16},{16,0},{1,17},{17,1},{2,18},{18,2},{3,19},{19,3},{4,20},{20... | collective-permute-start | bytes 1572872 | tf_op jit(solution)/shard_map/ppermute | solution.py:304
  369.7 33.0 %collective-permute-start.66 = (bf16[4,64,1024]{2,1,0:T(8,128)(2,1)S(1)}, bf16[4,64,1024]{2,1,0:T(8,128)(2,1)S(1)}, u32[]{:S(2)}, u32[]{:S(2)}) collective-permute-start(bf16[4,64,1024]{2,1,0:T(8,128)(2,1)S(1)} %fusion.90), channel_id=1, source_target_pairs={{0,8},{4,12},{8,0},{12,4},{1,9},{5,13},{9,1},{13,5},{2,10},{6,14},... | collective-permute-start | bytes 1572872 | tf_op jit(solution)/shard_map/ppermute | solution.py:266
  410.7 182.7 %all-gather.7.cloned.1.call-start = ((), (), s32[]{:S(2)}) async-start(), calls=%async_computation.3 | async-start | bytes 1310720 | tf_op jit(solution)/shard_map/all_gather | solution.py:589
  433.5 165.3 %all-gather.11.cloned.1.call-start = ((), (), s32[]{:S(2)}) async-start(), calls=%async_computation.5 | async-start | bytes 2621440 | tf_op jit(solution)/shard_map/all_gather | solution.py:507
  439.0 40.0 %collective-permute-start.52 = (bf16[4,128,1024]{2,1,0:T(8,128)(2,1)}, bf16[4,128,1024]{2,1,0:T(8,128)(2,1)S(1)}, u32[]{:S(2)}, u32[]{:S(2)}) collective-permute-start(bf16[4,128,1024]{2,1,0:T(8,128)(2,1)} %convolution_convert_fusion.1), channel_id=1, source_target_pairs={{0,4},{4,0},{8,12},{12,8},{1,5},{5,1},{9,13},{13,9},{2,6},{6,2},{1... | collective-permute-start | bytes 3145736 | tf_op jit(solution)/shard_map/ppermute | solution.py:261
  439.8 38.0 %collective-permute-start.79 = (bf16[2,256,512]{2,1,0:T(8,128)(2,1)S(1)}, bf16[2,256,512]{2,1,0:T(8,128)(2,1)S(1)}, u32[]{:S(2)}, u32[]{:S(2)}) collective-permute-start(bf16[2,256,512]{2,1,0:T(8,128)(2,1)S(1)} %get-tuple-element.138), channel_id=1, source_target_pairs={{2,0},{3,1},{0,2},{1,3},{6,4},{7,5},{4,6},{5,7},{10,8},{11,9},{8,1... | collective-permute-start | bytes 1572872 | tf_op jit(solution)/shard_map/ppermute | solution.py:271
  443.2 34.7 %collective-permute-start.78 = (bf16[2,256,512]{2,1,0:T(8,128)(2,1)S(1)}, bf16[2,256,512]{2,1,0:T(8,128)(2,1)S(1)}, u32[]{:S(2)}, u32[]{:S(2)}) collective-permute-start(bf16[2,256,512]{2,1,0:T(8,128)(2,1)S(1)} %get-tuple-element.136), channel_id=1, source_target_pairs={{1,0},{2,1},{3,2},{0,3},{5,4},{6,5},{7,6},{4,7},{9,8},{10,9},{11,1... | collective-permute-start | bytes 1572872 | tf_op jit(solution)/shard_map/ppermute | solution.py:271
  445.2 39.5 %collective-permute-start.51 = (bf16[4,128,1024]{2,1,0:T(8,128)(2,1)}, bf16[4,128,1024]{2,1,0:T(8,128)(2,1)}, u32[]{:S(2)}, u32[]{:S(2)}) collective-permute-start(bf16[4,128,1024]{2,1,0:T(8,128)(2,1)} %convolution_convert_fusion.2), channel_id=1, source_target_pairs={{0,4},{4,0},{8,12},{12,8},{1,5},{5,1},{9,13},{13,9},{2,6},{6,2},{1... | collective-permute-start | bytes 3145736 | tf_op jit(solution)/shard_map/ppermute | solution.py:261
  483.7 44.6 %collective-permute-start.53 = (bf16[128,1024]{1,0:T(8,128)(2,1)}, bf16[128,1024]{1,0:T(8,128)(2,1)S(1)}, u32[]{:S(2)}, u32[]{:S(2)}) collective-permute-start(bf16[128,1024]{1,0:T(8,128)(2,1)} %get-tuple-element.150), channel_id=1, source_target_pairs={{0,8},{4,12},{8,0},{12,4},{1,9},{5,13},{9,1},{13,5},{2,10},{6,14},... | collective-permute-start | bytes 786440 | tf_op jit(solution)/shard_map/ppermute | solution.py:266
  (160 other events, 1837.1 us)
Sparse Core Ops, SparseCore 0:
  23.4 56.9 all-gather.4
  343.7 62.3 reduce-scatter.1
  410.8 16.9 all-gather.8
  433.6 16.7 all-gather.6
  479.2 39.2 all-gather.10

commit v2 on v0

v2 whole, which is shorter than its diff:
```python
import functools

import jax
import jax.numpy as jnp
from jax import lax
from jax.experimental import pallas as pl
from jax.experimental.pallas import tpu as pltpu
from jax.sharding import PartitionSpec as P

HEAD_DIM = 64
SCALE = HEAD_DIM ** (-0.5)
BLOCK = 512
MASKED = -1e30
EPS = 1e-05
F32 = jnp.float32
BF16 = jnp.bfloat16
NT = (((1,), (1,)), ((), ()))
NN = (((1,), (0,)), ((), ()))
TN = (((0,), (0,)), ((), ()))


def dot(left, right, dims, precision=None):
    return lax.dot_general(left, right, dims, preferred_element_type=F32, precision=precision)


def shape(dims, dtype):
    return jax.ShapeDtypeStruct(tuple(dims), dtype)


def kernel_call(body, name, scalars, arrays, outs, scratch=(), flops=0):
    vmem = pl.BlockSpec(memory_space=pltpu.VMEM)
    smem = pl.BlockSpec(memory_space=pltpu.SMEM)
    moved = sum(a.size * a.dtype.itemsize for a in arrays)
    moved += sum(a.size * a.dtype.itemsize for a in outs)
    return pl.pallas_call(
        body,
        out_shape=tuple(outs),
        in_specs=[smem] * len(scalars) + [vmem] * len(arrays),
        out_specs=(vmem,) * len(outs),
        scratch_shapes=list(scratch),
        compiler_params=pltpu.CompilerParams(vmem_limit_bytes=56 << 20),
        cost_estimate=pl.CostEstimate(flops=flops // 1, bytes_accessed=moved // 1, transcendentals=0),
        name=name,
    )(*scalars, *arrays)


def span_of(at, i, parts):
    width = parts[i].shape[-1]
    return pl.ds(pl.multiple_of(at[i], 128), width) if len(parts) > 1 else slice(0, width)


def onto(read, parts, at, rows_of=lambda part: part[...]):
    return sum(
        dot(read(span_of(at, i, parts)), rows_of(part), NT) for i, part in enumerate(parts)
    )


def lanes_of(h, width=128):
    return (lax.broadcasted_iota(jnp.int32, (1, width), 1) < width // 2) == (h == 0)


def head(value, h):
    return jnp.where(lanes_of(h), value, jnp.zeros_like(value))


def normal(hidden, gain, shift):
    centre = hidden - jnp.mean(hidden, axis=-1, keepdims=True)
    spread = jnp.mean(centre * centre, axis=-1, keepdims=True)
    return centre * lax.rsqrt(spread + EPS) * gain + shift


def first_norm_kernel(tp, picks, tokens, enc, gain, shift, *rest):
    outs, keep = rest[:tp], rest[tp]
    rows, slots = tokens.shape[1], enc.shape[1]
    for s in range(tokens.shape[0]):
        keep[s] = normal(tokens[s].astype(F32), gain[...], shift[...]).astype(BF16)
    for e in range(tp):
        outs[e][:rows] = keep[picks[e]]
        for s in range(enc.shape[0]):
            outs[e][rows + s * slots : rows + (s + 1) * slots] = enc[s]


def norm_kernel(before, own, got, gain, shift, hidden, normed):
    for s in range(before.shape[0]):
        value = before[s].astype(F32) + own[s] + got[s].astype(F32)
        hidden[s] = value
        normed[s] = normal(value, gain[...], shift[...]).astype(BF16)


def norm_back_rows(hidden, gain, grad):
    centre = hidden - jnp.mean(hidden, axis=-1, keepdims=True)
    rate = lax.rsqrt(jnp.mean(centre * centre, axis=-1, keepdims=True) + EPS)
    unit, scaled = centre * rate, grad * gain
    back = rate * (
        scaled
        - jnp.mean(scaled, axis=-1, keepdims=True)
        - unit * jnp.mean(scaled * unit, axis=-1, keepdims=True)
    )
    return back, jnp.sum(grad * unit, axis=0, keepdims=True), jnp.sum(grad, axis=0, keepdims=True)


def norm_back_kernel(hidden, gain, after, own, *rest):
    got, (grad_out, rounded, sums) = rest[:-3], rest[-3:]
    gains = shifts = None
    for s in range(hidden.shape[0]):
        grad = own[s]
        for more in got:
            grad = grad + more[s].astype(F32)
        back, g, b = norm_back_rows(hidden[s], gain[...], grad)
        gains, shifts = (g, b) if gains is None else (gains + g, shifts + b)
        total = after[s].astype(F32) + back
        grad_out[s] = total
        rounded[s] = total.astype(BF16)
    sums[0:1, :] = gains
    sums[1:2, :] = shifts


def last_norm_kernel(seq_of, tokens, gain, after, own, other, grad_out, acc):
    acc[seq_of[0]] = own[...]
    acc[1 - seq_of[0]] = other[...].astype(F32)
    for s in range(tokens.shape[0]):
        back, _, _ = norm_back_rows(tokens[s].astype(F32), gain[...], acc[s])
        grad_out[s] = after[s] + back


def self_kernel(n_parts, tp, block, at, places, order, *refs):
    groups, refs = refs[:4], refs[4:]
    weights, refs = refs[:n_parts], refs[n_parts:]
    qkv, lse, outs, out_s = refs[0], refs[1], refs[2:-1], refs[-1]
    rows, width = out_s.shape[1], qkv.shape[2]
    length = qkv.shape[1]
    for g in range(4):
        group = groups[g]
        value = onto(
            lambda span: group[:, :rows, span].reshape(tp * rows, -1),
            weights,
            at,
            lambda part: part[0 : 3 * width],
        ).astype(BF16)
        for e in range(tp):
            row = pl.ds(pl.multiple_of(places[g * tp + e] * rows, rows), rows)
            for i in range(3):
                qkv[i, row, :] = value[e * rows : (e + 1) * rows, i * width : (i + 1) * width]
    row = lax.broadcasted_iota(jnp.int32, (block, block), 0)
    col = lax.broadcasted_iota(jnp.int32, (block, block), 1)
    for i in range(length // block):
        first, here = i * block, slice(i * block, (i + 1) * block)
        q = qkv[0, here, :]
        mixed = []
        for h in range(2):
            qh = head(q, h)
            near = jnp.where(row >= col, dot(qh, qkv[1, here, :], NT) * SCALE, MASKED)
            top = jnp.max(near, axis=1, keepdims=True)
            if first:
                far = dot(qh, qkv[1, 0:first, :], NT) * SCALE
                top = jnp.maximum(top, jnp.max(far, axis=1, keepdims=True))
                far = jnp.exp(far - top)
            near = jnp.exp(near - top)
            total = jnp.sum(near, axis=1, keepdims=True)
            acc = dot(near.astype(BF16), qkv[2, here, :], NN)
            if first:
                total = total + jnp.sum(far, axis=1, keepdims=True)
                acc = acc + dot(far.astype(BF16), qkv[2, 0:first, :], NN)
            mixed.append(acc / total)
            flat = jnp.broadcast_to(top + jnp.log(total), (block, 128)).T
            lse[h : h + 1, here] = flat[0:1, :]
        both = jnp.where(lanes_of(0), mixed[0], mixed[1]).astype(BF16)
        for t in range(block // rows):
            out_s[order[i * (block // rows) + t]] = both[t * rows : (t + 1) * rows, :]
    for kr in range(2):
        for j in range(2 * tp):
            outs[j][kr] = out_s[kr * 2 * tp + j]


def cut(ref, i):
    width = ref.shape[-1]
    return slice(i * width, (i + 1) * width)


def pair_rows(pack, i, t_of, tp, e):
    own, mate = t_of[e], t_of[e ^ (tp // 2)]
    return jnp.concatenate(
        [pack[i, own, 0:64], pack[i, mate, 0:64], pack[i, own, 64:128], pack[i, mate, 64:128]],
        axis=0,
    )


def out_kernel(tp, t_of, seq_of, *refs):
    came, refs = refs[: 2 * tp], refs[2 * tp :]
    pack, own, send, acc = refs
    rows = own.shape[1]
    own[...] = jnp.zeros_like(own)
    acc[...] = jnp.zeros_like(acc)
    for e in range(tp):
        value = jnp.concatenate(
            [came[ys * tp + e][...].reshape(2 * rows, -1) for ys in range(2)], axis=1
        )
        s = seq_of[e]
        for i in range(pack.shape[0]):
            span = cut(pack, i)
            got = dot(value, pair_rows(pack, i, t_of, tp, e), NN)
            own[s, :, span] += got[:rows]
            acc[s, :, span] += got[rows:]
    send[...] = acc[...].astype(BF16)


def grad_mixed_kernel(tp, t_of, seq_of, own, got, pack, *outs):
    rows = own.shape[1]
    for e in range(tp):
        s, value = seq_of[e], 0.0
        for i in range(pack.shape[0]):
            span = cut(pack, i)
            left = jnp.concatenate([own[s, :, span], got[s, :, span]], axis=0)
            value = value + dot(left, pair_rows(pack, i, t_of, tp, e), NT)
        value = value.astype(BF16)
        for ys in range(2):
            for kr in range(2):
                outs[ys * tp + e][kr] = value[
                    kr * rows : (kr + 1) * rows, ys * 128 : (ys + 1) * 128
                ]


def chip_rows(own, got, span):
    seqs, rows = own.shape[0], own.shape[1]
    return jnp.concatenate(
        [own[:, :, span].reshape(seqs * rows, -1), got[:, :, span].reshape(seqs * rows, -1)],
        axis=0,
    )


def seq_rows(ref, e, s, seqs, rows):
    return jnp.concatenate(
        [ref[e, (j * seqs + s) * rows : (j * seqs + s + 1) * rows, :] for j in range(2)], axis=0
    )


def keys_values(kv_own, kv_far, e, s, keys):
    part = slice(s * keys, (s + 1) * keys)
    return (
        jnp.concatenate([kv_own[e, 0:64, part], kv_far[e, 0:64, part]], axis=0),
        jnp.concatenate([kv_own[e, 64:128, part], kv_far[e, 64:128, part]], axis=0),
    )


def pair_of(pack, i, t, j):
    return pack[i, t, j * 128 : (j + 1) * 128]


def by_pair(own, got, pack, t, j):
    return sum(
        dot(chip_rows(own, got, cut(pack, i)), pair_of(pack, i, t, j), NT)
        for i in range(pack.shape[0])
    ).astype(BF16)


def pairs_back(value, pack, t_of, j, own, send):
    seqs, rows = own.shape[0], own.shape[1]
    half = seqs * rows
    for i in range(pack.shape[0]):
        span = cut(pack, i)
        total = sum(
            dot(value[e], pair_of(pack, i, t_of[e], j), NN) for e in range(value.shape[0])
        )
        own[:, :, span] = total[:half].reshape(seqs, rows, -1)
        send[:, :, span] = total[half:].astype(BF16).reshape(seqs, rows, -1)


def keys_kernel(n_parts, tp, at, places, *refs):
    groups, refs = refs[:4], refs[4:]
    weights, (enc_all, kv) = refs[:n_parts], refs[n_parts:]
    seqs, keys = enc_all.shape[0], enc_all.shape[1]
    slots = keys // (4 * tp)
    rows = groups[0].shape[1] - seqs * slots
    for g in range(4):
        for e in range(tp):
            row = pl.ds(pl.multiple_of(places[g * tp + e] * slots, slots), slots)
            for s in range(seqs):
                enc_all[s, row, :] = groups[g][e, rows + s * slots : rows + (s + 1) * slots]
    for s in range(seqs):
        total = 0.0
        for i in range(n_parts):
            span = span_of(at, i, weights)
            total = total + dot(weights[i][-kv.shape[0] :], enc_all[s, :, span], NT)
        kv[:, s * keys : (s + 1) * keys] = total.astype(BF16)


def cross_kernel(tp, lengths, t_of, own_in, got_in, kv_own, kv_far, pack, own, send, q_out, o_out, lse):
    seqs, rows = own.shape[0], own.shape[1]
    keys = kv_own.shape[2] // seqs
    for e in range(tp):
        q_out[e] = by_pair(own_in, got_in, pack, t_of[e], 1)
    col = lax.broadcasted_iota(jnp.int32, (2 * rows, keys), 1)
    for s in range(seqs):
        valid = col < lengths[s]
        for e in range(tp):
            q = seq_rows(q_out, e, s, seqs, rows)
            keys_in, values_in = keys_values(kv_own, kv_far, e, s, keys)
            mixed = []
            for h in range(2):
                scores = jnp.where(valid, dot(head(q, h), keys_in, NN) * SCALE, MASKED)
                top = jnp.max(scores, axis=1, keepdims=True)
                probs = jnp.exp(scores - top)
                total = jnp.sum(probs, axis=1, keepdims=True)
                mixed.append(dot(probs.astype(BF16), values_in, NT) / total)
                flat = jnp.broadcast_to(top + jnp.log(total), (2 * rows, 128)).T
                row = (s * tp + e) * 2 + h
                lse[row : row + 1, :] = flat[0:1, :]
            both = jnp.where(lanes_of(0), mixed[0], mixed[1]).astype(BF16)
            for j in range(2):
                o_out[e, (j * seqs + s) * rows : (j * seqs + s + 1) * rows, :] = both[
                    j * rows : (j + 1) * rows
                ]
    pairs_back(o_out, pack, t_of, 2, own, send)


def cross_back_kernel(tp, lengths, t_of, own_in, got_in, q_in, lse, kv_own, kv_far, pack, *refs):
    own, send, dq_out, dkv_own, dkv_far, do_s = refs
    seqs, rows = own.shape[0], own.shape[1]
    keys = kv_own.shape[2] // seqs
    for e in range(tp):
        do_s[e] = by_pair(own_in, got_in, pack, t_of[e], 2)
    key = lax.broadcasted_iota(jnp.int32, (keys, 2 * rows), 0)
    for s in range(seqs):
        valid = key < lengths[s]
        for e in range(tp):
            q, g = seq_rows(q_in, e, s, seqs, rows), seq_rows(do_s, e, s, seqs, rows)
            keys_in, values_in = (v.T for v in keys_values(kv_own, kv_far, e, s, keys))
            dks, dvs, dq = [], [], 0.0
            for h in range(2):
                kh, vh = head(keys_in, h), head(values_in, h)
                row = (s * tp + e) * 2 + h
                scores = dot(kh, q, NT) * SCALE - lse[row : row + 1, :]
                probs = jnp.exp(jnp.where(valid, scores, MASKED))
                dp = dot(vh, g, NT)
                ds = (probs * (dp - jnp.sum(probs * dp, axis=0, keepdims=True))).astype(BF16)
                dvs.append(dot(probs.astype(BF16), g, NN)[:, h * 64 : (h + 1) * 64])
                dks.append(dot(ds, q, NN)[:, h * 64 : (h + 1) * 64] * SCALE)
                dq = dq + dot(ds, kh, TN)
            dq = (dq * SCALE).astype(BF16)
            for j in range(2):
                dq_out[e, (j * seqs + s) * rows : (j * seqs + s + 1) * rows, :] = dq[
                    j * rows : (j + 1) * rows
                ]
            part = slice(s * keys, (s + 1) * keys)
            dkv_own[e, :, part] = jnp.concatenate([dks[0], dvs[0]], axis=1).T.astype(BF16)
            dkv_far[e, :, part] = jnp.concatenate([dks[1], dvs[1]], axis=1).T.astype(BF16)
    pairs_back(dq_out, pack, t_of, 1, own, send)


def ffn_kernel(tp, n_own, n_got, y_own, y_got, weights, *refs):
    active, d_inner, d_own, d_send, o_own, o_send = refs
    seqs, rows = n_own.shape[0], n_own.shape[1]
    half, parts, width = seqs * rows, weights.shape[0], weights.shape[4]
    spans = [slice(i * width, (i + 1) * width) for i in range(parts)]
    for e in range(tp):
        inner = sum(
            dot(chip_rows(n_own, n_got, spans[i]), weights[i, e, 0], NT) for i in range(parts)
        )
        grad = sum(
            dot(chip_rows(y_own, y_got, spans[i]), weights[i, e, 1], NT) for i in range(parts)
        )
        square = inner * inner
        bend = jnp.tanh(0.7978845608 * (inner + 0.044715 * square * inner))
        active[e] = (0.5 * inner * (1.0 + bend)).astype(BF16)
        slope = 0.5 * (1.0 + bend) + 0.5 * inner * (1.0 - bend * bend) * (
            0.7978845608 * (1.0 + 3.0 * 0.044715 * square)
        )
        d_inner[e] = (grad * slope).astype(BF16)
    for j, (out, send, rows_in) in enumerate(((d_own, d_send, d_inner), (o_own, o_send, active))):
        for i in range(parts):
            total = sum(dot(rows_in[e], weights[i, e, j], NN) for e in range(tp))
            out[:, :, spans[i]] = total[:half].reshape(seqs, rows, -1)
            send[:, :, spans[i]] = total[half:].astype(BF16).reshape(seqs, rows, -1)


def ffn_grad_kernel(tp, d_near, d_far, a_near, a_far, *refs):
    n_rows, y_rows, out = refs[:4], refs[4:8], refs[8]
    parts, width = out.shape[0], out.shape[4]
    for j, (near, far, given) in enumerate(
        ((d_near, d_far, n_rows), (a_near, a_far, y_rows))
    ):
        for i in range(parts):
            span = slice(i * width, (i + 1) * width)
            first, second = chip_rows(given[0], given[1], span), chip_rows(given[2], given[3], span)
            for e in range(tp):
                out[i, e, j] = (dot(near[e], first, TN) + dot(far[e], second, TN)).astype(BF16)


def cross_grad_kernel(tp, dq, o, n_own, n_got, y_own, y_got, dkv_far, keep, send):
    parts, width = keep.shape[1], keep.shape[4]
    for j, (left, a, b) in enumerate(((dq, n_own, n_got), (o, y_own, y_got))):
        right = chip_rows(a, b, slice(None))
        for e in range(tp):
            got = dot(left[e], right, TN)
            for i in range(parts):
                span = slice(i * width, (i + 1) * width)
                keep[e, i, j] = got[0:64, span]
                send[e, (2 * i + j) * 64 : (2 * i + j + 1) * 64] = got[64:128, span].astype(BF16)
    send[:, 2 * parts * 64 :] = dkv_far[...]


def out_grad_kernel(tp, seq_of, own, got, *refs):
    came, (keep, send, acc) = refs[: 2 * tp], refs[2 * tp :]
    rows = own.shape[1]
    acc[...] = jnp.zeros_like(acc)
    for e in range(tp):
        s, mate = seq_of[e], e ^ (tp // 2)
        right = jnp.concatenate([own[s], got[s]], axis=0)
        for ys in range(2):
            left = came[ys * tp + e][...].reshape(2 * rows, -1)
            value = dot(left, right, TN)
            acc[ys, e] += value[0:64]
            acc[ys, mate] += value[64:128]
    keep[...] = acc[0]
    send[...] = acc[1].astype(BF16)


def enc_grad_kernel(n_parts, tp, at, places, d_kv, enc_all, *refs):
    weights, (keep, send, grad_w, all_s) = refs[:n_parts], refs[n_parts:]
    seqs, keys, model = enc_all.shape
    slots = keys // (4 * tp)
    total = 0.0
    for s in range(seqs):
        part = d_kv[:, s * keys : (s + 1) * keys]
        total = total + dot(part, enc_all[s], NN)
        for i in range(n_parts):
            all_s[s, :, span_of(at, i, weights)] = dot(part, weights[i][-d_kv.shape[0] :], TN)
    grad_w[...] = total
    for g in range(4):
        for e in range(tp):
            row = pl.ds(pl.multiple_of(places[g * tp + e] * slots, slots), slots)
            for s in range(seqs):
                if g < 2:
                    keep[g, e, s] = all_s[s, row, :]
                else:
                    send[g - 2, e, s] = all_s[s, row, :].astype(BF16)


def turn_kernel(count, offsets, *refs):
    pieces, outs = refs[:4], refs[4:-1]
    all_s = refs[-1]
    for j, out in enumerate(outs):
        part = pieces[0].shape[1]
        for i in range(4):
            all_s[pl.ds(pl.multiple_of(offsets[i] * part, part), part), :] = pieces[i][j].astype(F32)
        out[...] = all_s[...].T if j < count else all_s[...]


def qkv_grad_kernel(n_parts, tp, at, grads, *refs):
    groups, refs = refs[:4], refs[4:]
    weights, outs, sums = refs[:n_parts], refs[n_parts:-1], refs[-1]
    rows, columns = grads.shape[1], grads.shape[2]
    left = [grads[g * tp : (g + 1) * tp].reshape(-1, columns) for g in range(4)]
    ones = jnp.ones((8, left[0].shape[0]), BF16)
    counts = sum(dot(ones, part, NN) for part in left)
    for i in range(n_parts):
        span = span_of(at, i, outs)
        total = 0.0
        for g in range(4):
            right = groups[g][:, :rows, span].reshape(left[g].shape[0], -1)
            total = total + dot(left[g], right, TN)
        outs[i][...] = total.astype(outs[i].dtype)
        weight = weights[i][0:columns].astype(F32)
        sums[0:1, span] = jnp.sum(total * weight, axis=0, keepdims=True)
        sums[1:2, span] = dot(counts, weight, NN, lax.Precision.HIGHEST)[0:1]


def self_back_kernel(n_parts, tp, block, at, order, qkv, lse, *refs):
    outs, grads, refs = refs[: 2 * tp], refs[2 * tp : 4 * tp], refs[4 * tp :]
    weights, (grad_qkv, keep, send, g_s, sum_s, dq_s) = refs[:n_parts], refs[n_parts:]
    length, width = qkv.shape[1], qkv.shape[2]
    rows = outs[0].shape[1]
    lane8 = lax.broadcasted_iota(jnp.int32, (8, width), 1)
    row8 = lax.broadcasted_iota(jnp.int32, (8, width), 0)
    chosen = jnp.where(lane8 // (width // 2) == row8, 1.0, 0.0).astype(F32)
    for j in range(2 * tp):
        for kr in range(2):
            r = kr * 2 * tp + j
            here = pl.ds(pl.multiple_of(order[r] * rows, rows), rows)
            g_s[here, :] = grads[j][kr]
            sum_s[:, here] = dot(
                chosen,
                grads[j][kr].astype(F32) * outs[j][kr].astype(F32),
                NT,
                lax.Precision.HIGHEST,
            )
    row = lax.broadcasted_iota(jnp.int32, (block, block), 0)
    col = lax.broadcasted_iota(jnp.int32, (block, block), 1)
    dq_s[...] = jnp.zeros_like(dq_s)
    blocks = length // block
    for j in range(blocks):
        here = slice(j * block, (j + 1) * block)
        kj, vj = qkv[1, here, :], qkv[2, here, :]
        dks, dvs = [], []
        for h in range(2):
            kh, vh = head(kj, h), head(vj, h)
            dk = dv = 0.0
            for i in range(j, blocks):
                there = slice(i * block, (i + 1) * block)
                q, g = qkv[0, there, :], g_s[there, :]
                scores = dot(kh, q, NT) * SCALE - lse[h : h + 1, there]
                if i == j:
                    scores = jnp.where(col >= row, scores, MASKED)
                probs = jnp.exp(scores)
                ds = (probs * (dot(vh, g, NT) - sum_s[h : h + 1, there])).astype(BF16)
                dv, dk = dv + dot(probs.astype(BF16), g, NN), dk + dot(ds, q, NN)
                dq_s[there, :] += dot(ds, kh, TN)
            dks.append(dk)
            dvs.append(dv)
        dk = (jnp.where(lanes_of(0), dks[0], dks[1]) * SCALE).astype(BF16)
        dv = jnp.where(lanes_of(0), dvs[0], dvs[1]).astype(BF16)
        qkv_rows = block // rows
        for t in range(qkv_rows):
            r, part = order[4 * tp + j * qkv_rows + t], slice(t * rows, (t + 1) * rows)
            grad_qkv[r, :, width : 2 * width] = dk[part]
            grad_qkv[r, :, 2 * width : 3 * width] = dv[part]
    for p in range(4 * tp):
        grad_qkv[order[4 * tp + p], :, 0:width] = (
            dq_s[p * rows : (p + 1) * rows, :] * SCALE
        ).astype(BF16)
    for g in (2, 3, 0, 1):
        left = grad_qkv[g * tp : (g + 1) * tp].reshape(tp * rows, -1)
        for i in range(n_parts):
            span = span_of(at, i, weights)
            value = dot(left, weights[i][0 : 3 * width], NN).reshape(tp, rows, -1)
            if g < 2:
                keep[g, :, :, span] = value
            else:
                send[g - 2, :, :, span] = value.astype(BF16)


def swap(value, axis, bit):
    return lax.ppermute(value, axis, [(i, i ^ bit) for i in range(lax.axis_size(axis))])


def swap_core(value):
    return swap(value, "ctx", 1)


def swap_y(value):
    return swap(value, "ctx", 2)


def from_tp(value, step):
    return swap(value, "tp", step)


def from_chip(value, far, step):
    ctx, size = lax.axis_size("ctx"), lax.axis_size("tp")
    if far == 0 and step == 0:
        return value
    pairs = [
        ((c ^ (2 * far)) * size + (i ^ step), c * size + i)
        for c in range(ctx)
        for i in range(size)
    ]
    return lax.ppermute(value, ("ctx", "tp"), pairs)


def after(value, *others):
    return lax.optimization_barrier((value, others))[0]


def pick(value, index, axis):
    return lax.dynamic_index_in_dim(value, index, axis, keepdims=False)


def gather_tp(value):
    return jnp.stack([value] + [from_tp(value, e) for e in range(1, lax.axis_size("tp"))])


def model_parts(value):
    if lax.axis_size("fsdp") == 2:
        return (value, swap(value, "fsdp", 1))
    return (lax.all_gather(value, "fsdp", axis=value.ndim - 1, tiled=True),)


def sum_model(value):
    if lax.axis_size("fsdp") != 2:
        return lax.psum_scatter(
            value.astype(BF16), "fsdp", scatter_dimension=value.ndim - 1, tiled=True
        ).astype(F32)
    width, mine = value.shape[-1] // 2, lax.axis_index("fsdp")
    keep = lax.dynamic_slice_in_dim(value, mine * width, width, value.ndim - 1)
    send = lax.dynamic_slice_in_dim(value, (1 - mine) * width, width, value.ndim - 1)
    return keep.astype(F32) + swap(send.astype(BF16), "fsdp", 1).astype(F32)


def sum_parts(parts):
    if len(parts) == 1:
        return sum_model(parts[0])
    return parts[0].astype(F32) + swap(parts[1], "fsdp", 1).astype(F32)


def sum_tp(pieces):
    total = pieces[0].astype(F32)
    for e in range(1, lax.axis_size("tp")):
        total = total + from_tp(pieces[e].astype(BF16), e).astype(F32)
    return total


def sum_all(value):
    for axis in ("ctx", "tp", "fsdp"):
        if axis == "fsdp" and lax.axis_size(axis) != 2:
            value = lax.psum(value, axis)
            continue
        bit = 1
        while bit < lax.axis_size(axis):
            value = value + swap(value, axis, bit)
            bit *= 2
    return value


def shards(
    tokens,
    enc_states,
    enc_lengths,
    cotangent,
    gain_self,
    shift_self,
    w_query,
    w_key,
    w_value,
    w_out,
    gain_cross,
    shift_cross,
    cross_query,
    cross_key,
    cross_value,
    cross_out,
    gain_ffn,
    shift_ffn,
    w_inner,
    w_outer,
):
    seqs, rows, model = tokens.shape
    tp, ctx = lax.axis_size("tp"), lax.axis_size("ctx")
    z, c = lax.axis_index("tp"), lax.axis_index("ctx")
    y, k = c // 2, c % 2
    span = tp // 2
    local = w_query.shape[0]
    hid = w_inner.shape[1] // ctx
    own_rows = tokens.shape
    chip = 2 * seqs * rows
    n_parts = 2 if lax.axis_size("fsdp") == 2 else 1
    mine = lax.axis_index("fsdp") * local if n_parts == 2 else 0
    at = jnp.stack([jnp.int32(mine), jnp.int32(model // 2 - mine)])
    step = jnp.arange(tp, dtype=jnp.int32)
    seq_of = (z ^ step) // span
    two = lambda vector: vector.reshape(1, -1)
    gains = [two(g) for g in (gain_self, shift_self, gain_cross, shift_cross, gain_ffn, shift_ffn)]

    rel = jnp.arange(4 * tp, dtype=jnp.int32)
    places = (2 * ((rel // tp) % 2 ^ y) + ((rel // (2 * tp)) ^ k)) * tp + ((rel % tp) ^ z)
    order = ((((rel // tp) % 2) ^ k) * 2 + ((rel // (2 * tp)) ^ y)) * tp + ((rel % tp) ^ z)
    places, order = places.astype(jnp.int32), order.astype(jnp.int32)

    def own_head(weight):
        return lax.dynamic_slice_in_dim(weight, c * HEAD_DIM, HEAD_DIM, 0)

    def core_half(weight):
        other = lax.dynamic_slice_in_dim(weight, (c ^ 2) * HEAD_DIM, HEAD_DIM, 0)
        return jnp.concatenate([own_head(weight), other])

    own_qkv = jnp.stack([own_head(w.T) for w in (w_query, w_key, w_value)])
    own_ckv = jnp.concatenate([own_head(cross_key.T), own_head(cross_value.T)])
    own_qkv, picks = lax.optimization_barrier((own_qkv, (z ^ step) // span))
    other_qkv = from_tp(own_qkv, span)
    slots = enc_states.shape[1]
    keys = 4 * tp * slots
    pieces = kernel_call(
        functools.partial(first_norm_kernel, tp),
        "norm_self",
        [picks],
        [tokens, enc_states, gains[0], gains[1]],
        [shape((rows + seqs * slots, model), BF16)] * tp,
        [pltpu.VMEM(own_rows, BF16)],
    )
    t_of = (z ^ step).astype(jnp.int32)
    pack = jnp.concatenate([core_half(w) for w in (w_out, cross_query.T, cross_out)])

    def gather_weights(value):
        got = lax.all_gather(value, ("fsdp", "tp"))
        got = got.reshape(-1, tp, *value.shape)
        if n_parts == 2:
            return got
        return jnp.moveaxis(got, 0, -2).reshape(1, tp, *value.shape[:-1], model)

    which = jnp.stack([c, c ^ 1, c ^ 2, c ^ 3]).astype(jnp.int32)
    near = [pieces[0]] + [None] * (tp - 1)
    bit = span
    while bit:
        for e in range(0, tp, 2 * bit):
            near[e + bit] = from_tp(pieces[bit] if e == 0 else near[e], bit)
        bit //= 2
    far = [swap_y(piece) for piece in near]
    near = jnp.stack(after(near, other_qkv, far[0]))
    h_qkv = model_parts(
        jnp.concatenate([jnp.stack([own_qkv, other_qkv], 1).reshape(-1, local), own_ckv])
    )
    far = after(jnp.stack(far), h_qkv)
    groups = [near, far, swap_core(near), swap_core(far)]

    h_ffn = jnp.stack(
        [
            lax.dynamic_slice_in_dim(w_inner, c * hid, hid, 1).T,
            lax.dynamic_slice_in_dim(w_outer, c * hid, hid, 0),
        ]
    )
    pack = gather_weights(after(pack, near))
    h_ffn = gather_weights(after(h_ffn, near))
    y_far = swap_y(after(cotangent, far))
    y_rows = [cotangent, swap_core(after(cotangent, near)), y_far]

    enc_all, kv_own = kernel_call(
        functools.partial(keys_kernel, n_parts, tp),
        "cross_keys",
        [at, places],
        [*groups, *h_qkv],
        [shape((seqs, keys, model), BF16), shape((2 * HEAD_DIM, seqs * keys), BF16)],
        flops=4 * seqs * keys * model * 2 * HEAD_DIM,
    )
    kv_at = kv_own
    kv_own = gather_tp(kv_own)

    length, width = ctx * tp * rows, 2 * HEAD_DIM
    qkv, lse_self, *o_sent = kernel_call(
        functools.partial(self_kernel, n_parts, tp, BLOCK),
        "self_attend",
        [after(at, kv_at), places, order],
        [*groups, *h_qkv],
        [shape((3, length, width), BF16), shape((2, length), F32)]
        + [shape((2, rows, width), BF16)] * (2 * tp),
        [pltpu.VMEM((4 * tp, rows, width), BF16)],
        flops=4 * length * length * width + 6 * length * model * width,
    )
    o_sent = after(o_sent, kv_own)
    kv_far = swap_y(kv_own)
    came = [
        from_chip(o_sent[ys * tp + e], ys, e) for ys in range(2) for e in range(tp)
    ]
    partial_own, partial_send = kernel_call(
        functools.partial(out_kernel, tp),
        "out_self",
        [t_of, seq_of],
        [*came, pack],
        [shape(own_rows, F32), shape(own_rows, BF16)],
        [pltpu.VMEM(own_rows, F32)],
        flops=2 * chip * 4 * width * model,
    )

    def add_norm(before, own, sent, which):
        return kernel_call(
            norm_kernel,
            "add_norm",
            [],
            [before, own, swap_core(sent), gains[2 * which], gains[2 * which + 1]],
            [shape(own_rows, F32), shape(own_rows, BF16)],
        )

    hidden1, n2 = add_norm(tokens, partial_own, partial_send, 1)

    n2_got = swap_core(n2)
    partial_own, partial_send, q_cross, o_cross, lse_cross = kernel_call(
        functools.partial(cross_kernel, tp),
        "cross_attend",
        [enc_lengths, after(t_of, y_far)],
        [n2, n2_got, kv_own, kv_far, pack],
        [
            shape(own_rows, F32),
            shape(own_rows, BF16),
            shape((tp, chip, width), BF16),
            shape((tp, chip, width), BF16),
            shape((seqs * tp * 2, 2 * rows), F32),
        ],
        flops=4 * chip * tp * width * (model + keys),
    )
    hidden2, n3 = add_norm(hidden1, partial_own, partial_send, 2)

    n3_far = swap_y(n3)
    y_rows.append(swap_core(after(y_far, n3)))
    n_rows = [n3, swap_core(n3), n3_far, swap_core(n3_far)]

    def feed(first):
        return kernel_call(
            functools.partial(ffn_kernel, tp),
            "feed_forward",
            [],
            [*n_rows[first : first + 2], *y_rows[first : first + 2], h_ffn],
            [shape((tp, chip, hid), BF16)] * 2 + [shape(own_rows, F32), shape(own_rows, BF16)] * 2,
            flops=8 * chip * model * tp * hid,
        )

    a_far, d_far, dn_far, dn_far_send, out_far, out_far_send = feed(2)
    a_near, d_near, dn_own, dn_near_send, out_own, out_near_send = feed(0)

    def far_sum(own, sent):
        return (own + swap_core(sent).astype(F32)).astype(BF16)

    dn_near = swap_core(dn_near_send)
    dn_far = far_sum(dn_far, dn_far_send)
    g_ffn = kernel_call(
        functools.partial(ffn_grad_kernel, tp),
        "grad_feed_forward",
        [],
        [after(d_near, dn_far, dn_near), d_far, a_near, a_far, *n_rows, *y_rows],
        [shape((n_parts, tp, 2, hid, model // n_parts), BF16)],
        flops=8 * chip * model * tp * hid,
    )[0]
    dn_far = swap_y(dn_far)

    def norm_back(hidden, gain, before, own, *got):
        return kernel_call(
            norm_back_kernel,
            "norm_back",
            [],
            [hidden, gain, before, own, *got],
            [shape(own_rows, F32), shape(own_rows, BF16), shape((2, model), F32)],
        )

    grad2, y2, sums_ffn = norm_back(
        hidden2, after(gains[4], g_ffn), cotangent, dn_own, dn_near, dn_far
    )
    if n_parts == 1:
        g_ffn = g_ffn.reshape(tp, 2, hid, -1, local).transpose(3, 0, 1, 2, 4)
    g_ffn = lax.psum_scatter(
        after(g_ffn.reshape(-1, 2, hid, local), y2), ("fsdp", "tp"), scatter_dimension=0
    )
    g_ffn = lax.all_gather(g_ffn.astype(BF16), "ctx", axis=1, tiled=True)

    y2_got = swap_core(y2)
    held, out_near_send, out_far_send = after((out_far, out_near_send, out_far_send), y2)
    out_near, out_far = swap_core(out_near_send), far_sum(held, out_far_send)
    dn_own, dn_send, dq_cross, dkv_own, dkv_far = kernel_call(
        functools.partial(cross_back_kernel, tp),
        "cross_attend_back",
        [enc_lengths, after(t_of, out_near, out_far)],
        [y2, y2_got, q_cross, lse_cross, kv_own, kv_far, pack],
        [
            shape(own_rows, F32),
            shape(own_rows, BF16),
            shape((tp, chip, width), BF16),
            shape(kv_own.shape, BF16),
            shape(kv_own.shape, BF16),
        ],
        [pltpu.VMEM((tp, chip, width), BF16)],
        flops=4 * chip * tp * width * (model + 3 * keys),
    )
    dn_got = swap_core(dn_send)
    half = seqs * keys
    halves = model // half
    keep, send = kernel_call(
        functools.partial(cross_grad_kernel, tp),
        "grad_cross",
        [],
        [dq_cross, o_cross, n2, n2_got, y2, y2_got, dkv_far],
        [
            shape((tp, halves, 2, HEAD_DIM, half), F32),
            shape((tp, 2 * halves * HEAD_DIM + width, half), BF16),
        ],
        flops=4 * chip * tp * width * model,
    )
    cross_got = swap_y(send)
    grad1, y1, sums_cross = norm_back(hidden1, gains[2], grad2, dn_own, dn_got)

    y1_got = swap_core(y1)
    do_sent = kernel_call(
        functools.partial(grad_mixed_kernel, tp),
        "grad_mixed",
        [t_of, seq_of],
        [y1, y1_got, pack],
        [shape((2, rows, width), BF16)] * (2 * tp),
        flops=2 * chip * 4 * width * model,
    )
    do_came = [
        from_chip(do_sent[ys * tp + e], ys, e) for ys in range(2) for e in range(tp)
    ]
    out_keep, out_send = kernel_call(
        functools.partial(out_grad_kernel, tp),
        "grad_out",
        [after(seq_of, do_sent)],
        [y1, y1_got, *came],
        [shape((tp, HEAD_DIM, model), F32), shape((tp, HEAD_DIM, model), BF16)],
        [pltpu.VMEM((2, tp, HEAD_DIM, model), F32)],
        flops=2 * chip * tp * width * model,
    )
    cross_got = after(cross_got, do_came)
    g_cross = keep + cross_got[:, :-width].reshape(keep.shape).astype(F32)
    d_kv = dkv_own.astype(F32) + cross_got[:, -width:].astype(F32)
    first = lax.axis_index("fsdp") if n_parts == 2 else 0
    cross_x = swap(pick(g_cross, 1 - first, 1).astype(BF16), "fsdp", 1) if n_parts == 2 else None
    out_far = swap_y(after(out_far, do_came))
    out_got = swap_y(after(out_send, do_came))
    d_qkv, dn_keep, dn_send = kernel_call(
        functools.partial(self_back_kernel, n_parts, tp, BLOCK),
        "self_attend_back",
        [after(at, out_keep, g_cross), jnp.concatenate([places, order])],
        [qkv, lse_self, *o_sent, *do_came, *h_qkv],
        [
            shape((4 * tp, rows, 3 * width), BF16),
            shape((2, tp, rows, model), F32),
            shape((2, tp, rows, model), BF16),
        ],
        [
            pltpu.VMEM((length, width), BF16),
            pltpu.VMEM((8, length), F32),
            pltpu.VMEM((length, width), F32),
        ],
        flops=10 * length * length * width + 6 * length * model * width,
    )
    dn_send, dn_keep, cross_x, out_got, out_far = after(
        (dn_send, dn_keep, cross_x, out_got, out_far), d_qkv
    )
    dn_got = swap_core(dn_send)
    dn_sent = [(dn_keep[1, e] + dn_got[1, e].astype(F32)).astype(BF16) for e in range(tp)]
    dn_near = [dn_keep[0, e] + dn_got[0, e].astype(F32) for e in range(tp)]
    g_cross, d_kv, cross_x, out_got, out_far = after(
        (g_cross, d_kv, cross_x, out_got, out_far), dn_sent
    )
    dn_upper = swap_y(jnp.stack(dn_sent[span:]))
    dn_lower = swap_y(jnp.stack(dn_sent[:span]))
    if n_parts == 2:
        g_cross = pick(g_cross, first, 1) + cross_x.astype(F32)
        g_cross = sum_tp(jnp.concatenate([g_cross.reshape(tp, -1, local), d_kv], axis=1))
        g_cross = after(g_cross, dn_upper)
        g_cross, d_kv = g_cross[: 2 * HEAD_DIM].reshape(2, HEAD_DIM, local), g_cross[2 * HEAD_DIM :]
    else:
        g_cross = sum_tp(
            sum_model(g_cross.transpose(0, 2, 3, 1, 4).reshape(tp, 2, HEAD_DIM, model))
        )
        d_kv = sum_tp(d_kv)
    out_tokens = (hidden2 + out_own + out_near.astype(F32) + out_far.astype(F32)).astype(BF16)
    grad_inner, grad_outer = after(g_ffn[0], dn_sent).T.astype(F32), g_ffn[1].astype(F32)
    *g_qkv, sums_self = kernel_call(
        functools.partial(qkv_grad_kernel, n_parts, tp),
        "grad_qkv",
        [after(at, dn_sent, grad_inner, grad_outer)],
        [d_qkv, *groups, *h_qkv],
        (
            [shape((3 * width, model), F32)]
            if n_parts == 1
            else [shape((3 * width, local), F32), shape((3 * width, local), BF16)]
        )
        + [shape((2, model), F32)],
        flops=6 * length * width * model,
    )
    enc_keep, enc_send, g_ckv = kernel_call(
        functools.partial(enc_grad_kernel, n_parts, tp),
        "grad_enc",
        [at, places],
        [d_kv.astype(BF16), enc_all, *h_qkv],
        [
            shape((2, tp, seqs, slots, model), F32),
            shape((2, tp, seqs, slots, model), BF16),
            shape((2 * HEAD_DIM, model), F32),
        ],
        [pltpu.VMEM((seqs, keys, model), F32)],
        flops=4 * seqs * keys * width * model,
    )
    enc_got = swap_core(enc_send)
    enc_far = swap_y((enc_keep[1] + enc_got[1].astype(F32)).astype(BF16))
    grad_enc = sum_tp(enc_keep[0] + enc_got[0].astype(F32) + enc_far.astype(F32))
    g_out = sum_model(out_keep + out_got.astype(F32))
    dn_pieces = [dn_near[e] + dn_lower[e].astype(F32) for e in range(span)]
    dn_pieces += [dn_near[span + e] + dn_upper[e].astype(F32) for e in range(span)]
    for first_piece in (span, 0):
        count = span
        while count > 1:
            count //= 2
            for e in range(count):
                got = from_tp(dn_pieces[first_piece + count + e].astype(BF16), count)
                if first_piece:
                    dn_began = got
                dn_pieces[first_piece + e] = dn_pieces[first_piece + e] + got.astype(F32)
    dn_other = from_tp(dn_pieces[span].astype(BF16), span)
    grad_tokens = kernel_call(
        last_norm_kernel,
        "norm_back_self",
        [seq_of],
        [tokens, gains[0], grad1, dn_pieces[0], dn_other],
        [shape(own_rows, F32)],
        [pltpu.VMEM(own_rows, F32)],
    )[0]

    sums = jnp.concatenate([sums_self, sums_cross, sums_ffn])
    sums = sum_all(after(sums, dn_began))
    grad_shift_self = sums[1]
    grad_gain_self = (sums[0] - shift_self * sums[1]) / gain_self

    def turned(pieces, count):
        quarters = pieces[0].shape[0]
        return kernel_call(
            functools.partial(turn_kernel, count),
            "turn",
            [which],
            pieces,
            [
                shape((pieces[0].shape[2], 4 * pieces[0].shape[1])[:: 1 if j < count else -1], F32)
                for j in range(quarters)
            ],
            [pltpu.VMEM((4 * pieces[0].shape[1], pieces[0].shape[2]), F32)],
        )

    def along_ctx(value):
        far = swap_y(value)
        return [value, swap_core(value), far, swap_core(far)]


    g_cross = jnp.concatenate([sum_model(g_ckv).reshape(2, HEAD_DIM, local), g_cross]).astype(BF16)
    g_cross = lax.all_gather(g_cross, "ctx", axis=1, tiled=True).astype(F32)
    g_qkv, g_out = after((sum_parts(g_qkv), g_out), dn_began)
    g_qkv = g_qkv.reshape(3, 2, HEAD_DIM, local)
    total, g_mate = g_out[0], g_qkv[:, 1].reshape(-1, local)
    for e in range(1, tp):
        piece = g_out[e]
        if e == span:
            got = from_tp(jnp.concatenate([piece, g_mate]).astype(BF16), e).astype(F32)
            total, g_mate = total + got[:HEAD_DIM], got[HEAD_DIM:]
        else:
            total = total + from_tp(piece.astype(BF16), e).astype(F32)
    g_qkv = g_qkv[:, 0] + g_mate.reshape(3, HEAD_DIM, local)
    g_self = jnp.concatenate([g_qkv, total[None]]).astype(BF16)
    g_self = turned(along_ctx(g_self), 3)
    return (
        out_tokens,
        grad_tokens,
        grad_enc,
        grad_gain_self,
        grad_shift_self,
        g_self[0],
        g_self[1],
        g_self[2],
        g_self[3],
        sums[2],
        sums[3],
        g_cross[2].T,
        g_cross[0].T,
        g_cross[1].T,
        g_cross[3],
        sums[4],
        sums[5],
        grad_inner,
        grad_outer,
    )


def solution(mesh):
    in_specs = (
        P("fsdp", ("ctx", "tp"), None),
        P("fsdp", ("ctx", "tp"), None),
        P("fsdp"),
        P("fsdp", ("ctx", "tp"), None),
        P(),
        P(),
        P("fsdp", "tp"),
        P("fsdp", "tp"),
        P("fsdp", "tp"),
        P("tp", "fsdp"),
        P(),
        P(),
        P("fsdp", "tp"),
        P("fsdp", "tp"),
        P("fsdp", "tp"),
        P("tp", "fsdp"),
        P(),
        P(),
        P("fsdp", "tp"),
        P("tp", "fsdp"),
    )
    out_specs = (
        P("fsdp", ("ctx", "tp"), None),
        P("fsdp", ("ctx", "tp"), None),
        P("fsdp", ("ctx", "tp"), None),
        P(),
        P(),
        P("fsdp", "tp"),
        P("fsdp", "tp"),
        P("fsdp", "tp"),
        P("tp", "fsdp"),
        P(),
        P(),
        P("fsdp", "tp"),
        P("fsdp", "tp"),
        P("fsdp", "tp"),
        P("tp", "fsdp"),
        P(),
        P(),
        P("fsdp", "tp"),
        P("tp", "fsdp"),
    )
    return jax.shard_map(shards, mesh=mesh, in_specs=in_specs, out_specs=out_specs, check_vma=False)
```

time: 1260 us -> 465 us (0.37)
  waiting for transfers between devices: 833 us -> 144 us
  matrix products: 195 us -> 0 us
  Pallas kernels: 0 us -> 140 us
  blocking collectives: 104 us -> 0 us
  starting transfers between devices: 2.36 us -> 93.6 us
  other arithmetic: 79.6 us -> 37.7 us
  local copies, waits for them, and re-layouts: 18.7 us -> 32 us
    reduce_scatter x21 -> x1, waiting for transfers between devices: 444 us -> 0.02 us  [shards(): lax.psum_scatter(after(g_ffn.reshape(-1, 2, hid, local), y2), ('fsdp', 't...]
    all_gather x11 -> x4, waiting for transfers between devices: 299 us -> 5.62 us  [the longest x2 5.62 us: gather_weights(): got = lax.all_gather(value, ('fsdp', 'tp'))]
    dot_general x40 -> x0, matrix products: 174 us -> none  [the longest x10 36.3 us: weight_grad(): jnp.einsum('std,ste->de', rows_in, grad_rows, preferred_element_type=jnp....]
    pallas_call x0 -> x21, Pallas kernels: none -> 140 us  [kernel_call(): pl.pallas_call(body, out_shape=tuple(outs), in_specs=[smem] * len(scalars...]
    ppermute x0 -> x78, waiting for transfers between devices: none -> 138 us  [the longest x64 122 us: swap(): lax.ppermute(value, axis, [(i, i ^ bit) for i in range(lax.axis_size(axis...]
    ppermute x0 -> x78, starting transfers between devices: none -> 93 us  [the longest x64 60.6 us: swap(): lax.ppermute(value, axis, [(i, i ^ bit) for i in range(lax.axis_size(axis...]
    psum x1 -> x0, waiting for transfers between devices: 87.1 us -> none  [shards(): lax.psum(s_query.astype(jnp.bfloat16), 'ctx').astype(jnp.float32)]
    all_gather x8 -> x0, blocking collectives: 64.1 us -> none  [the longest x1 10.2 us: shards(): lax.all_gather(w_key, 'fsdp', axis=0, tiled=True)]
  transfers between devices with their start and end apart: 33 -> 83, of which waited for: 26 -> 39; matrix products, arithmetic and copies ran while one was open for 17% -> 11% of each run, Pallas kernels for 0% -> 28%
where the time goes in v2:
time: 465 us; the launch traced here: 462 us
  waiting for transfers between devices  144 us (31%)
  Pallas kernels  140 us (30%)
  starting transfers between devices  93.6 us (20%)
  other arithmetic  37.7 us (8%)
  local copies, waits for them, and re-layouts  32 us (7%)
  between operations  15 us (3%)
    pallas_call x21, Pallas kernels, kernel_call(): pl.pallas_call(body, out_shape=tuple(outs), in_specs=[smem] * len(scalars...  140 us
    ppermute x64, waiting for transfers between devices, swap(): lax.ppermute(value, axis, [(i, i ^ bit) for i in range(lax.axis_size(axis...  122 us
    ppermute x64, starting transfers between devices, swap(): lax.ppermute(value, axis, [(i, i ^ bit) for i in range(lax.axis_size(axis...  60.6 us
    ppermute x14, starting transfers between devices, from_chip(): return lax.ppermute(value, ('ctx', 'tp'), pairs)  32.4 us
    unnamed x164, local copies, waits for them, and re-layouts  21.9 us
    ppermute x14, waiting for transfers between devices, from_chip(): return lax.ppermute(value, ('ctx', 'tp'), pairs)  15.9 us
  transfers between devices with their start and end apart: 83, of which 39 were waited for; matrix products, arithmetic and copies ran while one was open for 11% of the time, Pallas kernels for 28%

profile of v2, /device:TPU:0, one launch (start us, length us, event | category | flops | bytes accessed | tf_op | source)
XLA Modules:
  0.0 462.4 jit_solution(2740950483473423324)
XLA Ops:
  22.2 11.1 %collective-permute-done.1 = bf16[160,1024]{1,0:T(8,128)(2,1)S(1)} collective-permute-done((bf16[160,1024]{1,0:T(8,128)(2,1)}, bf16[160,1024]{1,0:T(8,128)(2,1)S(1)}, u32[]{:S(2)}, u32[]{:S(2)}) %collective-permute-start.1) | collective-permute-done | bytes 327712 | tf_op jit(solution)/shard_map/ppermute | solution.py:533
  35.2 13.4 %collective-permute-done.3 = bf16[3,64,512]{1,2,0:T(8,128)(2,1)S(1)} collective-permute-done((bf16[3,64,512]{1,2,0:T(8,128)(2,1)S(1)}, bf16[3,64,512]{1,2,0:T(8,128)(2,1)S(1)}, u32[]{:S(2)}, u32[]{:S(2)}) %collective-permute-start.3) | collective-permute-done | bytes 196640 | tf_op jit(solution)/shard_map/ppermute | solution.py:533
  55.3 4.3 collective-permute-start.8
  63.1 7.3 %collective-permute-done.6 = bf16[160,1024]{1,0:T(8,128)(2,1)S(1)} collective-permute-done((bf16[160,1024]{1,0:T(8,128)(2,1)}, bf16[160,1024]{1,0:T(8,128)(2,1)S(1)}, u32[]{:S(2)}, u32[]{:S(2)}) %collective-permute-start.6) | collective-permute-done | bytes 327712 | tf_op jit(solution)/shard_map/ppermute | solution.py:533
  70.4 5.5 %collective-permute-done.5 = bf16[160,1024]{1,0:T(8,128)(2,1)S(1)} collective-permute-done((bf16[160,1024]{1,0:T(8,128)(2,1)}, bf16[160,1024]{1,0:T(8,128)(2,1)S(1)}, u32[]{:S(2)}, u32[]{:S(2)}) %collective-permute-start.5) | collective-permute-done | bytes 327712 | tf_op jit(solution)/shard_map/ppermute | solution.py:533
  85.0 4.3 cross_keys.1
  94.4 14.3 %self_attend.1 = (bf16[3,2048,128]{2,1,0:T(8,128)(2,1)}, f32[2,2048]{1,0:T(2,128)}, bf16[2,128,128]{2,1,0:T(8,128)(2,1)}, bf16[2,128,128]{2,1,0:T(8,128)(2,1)}, ...) custom-call(s32[2]{0:T(128)} %pad_add_fusion.at, ...), custom_call_target="tpu_custom_call" | custom-call | flops 3758096384 | bytes 8404992 | tf_op jit(solution)/shard_map/self_attend/pallas_call | solution.py:35
  112.3 9.7 %collective-permute-start.14 = (bf16[2,128,128]{2,1,0:T(8,128)(2,1)}, bf16[2,128,128]{2,1,0:T(8,128)(2,1)S(1)}, u32[]{:S(2)}, u32[]{:S(2)}) collective-permute-start(bf16[2,128,128]{2,1,0:T(8,128)(2,1)} %get-tuple-element.164.refs_1_), channel_id=1, source_target_pairs={{1,0},{0,1},{3,2},{2,3},{5,4},{4,5},{7,6},{6,7},{9,8},{8,9},{11,10... | collective-permute-start | bytes 196616 | tf_op jit(solution)/shard_map/ppermute | solution.py:557
  148.3 8.9 %collective-permute-done.22.y_own.refs_6_ = bf16[2,128,1024]{2,1,0:T(8,128)(2,1)S(1)} collective-permute-done((bf16[2,128,1024]{2,1,0:T(8,128)(2,1)S(1)}, bf16[2,128,1024]{2,1,0:T(8,128)(2,1)S(1)}, u32[]{:S(2)}, u32[]{:S(2)}) %collective-permute-start.22) | collective-permute-done | bytes 524320 | tf_op jit(solution)/shard_map/ppermute | solution.py:533
  157.2 10.8 %collective-permute-done.24.kv_far = bf16[4,128,512]{2,1,0:T(8,128)(2,1)S(1)} collective-permute-done((bf16[4,128,512]{2,1,0:T(8,128)(2,1)S(1)}, bf16[4,128,512]{2,1,0:T(8,128)(2,1)S(1)}, u32[]{:S(2)}, u32[]{:S(2)}) %collective-permute-start.24) | collective-permute-done | bytes 524320 | tf_op jit(solution)/shard_map/ppermute | solution.py:533
  169.5 7.5 %cross_attend.1 = (f32[2,128,1024]{2,1,0:T(8,128)}, bf16[2,128,1024]{2,1,0:T(8,128)(2,1)}, bf16[4,512,128]{2,1,0:T(8,128)(2,1)}, bf16[4,512,128]{2,1,0:T(8,128)(2,1)}, f32[16,256]{1,0:T(8,128)}) custom-call(s32[2]{0:T(128)} %lengths.3, s32[4]{0:T(128)} %iota_xor_fusion.t_of, bf16[2,128,1024]{2,1,0:T(8,128)(2,1)} %get-tuple-element.177.own_in.n_own, ...), custom_call_target="tpu_custom_call" | custom-call | flops 1342177280 | bytes 7880704 | tf_op jit(solution)/shard_map/cross_attend/pallas_call | solution.py:35
  184.3 12.8 %collective-permute-done.28.n_own.refs_2_ = bf16[2,128,1024]{2,1,0:T(8,128)(2,1)S(1)} collective-permute-done((bf16[2,128,1024]{2,1,0:T(8,128)(2,1)}, bf16[2,128,1024]{2,1,0:T(8,128)(2,1)S(1)}, u32[]{:S(2)}, u32[]{:S(2)}) %collective-permute-start.28) | collective-permute-done | bytes 524320 | tf_op jit(solution)/shard_map/ppermute | solution.py:533
  197.6 5.6 %all-gather.12.cloned.1.call-done = bf16[16,256,512]{2,1,0:T(8,128)(2,1)} async-done(((bf16[2,256,512]{2,1,0:T(8,128)(2,1)}), bf16[16,256,512]{2,1,0:T(8,128)(2,1)}) %all-gather.12.cloned.1.call-update) | async-done | bytes 4194320 | tf_op jit(solution)/shard_map/all_gather | solution.py:683
  204.2 9.3 %feed_forward.3 = (bf16[4,512,256]{2,1,0:T(8,128)(2,1)}, bf16[4,512,256]{2,1,0:T(8,128)(2,1)}, f32[2,128,1024]{2,1,0:T(8,128)}, bf16[2,128,1024]{2,1,0:T(8,128)(...) custom-call(bf16[2,128,1024]{2,1,0:T(8,128)(2,1)} %copy-done.61, bf16[2,128,1024]{2,1,0:T(8,128)(2,1)} %copy-done.64, ...), custom_call_target="tpu_custom_call" | custom-call | flops 4294967296 | bytes 11534336 | tf_op jit(solution)/shard_map/feed_forward/pallas_call | solution.py:35
  213.6 9.9 %feed_forward.2 = (bf16[4,512,256]{2,1,0:T(8,128)(2,1)}, bf16[4,512,256]{2,1,0:T(8,128)(2,1)}, f32[2,128,1024]{2,1,0:T(8,128)}, bf16[2,128,1024]{2,1,0:T(8,128)(...) custom-call(bf16[2,128,1024]{2,1,0:T(8,128)(2,1)} %get-tuple-element.181.n_own.refs_0_, ...), custom_call_target="tpu_custom_call" | custom-call | flops 4294967296 | bytes 11534336 | tf_op jit(solution)/shard_map/feed_forward/pallas_call | solution.py:35
  225.6 10.1 %grad_feed_forward.1 = bf16[2,4,2,256,512]{4,3,2,1,0:T(8,128)(2,1)} custom-call(bf16[4,512,256]{2,1,0:T(8,128)(2,1)} %get-tuple-element.193.d_near, bf16[4,512,256]{2,1,0:T(8,128)(2,1)} %get-tuple-element.194.d_far, bf16[4,512,256]{2,1,0:T(8,128)(2,1)} %get-tuple-element.195.a_near, bf16[4,512,256]{2,1,0:T(8,128)(2,1)} %get-tuple-element.196.a_far, ...), custom_call_target="tpu_custom_call" | custom-call | flops 4294967296 | bytes 12582912 | tf_op jit(solution)/shard_map/grad_feed_forward/pallas_call | solution.py:35
  248.3 11.7 %cross_attend_back.1 = (f32[2,128,1024]{2,1,0:T(8,128)}, bf16[2,128,1024]{2,1,0:T(8,128)(2,1)}, bf16[4,512,128]{2,1,0:T(8,128)(2,1)}, bf16[4,128,512]{2,1,0:T(8,128)(2,1)}, bf16[4,128,512]{2,1,0:T(8,128)(2,1)}) custom-call(s32[2]{0:T(128)} %lengths.3, s32[4]{0:T(128)} %iota_xor_fusion.t_of, bf16[2,128,1024]{2,1,0:T(8,128)(2,1)} %get-tuple-element.199.own_in.y_own, ...), custom_call_target="tpu_custom_call" | custom-call | flops 1879048192 | bytes 8929280 | tf_op jit(solution)/shard_map/cross_attend_back/pallas_call | solution.py:35
  260.0 5.2 %grad_cross.1 = (f32[4,2,2,64,512]{4,3,2,1,0:T(8,128)}, bf16[4,384,512]{2,1,0:T(8,128)(2,1)}) custom-call(bf16[4,512,128]{2,1,0:T(8,128)(2,1)} %get-tuple-element.206.dq, bf16[4,512,128]{2,1,0:T(8,128)(2,1)} %get-tuple-element.207.o, bf16[2,128,1024]{2,1,0:T(8,128)(2,1)} %get-tuple-element.177.own_in.n_own, bf16[2,128,1024]{2,1,0:T(8,128)(2,1)} %copy-done.34, ...), custom_call_target="tpu_custom_call" | custom-call | flops 1073741824 | bytes 7340032 | tf_op jit(solution)/shard_map/grad_cross/pallas_call | solution.py:35
  296.8 10.6 %collective-permute-done.43.refs_12_ = bf16[2,128,128]{2,1,0:T(8,128)(2,1)S(1)} collective-permute-done((bf16[2,128,128]{2,1,0:T(8,128)(2,1)}, bf16[2,128,128]{2,1,0:T(8,128)(2,1)S(1)}, u32[]{:S(2)}, u32[]{:S(2)}) %collective-permute-start.43) | collective-permute-done | bytes 65568 | tf_op jit(solution)/shard_map/ppermute | solution.py:557
  313.8 24.1 %self_attend_back.1 = (bf16[16,128,384]{2,1,0:T(8,128)(2,1)}, f32[2,4,128,1024]{3,2,1,0:T(8,128)}, bf16[2,4,128,1024]{3,2,1,0:T(8,128)(2,1)}) custom-call(s32[2]{0:T(128)} %pad_add_fusion.at, s32[32]{0:T(128)} %pad_add_fusion.1.order, bf16[3,2048,128]{2,1,0:T(8,128)(2,1)} %get-tuple-element.228.qkv, f32[2,2048]{1,0:T(2,128)} %get-tuple-element.229.lse, ...), custom_call_target="tpu_custom_call" | custom-call | flops 6979321856 | bytes 11550720 | tf_op jit(solution)/shard_map/self_attend_back/pallas_call | solution.py:35
  361.4 6.0 %collective-permute-done.57 = bf16[256,512]{1,0:T(8,128)(2,1)S(1)} collective-permute-done((bf16[256,512]{1,0:T(8,128)(2,1)S(1)}, bf16[256,512]{1,0:T(8,128)(2,1)S(1)}, u32[]{:S(2)}, u32[]{:S(2)}) %collective-permute-start.57) | collective-permute-done | bytes 262176 | tf_op jit(solution)/shard_map/ppermute | solution.py:533
  367.5 4.9 %collective-permute-done.53 = bf16[2,128,1024]{2,1,0:T(8,128)(2,1)S(1)} collective-permute-done((bf16[2,128,1024]{2,1,0:T(8,128)(2,1)S(1)}, bf16[2,128,1024]{2,1,0:T(8,128)(2,1)S(1)}, u32[]{:S(2)}, u32[]{:S(2)}) %collective-permute-start.53) | collective-permute-done | bytes 524320 | tf_op jit(solution)/shard_map/ppermute | solution.py:533
  398.7 6.7 %grad_qkv.1 = (f32[384,512]{1,0:T(8,128)}, bf16[384,512]{1,0:T(8,128)(2,1)}, f32[2,1024]{1,0:T(2,128)}) custom-call(s32[2]{0:T(128)} %pad_add_fusion.at, bf16[16,128,384]{2,1,0:T(8,128)(2,1)} %get-tuple-element.235.grads, bf16[4,160,1024]{2,1,0:T(8,128)(2,1)} %copy-done.2, bf16[4,160,1024]{2,1,0:T(8,128)(2,1)} %pad_maximum_fusion.2.refs_1_, ...), custom_call_target="tpu_custom_call" | custom-call | flops 1610612736 | bytes 9052160 | tf_op jit(solution)/shard_map/grad_qkv/pallas_call | solution.py:35
  428.5 4.7 %collective-permute-done.67 = f32[6,1024]{1,0:T(8,128)S(1)} collective-permute-done((f32[6,1024]{1,0:T(8,128)S(1)}, f32[6,1024]{1,0:T(8,128)S(1)}, u32[]{:S(2)}, u32[]{:S(2)}) %collective-permute-start.67) | collective-permute-done | bytes 24608 | tf_op jit(solution)/shard_map/ppermute | solution.py:533
  (403 shorter events, 228.6 us)
Async XLA Ops:
  7.2 130.3 %all-gather.10.cloned.1.call-start = ((), (), s32[]{:S(2)}) async-start(), calls=%async_computation.3 | async-start | bytes 3538944 | tf_op jit(solution)/shard_map/all_gather | solution.py:683
  12.6 20.7 %collective-permute-start.1 = (bf16[160,1024]{1,0:T(8,128)(2,1)}, bf16[160,1024]{1,0:T(8,128)(2,1)S(1)}, u32[]{:S(2)}, u32[]{:S(2)}) collective-permute-start(bf16[160,1024]{1,0:T(8,128)(2,1)} %get-tuple-element.146), channel_id=1, source_target_pairs={{0,2},{1,3},{2,0},{3,1},{4,6},{5,7},{6,4},{7,5},{8,10},{9,11},{10,... | collective-permute-start | bytes 983048 | tf_op jit(solution)/shard_map/ppermute | solution.py:533
  16.6 31.9 %collective-permute-start.4 = (bf16[160,1024]{1,0:T(8,128)(2,1)}, bf16[160,1024]{1,0:T(8,128)(2,1)S(1)}, u32[]{:S(2)}, u32[]{:S(2)}) collective-permute-start(bf16[160,1024]{1,0:T(8,128)(2,1)} %get-tuple-element.148), channel_id=1, source_target_pairs={{0,8},{4,12},{8,0},{12,4},{1,9},{5,13},{9,1},{13,5},{2,10},{6,14},... | collective-permute-start | bytes 983048 | tf_op jit(solution)/shard_map/ppermute | solution.py:533
  18.2 30.4 %collective-permute-start = (bf16[160,1024]{1,0:T(8,128)(2,1)}, bf16[160,1024]{1,0:T(8,128)(2,1)}, u32[]{:S(2)}, u32[]{:S(2)}) collective-permute-start(bf16[160,1024]{1,0:T(8,128)(2,1)} %get-tuple-element.145), channel_id=1, source_target_pairs={{0,1},{1,0},{2,3},{3,2},{4,5},{5,4},{6,7},{7,6},{8,9},{9,8},{10,11... | collective-permute-start | bytes 983048 | tf_op jit(solution)/shard_map/ppermute | solution.py:533
  19.7 28.8 %collective-permute-start.3 = (bf16[3,64,512]{1,2,0:T(8,128)(2,1)S(1)}, bf16[3,64,512]{1,2,0:T(8,128)(2,1)S(1)}, u32[]{:S(2)}, u32[]{:S(2)}) collective-permute-start(bf16[3,64,512]{1,2,0:T(8,128)(2,1)S(1)} %pad_maximum_fusion.9), channel_id=1, source_target_pairs={{0,2},{1,3},{2,0},{3,1},{4,6},{5,7},{6,4},{7,5},{8,10},{9,11},{10,... | collective-permute-start | bytes 589832 | tf_op jit(solution)/shard_map/ppermute | solution.py:533
  50.9 152.3 %all-gather.12.cloned.1.call-start = ((), (), s32[]{:S(2)}) async-start(), calls=%async_computation.4 | async-start | bytes 4718592 | tf_op jit(solution)/shard_map/all_gather | solution.py:683
  53.3 286.9 %reduce-scatter.2.cloned.1.call-start = ((), (), s32[]{:S(2)}) async-start(), calls=%async_computation.1 | async-start | bytes 4718592 | tf_op jit(solution)/shard_map/reduce_scatter | solution.py:826
  55.3 26.3 %collective-permute-start.8 = (bf16[512,512]{1,0:T(8,128)(2,1)S(1)}, bf16[512,512]{1,0:T(8,128)(2,1)S(1)}, u32[]{:S(2)}, u32[]{:S(2)}) collective-permute-start(bf16[512,512]{1,0:T(8,128)(2,1)S(1)} %pad_maximum_fusion.4.refs_4_.refs_16_.refs_0_), channel_id=1, source_target_pairs={{0,16},{16,0},{1,17},{17,1},{2,18},{18,2},{3,19},{19,3},{4,20},{20... | collective-permute-start | bytes 1572872 | tf_op jit(solution)/shard_map/ppermute | solution.py:533
  143.8 24.1 %collective-permute-start.24 = (bf16[4,128,512]{2,1,0:T(8,128)(2,1)S(1)}, bf16[4,128,512]{2,1,0:T(8,128)(2,1)S(1)}, u32[]{:S(2)}, u32[]{:S(2)}) collective-permute-start(bf16[4,128,512]{2,1,0:T(8,128)(2,1)S(1)} %pad_maximum_fusion.5.kv_own), channel_id=1, source_target_pairs={{0,8},{4,12},{8,0},{12,4},{1,9},{5,13},{9,1},{13,5},{2,10},{6,14},... | collective-permute-start | bytes 1572872 | tf_op jit(solution)/shard_map/ppermute | solution.py:533
  242.9 152.2 %all-gather.14.cloned.1.call-start = ((), (), s32[]{:S(2)}) async-start(), calls=%async_computation.5 | async-start | bytes 2621440 | tf_op jit(solution)/shard_map/all_gather | solution.py:829
  265.2 44.4 %collective-permute-start.37 = (bf16[4,384,512]{2,1,0:T(8,128)(2,1)}, bf16[4,384,512]{2,1,0:T(8,128)(2,1)S(1)}, u32[]{:S(2)}, u32[]{:S(2)}) collective-permute-start(bf16[4,384,512]{2,1,0:T(8,128)(2,1)} %get-tuple-element.210), channel_id=1, source_target_pairs={{0,8},{4,12},{8,0},{12,4},{1,9},{5,13},{9,1},{13,5},{2,10},{6,14},... | collective-permute-start | bytes 4718600 | tf_op jit(solution)/shard_map/ppermute | solution.py:533
  284.5 23.0 %collective-permute-start.43 = (bf16[2,128,128]{2,1,0:T(8,128)(2,1)}, bf16[2,128,128]{2,1,0:T(8,128)(2,1)S(1)}, u32[]{:S(2)}, u32[]{:S(2)}) collective-permute-start(bf16[2,128,128]{2,1,0:T(8,128)(2,1)} %get-tuple-element.219), channel_id=1, source_target_pairs={{8,0},{9,1},{10,2},{11,3},{12,4},{13,5},{14,6},{15,7},{0,8},{1,9},... | collective-permute-start | bytes 196616 | tf_op jit(solution)/shard_map/ppermute | solution.py:557
  286.6 20.8 %collective-permute-start.44 = (bf16[2,128,128]{2,1,0:T(8,128)(2,1)}, bf16[2,128,128]{2,1,0:T(8,128)(2,1)S(1)}, u32[]{:S(2)}, u32[]{:S(2)}) collective-permute-start(bf16[2,128,128]{2,1,0:T(8,128)(2,1)} %get-tuple-element.220), channel_id=1, source_target_pairs={{9,0},{8,1},{11,2},{10,3},{13,4},{12,5},{15,6},{14,7},{1,8},{0,9},... | collective-permute-start | bytes 196616 | tf_op jit(solution)/shard_map/ppermute | solution.py:557
  287.6 19.9 %collective-permute-start.45 = (bf16[2,128,128]{2,1,0:T(8,128)(2,1)}, bf16[2,128,128]{2,1,0:T(8,128)(2,1)S(1)}, u32[]{:S(2)}, u32[]{:S(2)}) collective-permute-start(bf16[2,128,128]{2,1,0:T(8,128)(2,1)} %get-tuple-element.221), channel_id=1, source_target_pairs={{10,0},{11,1},{8,2},{9,3},{14,4},{15,5},{12,6},{13,7},{2,8},{3,9},... | collective-permute-start | bytes 196616 | tf_op jit(solution)/shard_map/ppermute | solution.py:557
  307.5 30.5 %collective-permute-start.49 = (bf16[2,128,1024]{2,1,0:T(8,128)(2,1)}, bf16[2,128,1024]{2,1,0:T(8,128)(2,1)}, u32[]{:S(2)}, u32[]{:S(2)}) collective-permute-start(bf16[2,128,1024]{2,1,0:T(8,128)(2,1)} %add_convert_fusion.1), channel_id=1, source_target_pairs={{0,8},{4,12},{8,0},{12,4},{1,9},{5,13},{9,1},{13,5},{2,10},{6,14},... | collective-permute-start | bytes 1572872 | tf_op jit(solution)/shard_map/ppermute | solution.py:533
  309.2 28.8 %collective-permute-start.48 = (bf16[4,64,1024]{2,1,0:T(8,128)(2,1)}, bf16[4,64,1024]{2,1,0:T(8,128)(2,1)}, u32[]{:S(2)}, u32[]{:S(2)}) collective-permute-start(bf16[4,64,1024]{2,1,0:T(8,128)(2,1)} %get-tuple-element.233), channel_id=1, source_target_pairs={{0,8},{4,12},{8,0},{12,4},{1,9},{5,13},{9,1},{13,5},{2,10},{6,14},... | collective-permute-start | bytes 1572872 | tf_op jit(solution)/shard_map/ppermute | solution.py:533
  313.2 24.7 %collective-permute-start.47 = (bf16[4,2,64,512]{3,2,1,0:T(8,128)(2,1)S(1)}, bf16[4,2,64,512]{3,2,1,0:T(8,128)(2,1)S(1)}, u32[]{:S(2)}, u32[]{:S(2)}) collective-permute-start(bf16[4,2,64,512]{3,2,1,0:T(8,128)(2,1)S(1)} %fusion.2), channel_id=1, source_target_pairs={{0,16},{16,0},{1,17},{17,1},{2,18},{18,2},{3,19},{19,3},{4,20},{20... | collective-permute-start | bytes 1572872 | tf_op jit(solution)/shard_map/ppermute | solution.py:533
  340.2 86.7 %all-gather.8.cloned.1.call-start = ((), (), s32[]{:S(2)}) async-start(), calls=%async_computation.2 | async-start | bytes 1310720 | tf_op jit(solution)/shard_map/all_gather | solution.py:1010
  346.0 21.3 %collective-permute-start.57 = (bf16[256,512]{1,0:T(8,128)(2,1)S(1)}, bf16[256,512]{1,0:T(8,128)(2,1)S(1)}, u32[]{:S(2)}, u32[]{:S(2)}) collective-permute-start(bf16[256,512]{1,0:T(8,128)(2,1)S(1)} %get-tuple-element.344), channel_id=1, source_target_pairs={{0,2},{1,3},{2,0},{3,1},{4,6},{5,7},{6,4},{7,5},{8,10},{9,11},{10,... | collective-permute-start | bytes 786440 | tf_op jit(solution)/shard_map/ppermute | solution.py:533
  347.1 20.3 %collective-permute-start.58 = (bf16[256,512]{1,0:T(8,128)(2,1)S(1)}, bf16[256,512]{1,0:T(8,128)(2,1)S(1)}, u32[]{:S(2)}, u32[]{:S(2)}) collective-permute-start(bf16[256,512]{1,0:T(8,128)(2,1)S(1)} %get-tuple-element.343), channel_id=1, source_target_pairs={{0,3},{1,2},{2,1},{3,0},{4,7},{5,6},{6,5},{7,4},{8,11},{9,10},{10,... | collective-permute-start | bytes 786440 | tf_op jit(solution)/shard_map/ppermute | solution.py:533
  349.7 22.8 %collective-permute-start.53 = (bf16[2,128,1024]{2,1,0:T(8,128)(2,1)S(1)}, bf16[2,128,1024]{2,1,0:T(8,128)(2,1)S(1)}, u32[]{:S(2)}, u32[]{:S(2)}) collective-permute-start(bf16[2,128,1024]{2,1,0:T(8,128)(2,1)S(1)} %pad_maximum_fusion.8), channel_id=1, source_target_pairs={{0,8},{4,12},{8,0},{12,4},{1,9},{5,13},{9,1},{13,5},{2,10},{6,14},... | collective-permute-start | bytes 1572872 | tf_op jit(solution)/shard_map/ppermute | solution.py:533
  359.7 24.6 %collective-permute-start.51 = (bf16[2,128,1024]{2,1,0:T(8,128)(2,1)S(1)}, bf16[2,128,1024]{2,1,0:T(8,128)(2,1)S(1)}, u32[]{:S(2)}, u32[]{:S(2)}) collective-permute-start(bf16[2,128,1024]{2,1,0:T(8,128)(2,1)S(1)} %pad_maximum_fusion.7), channel_id=1, source_target_pairs={{0,8},{4,12},{8,0},{12,4},{1,9},{5,13},{9,1},{13,5},{2,10},{6,14},... | collective-permute-start | bytes 1572872 | tf_op jit(solution)/shard_map/ppermute | solution.py:533
  389.9 27.3 %collective-permute-start.52 = (bf16[128,1024]{1,0:T(8,128)(2,1)}, bf16[128,1024]{1,0:T(8,128)(2,1)S(1)}, u32[]{:S(2)}, u32[]{:S(2)}) collective-permute-start(bf16[128,1024]{1,0:T(8,128)(2,1)} %get-tuple-element.327), channel_id=1, source_target_pairs={{0,1},{1,0},{2,3},{3,2},{4,5},{5,4},{6,7},{7,6},{8,9},{9,8},{10,11... | collective-permute-start | bytes 786440 | tf_op jit(solution)/shard_map/ppermute | solution.py:533
  391.4 26.5 %collective-permute-start.55 = (bf16[128,1024]{1,0:T(8,128)(2,1)}, bf16[128,1024]{1,0:T(8,128)(2,1)}, u32[]{:S(2)}, u32[]{:S(2)}) collective-permute-start(bf16[128,1024]{1,0:T(8,128)(2,1)} %get-tuple-element.326), channel_id=1, source_target_pairs={{0,2},{1,3},{2,0},{3,1},{4,6},{5,7},{6,4},{7,5},{8,10},{9,11},{10,... | collective-permute-start | bytes 786440 | tf_op jit(solution)/shard_map/ppermute | solution.py:533
  (134 other events, 1240.7 us)
Sparse Core Ops, SparseCore 0:
  51.0 75.7 all-gather.9
  129.5 73.7 all-gather.11
  243.0 91.9 reduce-scatter.1
  340.3 30.5 all-gather.13
  384.5 21.0 all-gather.7

commit v3 on v2

--- a/solution.py
+++ b/solution.py
@@ -246,21 +246,27 @@
     return pack[i, t, j * 128 : (j + 1) * 128]
 
 
-def by_pair(own, got, pack, t, j):
-    return sum(
-        dot(chip_rows(own, got, cut(pack, i)), pair_of(pack, i, t, j), NT)
+def all_pairs(pack, i, t_of, tp, j):
+    return jnp.concatenate([pair_of(pack, i, t_of[e], j) for e in range(tp)], axis=0)
+
+
+def by_pairs(own, got, pack, t_of, j, out):
+    tp = out.shape[0]
+    total = sum(
+        dot(chip_rows(own, got, cut(pack, i)), all_pairs(pack, i, t_of, tp, j), NT)
         for i in range(pack.shape[0])
     ).astype(BF16)
+    for e in range(tp):
+        out[e] = total[:, e * 128 : (e + 1) * 128]
 
 
 def pairs_back(value, pack, t_of, j, own, send):
     seqs, rows = own.shape[0], own.shape[1]
     half = seqs * rows
+    left = jnp.concatenate([value[e] for e in range(value.shape[0])], axis=1)
     for i in range(pack.shape[0]):
         span = cut(pack, i)
-        total = sum(
-            dot(value[e], pair_of(pack, i, t_of[e], j), NN) for e in range(value.shape[0])
-        )
+        total = dot(left, all_pairs(pack, i, t_of, value.shape[0], j), NN)
         own[:, :, span] = total[:half].reshape(seqs, rows, -1)
         send[:, :, span] = total[half:].astype(BF16).reshape(seqs, rows, -1)
 
@@ -287,8 +293,7 @@
 def cross_kernel(tp, lengths, t_of, own_in, got_in, kv_own, kv_far, pack, own, send, q_out, o_out, lse):
     seqs, rows = own.shape[0], own.shape[1]
     keys = kv_own.shape[2] // seqs
-    for e in range(tp):
-        q_out[e] = by_pair(own_in, got_in, pack, t_of[e], 1)
+    by_pairs(own_in, got_in, pack, t_of, 1, q_out)
     col = lax.broadcasted_iota(jnp.int32, (2 * rows, keys), 1)
     for s in range(seqs):
         valid = col < lengths[s]
@@ -317,8 +322,7 @@
     own, send, dq_out, dkv_own, dkv_far, do_s = refs
     seqs, rows = own.shape[0], own.shape[1]
     keys = kv_own.shape[2] // seqs
-    for e in range(tp):
-        do_s[e] = by_pair(own_in, got_in, pack, t_of[e], 2)
+    by_pairs(own_in, got_in, pack, t_of, 2, do_s)
     key = lax.broadcasted_iota(jnp.int32, (keys, 2 * rows), 0)
     for s in range(seqs):
         valid = key < lengths[s]
@@ -352,12 +356,14 @@
     seqs, rows = n_own.shape[0], n_own.shape[1]
     half, parts, width = seqs * rows, weights.shape[0], weights.shape[4]
     spans = [slice(i * width, (i + 1) * width) for i in range(parts)]
+    n_rows = [chip_rows(n_own, n_got, span) for span in spans]
+    y_rows = [chip_rows(y_own, y_got, span) for span in spans]
     for e in range(tp):
         inner = sum(
-            dot(chip_rows(n_own, n_got, spans[i]), weights[i, e, 0], NT) for i in range(parts)
+            dot(n_rows[i], weights[i, e, 0], NT) for i in range(parts)
         )
         grad = sum(
-            dot(chip_rows(y_own, y_got, spans[i]), weights[i, e, 1], NT) for i in range(parts)
+            dot(y_rows[i], weights[i, e, 1], NT) for i in range(parts)
         )
         square = inner * inner
         bend = jnp.tanh(0.7978845608 * (inner + 0.044715 * square * inner))
@@ -367,8 +373,9 @@
         )
         d_inner[e] = (grad * slope).astype(BF16)
     for j, (out, send, rows_in) in enumerate(((d_own, d_send, d_inner), (o_own, o_send, active))):
+        left = jnp.concatenate([rows_in[e] for e in range(tp)], axis=1)
         for i in range(parts):
-            total = sum(dot(rows_in[e], weights[i, e, j], NN) for e in range(tp))
+            total = dot(left, weights[i, :, j].reshape(left.shape[1], width), NN)
             out[:, :, spans[i]] = total[:half].reshape(seqs, rows, -1)
             send[:, :, spans[i]] = total[half:].astype(BF16).reshape(seqs, rows, -1)
 
@@ -379,11 +386,18 @@
     for j, (near, far, given) in enumerate(
         ((d_near, d_far, n_rows), (a_near, a_far, y_rows))
     ):
-        for i in range(parts):
-            span = slice(i * width, (i + 1) * width)
-            first, second = chip_rows(given[0], given[1], span), chip_rows(given[2], given[3], span)
-            for e in range(tp):
-                out[i, e, j] = (dot(near[e], first, TN) + dot(far[e], second, TN)).astype(BF16)
+        right = jnp.concatenate(
+            [
+                chip_rows(given[0], given[1], slice(None)),
+                chip_rows(given[2], given[3], slice(None)),
+            ],
+            axis=0,
+        )
+        for e in range(tp):
+            left = jnp.concatenate([near[e], far[e]], axis=0)
+            value = dot(left, right, TN).astype(BF16)
+            for i in range(parts):
+                out[i, e, j] = value[:, i * width : (i + 1) * width]
 
 
 def cross_grad_kernel(tp, dq, o, n_own, n_got, y_own, y_got, dkv_far, keep, send):
@@ -453,12 +467,13 @@
     left = [grads[g * tp : (g + 1) * tp].reshape(-1, columns) for g in range(4)]
     ones = jnp.ones((8, left[0].shape[0]), BF16)
     counts = sum(dot(ones, part, NN) for part in left)
+    turned = [part.T for part in left]
     for i in range(n_parts):
         span = span_of(at, i, outs)
         total = 0.0
         for g in range(4):
             right = groups[g][:, :rows, span].reshape(left[g].shape[0], -1)
-            total = total + dot(left[g], right, TN)
+            total = total + dot(turned[g], right, NN)
         outs[i][...] = total.astype(outs[i].dtype)
         weight = weights[i][0:columns].astype(F32)
         sums[0:1, span] = jnp.sum(total * weight, axis=0, keepdims=True)
@@ -846,6 +861,8 @@
         [pltpu.VMEM((tp, chip, width), BF16)],
         flops=4 * chip * tp * width * (model + 3 * keys),
     )
+    out_far = swap_y(out_far)
+    dn_send = after(dn_send, out_far)
     dn_got = swap_core(dn_send)
     half = seqs * keys
     halves = model // half
@@ -889,7 +906,6 @@
     d_kv = dkv_own.astype(F32) + cross_got[:, -width:].astype(F32)
     first = lax.axis_index("fsdp") if n_parts == 2 else 0
     cross_x = swap(pick(g_cross, 1 - first, 1).astype(BF16), "fsdp", 1) if n_parts == 2 else None
-    out_far = swap_y(after(out_far, do_came))
     out_got = swap_y(after(out_send, do_came))
     d_qkv, dn_keep, dn_send = kernel_call(
         functools.partial(self_back_kernel, n_parts, tp, BLOCK),
@@ -934,7 +950,7 @@
     *g_qkv, sums_self = kernel_call(
         functools.partial(qkv_grad_kernel, n_parts, tp),
         "grad_qkv",
-        [after(at, dn_sent, grad_inner, grad_outer)],
+        [after(at, dn_upper, grad_inner, grad_outer)],
         [d_qkv, *groups, *h_qkv],
         (
             [shape((3 * width, model), F32)]
@@ -983,7 +999,7 @@
     )[0]
 
     sums = jnp.concatenate([sums_self, sums_cross, sums_ffn])
-    sums = sum_all(after(sums, dn_began))
+    sums = sum_all(after(sums, dn_other))
     grad_shift_self = sums[1]
     grad_gain_self = (sums[0] - shift_self * sums[1]) / gain_self
 

time: 465 us -> 460 us (0.989)
    unnamed x164 -> x170, local copies, waits for them, and re-layouts: 21.9 us -> 22.1 us
  transfers between devices with their start and end apart: 83 -> 83, of which waited for: 39 -> 33; matrix products, arithmetic and copies ran while one was open for 11% -> 11% of each run, Pallas kernels for 28% -> 28%
where the time goes in v3:
time: 460 us; the launch traced here: 456 us
  waiting for transfers between devices  140 us (30%)
  Pallas kernels  138 us (30%)
  starting transfers between devices  94.6 us (21%)
  other arithmetic  35.9 us (8%)
  local copies, waits for them, and re-layouts  32.2 us (7%)
  between operations  15.1 us (3%)
    pallas_call x21, Pallas kernels, kernel_call(): pl.pallas_call(body, out_shape=tuple(outs), in_specs=[smem] * len(scalars...  138 us
    ppermute x64, waiting for transfers between devices, swap(): lax.ppermute(value, axis, [(i, i ^ bit) for i in range(lax.axis_size(axis...  120 us
    ppermute x64, starting transfers between devices, swap(): lax.ppermute(value, axis, [(i, i ^ bit) for i in range(lax.axis_size(axis...  61.3 us
    ppermute x14, starting transfers between devices, from_chip(): return lax.ppermute(value, ('ctx', 'tp'), pairs)  33 us
    unnamed x170, local copies, waits for them, and re-layouts  22.1 us
    ppermute x14, waiting for transfers between devices, from_chip(): return lax.ppermute(value, ('ctx', 'tp'), pairs)  15.2 us
  transfers between devices with their start and end apart: 83, of which 33 were waited for; matrix products, arithmetic and copies ran while one was open for 11% of the time, Pallas kernels for 28%

profile of v3, /device:TPU:0, one launch (start us, length us, event | category | flops | bytes accessed | tf_op | source)
XLA Modules:
  0.0 455.9 jit_solution(16718654217359992641)
XLA Ops:
  22.2 11.1 %collective-permute-done.1 = bf16[160,1024]{1,0:T(8,128)(2,1)S(1)} collective-permute-done((bf16[160,1024]{1,0:T(8,128)(2,1)}, bf16[160,1024]{1,0:T(8,128)(2,1)S(1)}, u32[]{:S(2)}, u32[]{:S(2)}) %collective-permute-start.1) | collective-permute-done | bytes 327712 | tf_op jit(solution)/shard_map/ppermute | solution.py:548
  35.2 13.4 %collective-permute-done.3 = bf16[3,64,512]{1,2,0:T(8,128)(2,1)S(1)} collective-permute-done((bf16[3,64,512]{1,2,0:T(8,128)(2,1)S(1)}, bf16[3,64,512]{1,2,0:T(8,128)(2,1)S(1)}, u32[]{:S(2)}, u32[]{:S(2)}) %collective-permute-start.3) | collective-permute-done | bytes 196640 | tf_op jit(solution)/shard_map/ppermute | solution.py:548
  55.3 4.3 collective-permute-start.8
  63.1 7.3 %collective-permute-done.6 = bf16[160,1024]{1,0:T(8,128)(2,1)S(1)} collective-permute-done((bf16[160,1024]{1,0:T(8,128)(2,1)}, bf16[160,1024]{1,0:T(8,128)(2,1)S(1)}, u32[]{:S(2)}, u32[]{:S(2)}) %collective-permute-start.6) | collective-permute-done | bytes 327712 | tf_op jit(solution)/shard_map/ppermute | solution.py:548
  70.4 5.5 %collective-permute-done.5 = bf16[160,1024]{1,0:T(8,128)(2,1)S(1)} collective-permute-done((bf16[160,1024]{1,0:T(8,128)(2,1)}, bf16[160,1024]{1,0:T(8,128)(2,1)S(1)}, u32[]{:S(2)}, u32[]{:S(2)}) %collective-permute-start.5) | collective-permute-done | bytes 327712 | tf_op jit(solution)/shard_map/ppermute | solution.py:548
  85.0 4.3 cross_keys.1
  94.4 14.3 %self_attend.1 = (bf16[3,2048,128]{2,1,0:T(8,128)(2,1)}, f32[2,2048]{1,0:T(2,128)}, bf16[2,128,128]{2,1,0:T(8,128)(2,1)}, bf16[2,128,128]{2,1,0:T(8,128)(2,1)}, ...) custom-call(s32[2]{0:T(128)} %pad_add_fusion.at, ...), custom_call_target="tpu_custom_call" | custom-call | flops 3758096384 | bytes 8404992 | tf_op jit(solution)/shard_map/self_attend/pallas_call | solution.py:35
  112.3 9.7 %collective-permute-start.14 = (bf16[2,128,128]{2,1,0:T(8,128)(2,1)}, bf16[2,128,128]{2,1,0:T(8,128)(2,1)S(1)}, u32[]{:S(2)}, u32[]{:S(2)}) collective-permute-start(bf16[2,128,128]{2,1,0:T(8,128)(2,1)} %get-tuple-element.164.refs_1_), channel_id=1, source_target_pairs={{1,0},{0,1},{3,2},{2,3},{5,4},{4,5},{7,6},{6,7},{9,8},{8,9},{11,10... | collective-permute-start | bytes 196616 | tf_op jit(solution)/shard_map/ppermute | solution.py:572
  148.2 8.9 %collective-permute-done.22.y_own.refs_6_ = bf16[2,128,1024]{2,1,0:T(8,128)(2,1)S(1)} collective-permute-done((bf16[2,128,1024]{2,1,0:T(8,128)(2,1)S(1)}, bf16[2,128,1024]{2,1,0:T(8,128)(2,1)S(1)}, u32[]{:S(2)}, u32[]{:S(2)}) %collective-permute-start.22) | collective-permute-done | bytes 524320 | tf_op jit(solution)/shard_map/ppermute | solution.py:548
  157.0 10.8 %collective-permute-done.24.kv_far = bf16[4,128,512]{2,1,0:T(8,128)(2,1)S(1)} collective-permute-done((bf16[4,128,512]{2,1,0:T(8,128)(2,1)S(1)}, bf16[4,128,512]{2,1,0:T(8,128)(2,1)S(1)}, u32[]{:S(2)}, u32[]{:S(2)}) %collective-permute-start.24) | collective-permute-done | bytes 524320 | tf_op jit(solution)/shard_map/ppermute | solution.py:548
  169.4 6.9 %cross_attend.1 = (f32[2,128,1024]{2,1,0:T(8,128)}, bf16[2,128,1024]{2,1,0:T(8,128)(2,1)}, bf16[4,512,128]{2,1,0:T(8,128)(2,1)}, bf16[4,512,128]{2,1,0:T(8,128)(2,1)}, f32[16,256]{1,0:T(8,128)}) custom-call(s32[2]{0:T(128)} %lengths.3, s32[4]{0:T(128)} %iota_xor_fusion.t_of, bf16[2,128,1024]{2,1,0:T(8,128)(2,1)} %get-tuple-element.177.own_in.n_own, ...), custom_call_target="tpu_custom_call" | custom-call | flops 1342177280 | bytes 7880704 | tf_op jit(solution)/shard_map/cross_attend/pallas_call | solution.py:35
  183.7 12.7 %collective-permute-done.28.n_own.refs_2_ = bf16[2,128,1024]{2,1,0:T(8,128)(2,1)S(1)} collective-permute-done((bf16[2,128,1024]{2,1,0:T(8,128)(2,1)}, bf16[2,128,1024]{2,1,0:T(8,128)(2,1)S(1)}, u32[]{:S(2)}, u32[]{:S(2)}) %collective-permute-start.28) | collective-permute-done | bytes 524320 | tf_op jit(solution)/shard_map/ppermute | solution.py:548
  196.9 4.6 %all-gather.12.cloned.1.call-done = bf16[16,256,512]{2,1,0:T(8,128)(2,1)} async-done(((bf16[2,256,512]{2,1,0:T(8,128)(2,1)}), bf16[16,256,512]{2,1,0:T(8,128)(2,1)}) %all-gather.12.cloned.1.call-update) | async-done | bytes 4194320 | tf_op jit(solution)/shard_map/all_gather | solution.py:698
  202.5 9.2 %feed_forward.3 = (bf16[4,512,256]{2,1,0:T(8,128)(2,1)}, bf16[4,512,256]{2,1,0:T(8,128)(2,1)}, f32[2,128,1024]{2,1,0:T(8,128)}, bf16[2,128,1024]{2,1,0:T(8,128)(...) custom-call(bf16[2,128,1024]{2,1,0:T(8,128)(2,1)} %copy-done.65, bf16[2,128,1024]{2,1,0:T(8,128)(2,1)} %copy-done.67, ...), custom_call_target="tpu_custom_call" | custom-call | flops 4294967296 | bytes 11534336 | tf_op jit(solution)/shard_map/feed_forward/pallas_call | solution.py:35
  211.7 9.4 %feed_forward.2 = (bf16[4,512,256]{2,1,0:T(8,128)(2,1)}, bf16[4,512,256]{2,1,0:T(8,128)(2,1)}, f32[2,128,1024]{2,1,0:T(8,128)}, bf16[2,128,1024]{2,1,0:T(8,128)(...) custom-call(bf16[2,128,1024]{2,1,0:T(8,128)(2,1)} %get-tuple-element.181.n_own.refs_0_, ...), custom_call_target="tpu_custom_call" | custom-call | flops 4294967296 | bytes 11534336 | tf_op jit(solution)/shard_map/feed_forward/pallas_call | solution.py:35
  223.3 10.1 %grad_feed_forward.1 = bf16[2,4,2,256,512]{4,3,2,1,0:T(8,128)(2,1)} custom-call(bf16[4,512,256]{2,1,0:T(8,128)(2,1)} %get-tuple-element.193.d_near, bf16[4,512,256]{2,1,0:T(8,128)(2,1)} %get-tuple-element.194.d_far, bf16[4,512,256]{2,1,0:T(8,128)(2,1)} %get-tuple-element.195.a_near, bf16[4,512,256]{2,1,0:T(8,128)(2,1)} %get-tuple-element.196.a_far, ...), custom_call_target="tpu_custom_call" | custom-call | flops 4294967296 | bytes 12582912 | tf_op jit(solution)/shard_map/grad_feed_forward/pallas_call | solution.py:35
  246.0 10.8 %cross_attend_back.1 = (f32[2,128,1024]{2,1,0:T(8,128)}, bf16[2,128,1024]{2,1,0:T(8,128)(2,1)}, bf16[4,512,128]{2,1,0:T(8,128)(2,1)}, bf16[4,128,512]{2,1,0:T(8,128)(2,1)}, bf16[4,128,512]{2,1,0:T(8,128)(2,1)}) custom-call(s32[2]{0:T(128)} %lengths.3, s32[4]{0:T(128)} %iota_xor_fusion.t_of, bf16[2,128,1024]{2,1,0:T(8,128)(2,1)} %get-tuple-element.199.own_in.y_own, ...), custom_call_target="tpu_custom_call" | custom-call | flops 1879048192 | bytes 8929280 | tf_op jit(solution)/shard_map/cross_attend_back/pallas_call | solution.py:35
  256.8 5.2 %grad_cross.1 = (f32[4,2,2,64,512]{4,3,2,1,0:T(8,128)}, bf16[4,384,512]{2,1,0:T(8,128)(2,1)}) custom-call(bf16[4,512,128]{2,1,0:T(8,128)(2,1)} %get-tuple-element.206.dq, bf16[4,512,128]{2,1,0:T(8,128)(2,1)} %get-tuple-element.207.o, bf16[2,128,1024]{2,1,0:T(8,128)(2,1)} %get-tuple-element.177.own_in.n_own, bf16[2,128,1024]{2,1,0:T(8,128)(2,1)} %copy-done.36, ...), custom_call_target="tpu_custom_call" | custom-call | flops 1073741824 | bytes 7340032 | tf_op jit(solution)/shard_map/grad_cross/pallas_call | solution.py:35
  294.7 9.7 %collective-permute-done.44.refs_12_ = bf16[2,128,128]{2,1,0:T(8,128)(2,1)S(1)} collective-permute-done((bf16[2,128,128]{2,1,0:T(8,128)(2,1)}, bf16[2,128,128]{2,1,0:T(8,128)(2,1)S(1)}, u32[]{:S(2)}, u32[]{:S(2)}) %collective-permute-start.44) | collective-permute-done | bytes 65568 | tf_op jit(solution)/shard_map/ppermute | solution.py:572
  310.1 24.1 %self_attend_back.1 = (bf16[16,128,384]{2,1,0:T(8,128)(2,1)}, f32[2,4,128,1024]{3,2,1,0:T(8,128)}, bf16[2,4,128,1024]{3,2,1,0:T(8,128)(2,1)}) custom-call(s32[2]{0:T(128)} %pad_add_fusion.at, s32[32]{0:T(128)} %pad_add_fusion.1.order, bf16[3,2048,128]{2,1,0:T(8,128)(2,1)} %get-tuple-element.229.qkv, f32[2,2048]{1,0:T(2,128)} %get-tuple-element.230.lse, ...), custom_call_target="tpu_custom_call" | custom-call | flops 6979321856 | bytes 11550720 | tf_op jit(solution)/shard_map/self_attend_back/pallas_call | solution.py:35
  357.4 6.3 %collective-permute-done.57 = bf16[256,512]{1,0:T(8,128)(2,1)S(1)} collective-permute-done((bf16[256,512]{1,0:T(8,128)(2,1)S(1)}, bf16[256,512]{1,0:T(8,128)(2,1)S(1)}, u32[]{:S(2)}, u32[]{:S(2)}) %collective-permute-start.57) | collective-permute-done | bytes 262176 | tf_op jit(solution)/shard_map/ppermute | solution.py:548
  363.9 4.2 collective-permute-done.53
  394.5 6.7 %grad_qkv.1 = (f32[384,512]{1,0:T(8,128)}, bf16[384,512]{1,0:T(8,128)(2,1)}, f32[2,1024]{1,0:T(2,128)}) custom-call(s32[2]{0:T(128)} %pad_add_fusion.at, bf16[16,128,384]{2,1,0:T(8,128)(2,1)} %get-tuple-element.235.grads, bf16[4,160,1024]{2,1,0:T(8,128)(2,1)} %copy-done.2, bf16[4,160,1024]{2,1,0:T(8,128)(2,1)} %pad_maximum_fusion.2.refs_1_, ...), custom_call_target="tpu_custom_call" | custom-call | flops 1610612736 | bytes 9052160 | tf_op jit(solution)/shard_map/grad_qkv/pallas_call | solution.py:35
  422.4 5.0 %collective-permute-done.67 = f32[6,1024]{1,0:T(8,128)S(1)} collective-permute-done((f32[6,1024]{1,0:T(8,128)S(1)}, f32[6,1024]{1,0:T(8,128)S(1)}, u32[]{:S(2)}, u32[]{:S(2)}) %collective-permute-start.67) | collective-permute-done | bytes 24608 | tf_op jit(solution)/shard_map/ppermute | solution.py:548
  (409 shorter events, 226.2 us)
Async XLA Ops:
  7.2 130.3 %all-gather.10.cloned.1.call-start = ((), (), s32[]{:S(2)}) async-start(), calls=%async_computation.3 | async-start | bytes 3538944 | tf_op jit(solution)/shard_map/all_gather | solution.py:698
  12.6 20.7 %collective-permute-start.1 = (bf16[160,1024]{1,0:T(8,128)(2,1)}, bf16[160,1024]{1,0:T(8,128)(2,1)S(1)}, u32[]{:S(2)}, u32[]{:S(2)}) collective-permute-start(bf16[160,1024]{1,0:T(8,128)(2,1)} %get-tuple-element.146), channel_id=1, source_target_pairs={{0,2},{1,3},{2,0},{3,1},{4,6},{5,7},{6,4},{7,5},{8,10},{9,11},{10,... | collective-permute-start | bytes 983048 | tf_op jit(solution)/shard_map/ppermute | solution.py:548
  16.6 31.9 %collective-permute-start.4 = (bf16[160,1024]{1,0:T(8,128)(2,1)}, bf16[160,1024]{1,0:T(8,128)(2,1)S(1)}, u32[]{:S(2)}, u32[]{:S(2)}) collective-permute-start(bf16[160,1024]{1,0:T(8,128)(2,1)} %get-tuple-element.148), channel_id=1, source_target_pairs={{0,8},{4,12},{8,0},{12,4},{1,9},{5,13},{9,1},{13,5},{2,10},{6,14},... | collective-permute-start | bytes 983048 | tf_op jit(solution)/shard_map/ppermute | solution.py:548
  18.2 30.4 %collective-permute-start = (bf16[160,1024]{1,0:T(8,128)(2,1)}, bf16[160,1024]{1,0:T(8,128)(2,1)}, u32[]{:S(2)}, u32[]{:S(2)}) collective-permute-start(bf16[160,1024]{1,0:T(8,128)(2,1)} %get-tuple-element.145), channel_id=1, source_target_pairs={{0,1},{1,0},{2,3},{3,2},{4,5},{5,4},{6,7},{7,6},{8,9},{9,8},{10,11... | collective-permute-start | bytes 983048 | tf_op jit(solution)/shard_map/ppermute | solution.py:548
  19.7 28.8 %collective-permute-start.3 = (bf16[3,64,512]{1,2,0:T(8,128)(2,1)S(1)}, bf16[3,64,512]{1,2,0:T(8,128)(2,1)S(1)}, u32[]{:S(2)}, u32[]{:S(2)}) collective-permute-start(bf16[3,64,512]{1,2,0:T(8,128)(2,1)S(1)} %pad_maximum_fusion.9), channel_id=1, source_target_pairs={{0,2},{1,3},{2,0},{3,1},{4,6},{5,7},{6,4},{7,5},{8,10},{9,11},{10,... | collective-permute-start | bytes 589832 | tf_op jit(solution)/shard_map/ppermute | solution.py:548
  50.9 150.6 %all-gather.12.cloned.1.call-start = ((), (), s32[]{:S(2)}) async-start(), calls=%async_computation.4 | async-start | bytes 4718592 | tf_op jit(solution)/shard_map/all_gather | solution.py:698
  53.3 283.1 %reduce-scatter.2.cloned.1.call-start = ((), (), s32[]{:S(2)}) async-start(), calls=%async_computation.1 | async-start | bytes 4718592 | tf_op jit(solution)/shard_map/reduce_scatter | solution.py:841
  55.3 26.3 %collective-permute-start.8 = (bf16[512,512]{1,0:T(8,128)(2,1)S(1)}, bf16[512,512]{1,0:T(8,128)(2,1)S(1)}, u32[]{:S(2)}, u32[]{:S(2)}) collective-permute-start(bf16[512,512]{1,0:T(8,128)(2,1)S(1)} %pad_maximum_fusion.4.refs_4_.refs_16_.refs_0_), channel_id=1, source_target_pairs={{0,16},{16,0},{1,17},{17,1},{2,18},{18,2},{3,19},{19,3},{4,20},{20... | collective-permute-start | bytes 1572872 | tf_op jit(solution)/shard_map/ppermute | solution.py:548
  63.1 19.8 %collective-permute-start.9 = (bf16[4,160,1024]{2,1,0:T(8,128)(2,1)S(1)}, bf16[4,160,1024]{2,1,0:T(8,128)(2,1)}, u32[]{:S(2)}, u32[]{:S(2)}) collective-permute-start(bf16[4,160,1024]{2,1,0:T(8,128)(2,1)S(1)} %pad_maximum_fusion.1.refs_0_), channel_id=1, source_target_pairs={{0,4},{4,0},{8,12},{12,8},{1,5},{5,1},{9,13},{13,9},{2,6},{6,2},{1... | collective-permute-start | bytes 3932168 | tf_op jit(solution)/shard_map/ppermute | solution.py:548
  143.7 24.1 %collective-permute-start.24 = (bf16[4,128,512]{2,1,0:T(8,128)(2,1)S(1)}, bf16[4,128,512]{2,1,0:T(8,128)(2,1)S(1)}, u32[]{:S(2)}, u32[]{:S(2)}) collective-permute-start(bf16[4,128,512]{2,1,0:T(8,128)(2,1)S(1)} %pad_maximum_fusion.5.kv_own), channel_id=1, source_target_pairs={{0,8},{4,12},{8,0},{12,4},{1,9},{5,13},{9,1},{13,5},{2,10},{6,14},... | collective-permute-start | bytes 1572872 | tf_op jit(solution)/shard_map/ppermute | solution.py:548
  148.0 19.8 %collective-permute-start.23 = (bf16[2,128,1024]{2,1,0:T(8,128)(2,1)}, bf16[2,128,1024]{2,1,0:T(8,128)(2,1)S(1)}, u32[]{:S(2)}, u32[]{:S(2)}) collective-permute-start(bf16[2,128,1024]{2,1,0:T(8,128)(2,1)} %get-tuple-element.177.own_in.n_own), channel_id=1, source_target_pairs={{0,4},{4,0},{8,12},{12,8},{1,5},{5,1},{9,13},{13,9},{2,6},{6,2},{1... | collective-permute-start | bytes 1572872 | tf_op jit(solution)/shard_map/ppermute | solution.py:548
  240.6 150.3 %all-gather.14.cloned.1.call-start = ((), (), s32[]{:S(2)}) async-start(), calls=%async_computation.5 | async-start | bytes 2621440 | tf_op jit(solution)/shard_map/all_gather | solution.py:844
  243.7 19.9 %collective-permute-start.38 = (bf16[2,128,1024]{2,1,0:T(8,128)(2,1)S(1)}, bf16[2,128,1024]{2,1,0:T(8,128)(2,1)S(1)}, u32[]{:S(2)}, u32[]{:S(2)}) collective-permute-start(bf16[2,128,1024]{2,1,0:T(8,128)(2,1)S(1)} %add_convert_fusion.1), channel_id=1, source_target_pairs={{0,8},{4,12},{8,0},{12,4},{1,9},{5,13},{9,1},{13,5},{2,10},{6,14},... | collective-permute-start | bytes 1572872 | tf_op jit(solution)/shard_map/ppermute | solution.py:548
  262.0 44.0 %collective-permute-start.37 = (bf16[4,384,512]{2,1,0:T(8,128)(2,1)}, bf16[4,384,512]{2,1,0:T(8,128)(2,1)S(1)}, u32[]{:S(2)}, u32[]{:S(2)}) collective-permute-start(bf16[4,384,512]{2,1,0:T(8,128)(2,1)} %get-tuple-element.210), channel_id=1, source_target_pairs={{0,8},{4,12},{8,0},{12,4},{1,9},{5,13},{9,1},{13,5},{2,10},{6,14},... | collective-permute-start | bytes 4718600 | tf_op jit(solution)/shard_map/ppermute | solution.py:548
  281.5 22.8 %collective-permute-start.44 = (bf16[2,128,128]{2,1,0:T(8,128)(2,1)}, bf16[2,128,128]{2,1,0:T(8,128)(2,1)S(1)}, u32[]{:S(2)}, u32[]{:S(2)}) collective-permute-start(bf16[2,128,128]{2,1,0:T(8,128)(2,1)} %get-tuple-element.220), channel_id=1, source_target_pairs={{8,0},{9,1},{10,2},{11,3},{12,4},{13,5},{14,6},{15,7},{0,8},{1,9},... | collective-permute-start | bytes 196616 | tf_op jit(solution)/shard_map/ppermute | solution.py:572
  284.5 19.8 %collective-permute-start.45 = (bf16[2,128,128]{2,1,0:T(8,128)(2,1)}, bf16[2,128,128]{2,1,0:T(8,128)(2,1)S(1)}, u32[]{:S(2)}, u32[]{:S(2)}) collective-permute-start(bf16[2,128,128]{2,1,0:T(8,128)(2,1)} %get-tuple-element.221), channel_id=1, source_target_pairs={{9,0},{8,1},{11,2},{10,3},{13,4},{12,5},{15,6},{14,7},{1,8},{0,9},... | collective-permute-start | bytes 196616 | tf_op jit(solution)/shard_map/ppermute | solution.py:572
  304.4 29.9 %collective-permute-start.49 = (bf16[4,64,1024]{2,1,0:T(8,128)(2,1)}, bf16[4,64,1024]{2,1,0:T(8,128)(2,1)}, u32[]{:S(2)}, u32[]{:S(2)}) collective-permute-start(bf16[4,64,1024]{2,1,0:T(8,128)(2,1)} %get-tuple-element.234), channel_id=1, source_target_pairs={{0,8},{4,12},{8,0},{12,4},{1,9},{5,13},{9,1},{13,5},{2,10},{6,14},... | collective-permute-start | bytes 1572872 | tf_op jit(solution)/shard_map/ppermute | solution.py:548
  309.4 24.9 %collective-permute-start.48 = (bf16[4,2,64,512]{3,2,1,0:T(8,128)(2,1)S(1)}, bf16[4,2,64,512]{3,2,1,0:T(8,128)(2,1)S(1)}, u32[]{:S(2)}, u32[]{:S(2)}) collective-permute-start(bf16[4,2,64,512]{3,2,1,0:T(8,128)(2,1)S(1)} %fusion.2), channel_id=1, source_target_pairs={{0,16},{16,0},{1,17},{17,1},{2,18},{18,2},{3,19},{19,3},{4,20},{20... | collective-permute-start | bytes 1572872 | tf_op jit(solution)/shard_map/ppermute | solution.py:548
  336.5 84.4 %all-gather.8.cloned.1.call-start = ((), (), s32[]{:S(2)}) async-start(), calls=%async_computation.2 | async-start | bytes 1310720 | tf_op jit(solution)/shard_map/all_gather | solution.py:1026
  342.4 21.3 %collective-permute-start.57 = (bf16[256,512]{1,0:T(8,128)(2,1)S(1)}, bf16[256,512]{1,0:T(8,128)(2,1)S(1)}, u32[]{:S(2)}, u32[]{:S(2)}) collective-permute-start(bf16[256,512]{1,0:T(8,128)(2,1)S(1)} %get-tuple-element.344), channel_id=1, source_target_pairs={{0,2},{1,3},{2,0},{3,1},{4,6},{5,7},{6,4},{7,5},{8,10},{9,11},{10,... | collective-permute-start | bytes 786440 | tf_op jit(solution)/shard_map/ppermute | solution.py:548
  343.4 20.4 %collective-permute-start.58 = (bf16[256,512]{1,0:T(8,128)(2,1)S(1)}, bf16[256,512]{1,0:T(8,128)(2,1)S(1)}, u32[]{:S(2)}, u32[]{:S(2)}) collective-permute-start(bf16[256,512]{1,0:T(8,128)(2,1)S(1)} %get-tuple-element.343), channel_id=1, source_target_pairs={{0,3},{1,2},{2,1},{3,0},{4,7},{5,6},{6,5},{7,4},{8,11},{9,10},{10,... | collective-permute-start | bytes 786440 | tf_op jit(solution)/shard_map/ppermute | solution.py:548
  345.9 22.2 %collective-permute-start.53 = (bf16[2,128,1024]{2,1,0:T(8,128)(2,1)S(1)}, bf16[2,128,1024]{2,1,0:T(8,128)(2,1)S(1)}, u32[]{:S(2)}, u32[]{:S(2)}) collective-permute-start(bf16[2,128,1024]{2,1,0:T(8,128)(2,1)S(1)} %pad_maximum_fusion.8), channel_id=1, source_target_pairs={{0,8},{4,12},{8,0},{12,4},{1,9},{5,13},{9,1},{13,5},{2,10},{6,14},... | collective-permute-start | bytes 1572872 | tf_op jit(solution)/shard_map/ppermute | solution.py:548
  355.5 24.6 %collective-permute-start.51 = (bf16[2,128,1024]{2,1,0:T(8,128)(2,1)S(1)}, bf16[2,128,1024]{2,1,0:T(8,128)(2,1)S(1)}, u32[]{:S(2)}, u32[]{:S(2)}) collective-permute-start(bf16[2,128,1024]{2,1,0:T(8,128)(2,1)S(1)} %pad_maximum_fusion.7), channel_id=1, source_target_pairs={{0,8},{4,12},{8,0},{12,4},{1,9},{5,13},{9,1},{13,5},{2,10},{6,14},... | collective-permute-start | bytes 1572872 | tf_op jit(solution)/shard_map/ppermute | solution.py:548
  388.0 23.7 %collective-permute-start.52 = (bf16[128,1024]{1,0:T(8,128)(2,1)}, bf16[128,1024]{1,0:T(8,128)(2,1)}, u32[]{:S(2)}, u32[]{:S(2)}) collective-permute-start(bf16[128,1024]{1,0:T(8,128)(2,1)} %get-tuple-element.327), channel_id=1, source_target_pairs={{0,1},{1,0},{2,3},{3,2},{4,5},{5,4},{6,7},{7,6},{8,9},{9,8},{10,11... | collective-permute-start | bytes 786440 | tf_op jit(solution)/shard_map/ppermute | solution.py:548
  (137 other events, 1242.7 us)
Sparse Core Ops, SparseCore 0:
  51.0 74.9 all-gather.9
  128.7 72.7 all-gather.11
  240.7 93.7 reduce-scatter.1
  336.6 29.3 all-gather.13
  380.2 21.0 all-gather.7

commit v4 on v3

--- a/solution.py
+++ b/solution.py
@@ -539,7 +539,7 @@
             span = span_of(at, i, weights)
             value = dot(left, weights[i][0 : 3 * width], NN).reshape(tp, rows, -1)
             if g < 2:
-                keep[g, :, :, span] = value
+                keep[g, :, :, span] = value.astype(BF16)
             else:
                 send[g - 2, :, :, span] = value.astype(BF16)
 
@@ -749,7 +749,7 @@
         [pltpu.VMEM((4 * tp, rows, width), BF16)],
         flops=4 * length * length * width + 6 * length * model * width,
     )
-    o_sent = after(o_sent, kv_own)
+    o_sent = after(o_sent, kv_own, y_far)
     kv_far = swap_y(kv_own)
     came = [
         from_chip(o_sent[ys * tp + e], ys, e) for ys in range(2) for e in range(tp)
@@ -779,7 +779,7 @@
     partial_own, partial_send, q_cross, o_cross, lse_cross = kernel_call(
         functools.partial(cross_kernel, tp),
         "cross_attend",
-        [enc_lengths, after(t_of, y_far)],
+        [enc_lengths, t_of],
         [n2, n2_got, kv_own, kv_far, pack],
         [
             shape(own_rows, F32),
@@ -839,7 +839,7 @@
     if n_parts == 1:
         g_ffn = g_ffn.reshape(tp, 2, hid, -1, local).transpose(3, 0, 1, 2, 4)
     g_ffn = lax.psum_scatter(
-        after(g_ffn.reshape(-1, 2, hid, local), y2), ("fsdp", "tp"), scatter_dimension=0
+        after(g_ffn.reshape(-1, 2, hid, local), dn_far), ("fsdp", "tp"), scatter_dimension=0
     )
     g_ffn = lax.all_gather(g_ffn.astype(BF16), "ctx", axis=1, tiled=True)
 
@@ -914,7 +914,7 @@
         [qkv, lse_self, *o_sent, *do_came, *h_qkv],
         [
             shape((4 * tp, rows, 3 * width), BF16),
-            shape((2, tp, rows, model), F32),
+            shape((2, tp, rows, model), BF16),
             shape((2, tp, rows, model), BF16),
         ],
         [
@@ -928,8 +928,10 @@
         (dn_send, dn_keep, cross_x, out_got, out_far), d_qkv
     )
     dn_got = swap_core(dn_send)
-    dn_sent = [(dn_keep[1, e] + dn_got[1, e].astype(F32)).astype(BF16) for e in range(tp)]
-    dn_near = [dn_keep[0, e] + dn_got[0, e].astype(F32) for e in range(tp)]
+    dn_sent = [(dn_keep[1, e].astype(F32) + dn_got[1, e].astype(F32)).astype(BF16) for e in range(tp)]
+    dn_near = [
+        dn_keep[0, e].astype(F32) + dn_got[0, e].astype(F32) for e in range(tp)
+    ]
     g_cross, d_kv, cross_x, out_got, out_far = after(
         (g_cross, d_kv, cross_x, out_got, out_far), dn_sent
     )

time: 460 us -> 458 us (level)
    ppermute x64, waiting for transfers between devices: 120 us -> 108 us  [swap(): lax.ppermute(value, axis, [(i, i ^ bit) for i in range(lax.axis_size(axis...]
    all_gather x2, waiting for transfers between devices: 4.63 us -> 15.3 us  [gather_weights(): got = lax.all_gather(value, ('fsdp', 'tp'))]
  transfers between devices with their start and end apart: 83 -> 83, of which waited for: 33 -> 33; matrix products, arithmetic and copies ran while one was open for 11% -> 11% of each run, Pallas kernels for 28% -> 29%
where the time goes in v4:
time: 458 us; the launch traced here: 454 us
  waiting for transfers between devices  141 us (31%)
  Pallas kernels  137 us (30%)
  starting transfers between devices  92.3 us (20%)
  other arithmetic  36.6 us (8%)
  local copies, waits for them, and re-layouts  31.5 us (7%)
  between operations  15.1 us (3%)
    pallas_call x21, Pallas kernels, kernel_call(): pl.pallas_call(body, out_shape=tuple(outs), in_specs=[smem] * len(scalars...  137 us
    ppermute x64, waiting for transfers between devices, swap(): lax.ppermute(value, axis, [(i, i ^ bit) for i in range(lax.axis_size(axis...  108 us
    ppermute x64, starting transfers between devices, swap(): lax.ppermute(value, axis, [(i, i ^ bit) for i in range(lax.axis_size(axis...  62 us
    ppermute x14, starting transfers between devices, from_chip(): return lax.ppermute(value, ('ctx', 'tp'), pairs)  29.9 us
    unnamed x170, local copies, waits for them, and re-layouts  21.4 us
    ppermute x14, waiting for transfers between devices, from_chip(): return lax.ppermute(value, ('ctx', 'tp'), pairs)  18.1 us
    all_gather x2, waiting for transfers between devices, gather_weights(): got = lax.all_gather(value, ('fsdp', 'tp'))  15.3 us
  transfers between devices with their start and end apart: 83, of which 33 were waited for; matrix products, arithmetic and copies ran while one was open for 11% of the time, Pallas kernels for 29%

profile of v4, /device:TPU:0, one launch (start us, length us, event | category | flops | bytes accessed | tf_op | source)
XLA Modules:
  0.0 453.5 jit_solution(16967414525756058403)
XLA Ops:
  22.2 11.1 %collective-permute-done.1 = bf16[160,1024]{1,0:T(8,128)(2,1)S(1)} collective-permute-done((bf16[160,1024]{1,0:T(8,128)(2,1)}, bf16[160,1024]{1,0:T(8,128)(2,1)S(1)}, u32[]{:S(2)}, u32[]{:S(2)}) %collective-permute-start.1) | collective-permute-done | bytes 327712 | tf_op jit(solution)/shard_map/ppermute | solution.py:548
  35.2 13.4 %collective-permute-done.3 = bf16[3,64,512]{1,2,0:T(8,128)(2,1)S(1)} collective-permute-done((bf16[3,64,512]{1,2,0:T(8,128)(2,1)S(1)}, bf16[3,64,512]{1,2,0:T(8,128)(2,1)S(1)}, u32[]{:S(2)}, u32[]{:S(2)}) %collective-permute-start.3) | collective-permute-done | bytes 196640 | tf_op jit(solution)/shard_map/ppermute | solution.py:548
  55.3 4.3 collective-permute-start.8
  63.1 7.3 %collective-permute-done.6 = bf16[160,1024]{1,0:T(8,128)(2,1)S(1)} collective-permute-done((bf16[160,1024]{1,0:T(8,128)(2,1)}, bf16[160,1024]{1,0:T(8,128)(2,1)S(1)}, u32[]{:S(2)}, u32[]{:S(2)}) %collective-permute-start.6) | collective-permute-done | bytes 327712 | tf_op jit(solution)/shard_map/ppermute | solution.py:548
  70.4 5.5 %collective-permute-done.5 = bf16[160,1024]{1,0:T(8,128)(2,1)S(1)} collective-permute-done((bf16[160,1024]{1,0:T(8,128)(2,1)}, bf16[160,1024]{1,0:T(8,128)(2,1)S(1)}, u32[]{:S(2)}, u32[]{:S(2)}) %collective-permute-start.5) | collective-permute-done | bytes 327712 | tf_op jit(solution)/shard_map/ppermute | solution.py:548
  85.0 4.3 cross_keys.1
  94.4 14.3 %self_attend.1 = (bf16[3,2048,128]{2,1,0:T(8,128)(2,1)}, f32[2,2048]{1,0:T(2,128)}, bf16[2,128,128]{2,1,0:T(8,128)(2,1)}, bf16[2,128,128]{2,1,0:T(8,128)(2,1)}, ...) custom-call(s32[2]{0:T(128)} %pad_add_fusion.at, ...), custom_call_target="tpu_custom_call" | custom-call | flops 3758096384 | bytes 8404992 | tf_op jit(solution)/shard_map/self_attend/pallas_call | solution.py:35
  112.7 9.7 %collective-permute-start.15 = (bf16[2,128,128]{2,1,0:T(8,128)(2,1)}, bf16[2,128,128]{2,1,0:T(8,128)(2,1)S(1)}, u32[]{:S(2)}, u32[]{:S(2)}) collective-permute-start(bf16[2,128,128]{2,1,0:T(8,128)(2,1)} %get-tuple-element.164.refs_1_), channel_id=1, source_target_pairs={{1,0},{0,1},{3,2},{2,3},{5,4},{4,5},{7,6},{6,7},{9,8},{8,9},{11,10... | collective-permute-start | bytes 196616 | tf_op jit(solution)/shard_map/ppermute | solution.py:572
  130.2 4.2 collective-permute-start.21
  148.1 8.4 %collective-permute-done.24.kv_far = bf16[4,128,512]{2,1,0:T(8,128)(2,1)S(1)} collective-permute-done((bf16[4,128,512]{2,1,0:T(8,128)(2,1)S(1)}, bf16[4,128,512]{2,1,0:T(8,128)(2,1)S(1)}, u32[]{:S(2)}, u32[]{:S(2)}) %collective-permute-start.24) | collective-permute-done | bytes 524320 | tf_op jit(solution)/shard_map/ppermute | solution.py:548
  158.2 6.9 %cross_attend.1 = (f32[2,128,1024]{2,1,0:T(8,128)}, bf16[2,128,1024]{2,1,0:T(8,128)(2,1)}, bf16[4,512,128]{2,1,0:T(8,128)(2,1)}, bf16[4,512,128]{2,1,0:T(8,128)(2,1)}, f32[16,256]{1,0:T(8,128)}) custom-call(s32[2]{0:T(128)} %lengths.3, s32[4]{0:T(128)} %iota_xor_fusion.t_of, bf16[2,128,1024]{2,1,0:T(8,128)(2,1)} %get-tuple-element.175.own_in.n_own, ...), custom_call_target="tpu_custom_call" | custom-call | flops 1342177280 | bytes 7880704 | tf_op jit(solution)/shard_map/cross_attend/pallas_call | solution.py:35
  172.5 12.7 %collective-permute-done.28.n_own.refs_2_ = bf16[2,128,1024]{2,1,0:T(8,128)(2,1)S(1)} collective-permute-done((bf16[2,128,1024]{2,1,0:T(8,128)(2,1)}, bf16[2,128,1024]{2,1,0:T(8,128)(2,1)S(1)}, u32[]{:S(2)}, u32[]{:S(2)}) %collective-permute-start.28) | collective-permute-done | bytes 524320 | tf_op jit(solution)/shard_map/ppermute | solution.py:548
  185.6 15.3 %all-gather.12.cloned.1.call-done = bf16[16,256,512]{2,1,0:T(8,128)(2,1)} async-done(((bf16[2,256,512]{2,1,0:T(8,128)(2,1)}), bf16[16,256,512]{2,1,0:T(8,128)(2,1)}) %all-gather.12.cloned.1.call-update) | async-done | bytes 4194320 | tf_op jit(solution)/shard_map/all_gather | solution.py:698
  201.9 9.1 %feed_forward.3 = (bf16[4,512,256]{2,1,0:T(8,128)(2,1)}, bf16[4,512,256]{2,1,0:T(8,128)(2,1)}, f32[2,128,1024]{2,1,0:T(8,128)}, bf16[2,128,1024]{2,1,0:T(8,128)(...) custom-call(bf16[2,128,1024]{2,1,0:T(8,128)(2,1)} %copy-done.66, bf16[2,128,1024]{2,1,0:T(8,128)(2,1)} %copy-done.68, ...), custom_call_target="tpu_custom_call" | custom-call | flops 4294967296 | bytes 11534336 | tf_op jit(solution)/shard_map/feed_forward/pallas_call | solution.py:35
  211.1 9.5 %feed_forward.2 = (bf16[4,512,256]{2,1,0:T(8,128)(2,1)}, bf16[4,512,256]{2,1,0:T(8,128)(2,1)}, f32[2,128,1024]{2,1,0:T(8,128)}, bf16[2,128,1024]{2,1,0:T(8,128)(...) custom-call(bf16[2,128,1024]{2,1,0:T(8,128)(2,1)} %get-tuple-element.179.n_own.refs_0_, ...), custom_call_target="tpu_custom_call" | custom-call | flops 4294967296 | bytes 11534336 | tf_op jit(solution)/shard_map/feed_forward/pallas_call | solution.py:35
  222.7 10.1 %grad_feed_forward.1 = bf16[2,4,2,256,512]{4,3,2,1,0:T(8,128)(2,1)} custom-call(bf16[4,512,256]{2,1,0:T(8,128)(2,1)} %get-tuple-element.191.d_near, bf16[4,512,256]{2,1,0:T(8,128)(2,1)} %get-tuple-element.192.d_far, bf16[4,512,256]{2,1,0:T(8,128)(2,1)} %get-tuple-element.193.a_near, bf16[4,512,256]{2,1,0:T(8,128)(2,1)} %get-tuple-element.194.a_far, ...), custom_call_target="tpu_custom_call" | custom-call | flops 4294967296 | bytes 12582912 | tf_op jit(solution)/shard_map/grad_feed_forward/pallas_call | solution.py:35
  244.5 10.8 %cross_attend_back.1 = (f32[2,128,1024]{2,1,0:T(8,128)}, bf16[2,128,1024]{2,1,0:T(8,128)(2,1)}, bf16[4,512,128]{2,1,0:T(8,128)(2,1)}, bf16[4,128,512]{2,1,0:T(8,128)(2,1)}, bf16[4,128,512]{2,1,0:T(8,128)(2,1)}) custom-call(s32[2]{0:T(128)} %lengths.3, s32[4]{0:T(128)} %iota_xor_fusion.t_of, bf16[2,128,1024]{2,1,0:T(8,128)(2,1)} %get-tuple-element.197.own_in.y_own, ...), custom_call_target="tpu_custom_call" | custom-call | flops 1879048192 | bytes 8929280 | tf_op jit(solution)/shard_map/cross_attend_back/pallas_call | solution.py:35
  255.4 5.2 %grad_cross.1 = (f32[4,2,2,64,512]{4,3,2,1,0:T(8,128)}, bf16[4,384,512]{2,1,0:T(8,128)(2,1)}) custom-call(bf16[4,512,128]{2,1,0:T(8,128)(2,1)} %get-tuple-element.204.dq, bf16[4,512,128]{2,1,0:T(8,128)(2,1)} %get-tuple-element.205.o, bf16[2,128,1024]{2,1,0:T(8,128)(2,1)} %get-tuple-element.175.own_in.n_own, bf16[2,128,1024]{2,1,0:T(8,128)(2,1)} %copy-done.36, ...), custom_call_target="tpu_custom_call" | custom-call | flops 1073741824 | bytes 7340032 | tf_op jit(solution)/shard_map/grad_cross/pallas_call | solution.py:35
  291.0 11.9 %collective-permute-done.44.refs_12_ = bf16[2,128,128]{2,1,0:T(8,128)(2,1)S(1)} collective-permute-done((bf16[2,128,128]{2,1,0:T(8,128)(2,1)}, bf16[2,128,128]{2,1,0:T(8,128)(2,1)S(1)}, u32[]{:S(2)}, u32[]{:S(2)}) %collective-permute-start.44) | collective-permute-done | bytes 65568 | tf_op jit(solution)/shard_map/ppermute | solution.py:572
  308.7 23.1 %self_attend_back.1 = (bf16[16,128,384]{2,1,0:T(8,128)(2,1)}, bf16[2,4,128,1024]{3,2,1,0:T(8,128)(2,1)}, bf16[2,4,128,1024]{3,2,1,0:T(8,128)(2,1)}) custom-call(s32[2]{0:T(128)} %pad_add_fusion.at, s32[32]{0:T(128)} %pad_add_fusion.1.order, bf16[3,2048,128]{2,1,0:T(8,128)(2,1)} %get-tuple-element.227.qkv, f32[2,2048]{1,0:T(2,128)} %get-tuple-element.228.lse, ...), custom_call_target="tpu_custom_call" | custom-call | flops 6979321856 | bytes 9453568 | tf_op jit(solution)/shard_map/self_attend_back/pallas_call | solution.py:35
  354.8 6.2 %collective-permute-done.57 = bf16[256,512]{1,0:T(8,128)(2,1)S(1)} collective-permute-done((bf16[256,512]{1,0:T(8,128)(2,1)S(1)}, bf16[256,512]{1,0:T(8,128)(2,1)S(1)}, u32[]{:S(2)}, u32[]{:S(2)}) %collective-permute-start.57) | collective-permute-done | bytes 262176 | tf_op jit(solution)/shard_map/ppermute | solution.py:548
  361.1 4.3 collective-permute-done.53
  392.1 6.7 %grad_qkv.1 = (f32[384,512]{1,0:T(8,128)}, bf16[384,512]{1,0:T(8,128)(2,1)}, f32[2,1024]{1,0:T(2,128)}) custom-call(s32[2]{0:T(128)} %pad_add_fusion.at, bf16[16,128,384]{2,1,0:T(8,128)(2,1)} %get-tuple-element.233.grads, bf16[4,160,1024]{2,1,0:T(8,128)(2,1)} %copy-done.2, bf16[4,160,1024]{2,1,0:T(8,128)(2,1)} %pad_maximum_fusion.2.refs_1_, ...), custom_call_target="tpu_custom_call" | custom-call | flops 1610612736 | bytes 9052160 | tf_op jit(solution)/shard_map/grad_qkv/pallas_call | solution.py:35
  420.0 5.1 %collective-permute-done.67 = f32[6,1024]{1,0:T(8,128)S(1)} collective-permute-done((f32[6,1024]{1,0:T(8,128)S(1)}, f32[6,1024]{1,0:T(8,128)S(1)}, u32[]{:S(2)}, u32[]{:S(2)}) %collective-permute-start.67) | collective-permute-done | bytes 24608 | tf_op jit(solution)/shard_map/ppermute | solution.py:548
  (409 shorter events, 219.0 us)
Async XLA Ops:
  7.2 130.3 %all-gather.10.cloned.1.call-start = ((), (), s32[]{:S(2)}) async-start(), calls=%async_computation.3 | async-start | bytes 3538944 | tf_op jit(solution)/shard_map/all_gather | solution.py:698
  12.6 20.7 %collective-permute-start.1 = (bf16[160,1024]{1,0:T(8,128)(2,1)}, bf16[160,1024]{1,0:T(8,128)(2,1)S(1)}, u32[]{:S(2)}, u32[]{:S(2)}) collective-permute-start(bf16[160,1024]{1,0:T(8,128)(2,1)} %get-tuple-element.145), channel_id=1, source_target_pairs={{0,2},{1,3},{2,0},{3,1},{4,6},{5,7},{6,4},{7,5},{8,10},{9,11},{10,... | collective-permute-start | bytes 983048 | tf_op jit(solution)/shard_map/ppermute | solution.py:548
  16.6 31.9 %collective-permute-start.4 = (bf16[160,1024]{1,0:T(8,128)(2,1)}, bf16[160,1024]{1,0:T(8,128)(2,1)S(1)}, u32[]{:S(2)}, u32[]{:S(2)}) collective-permute-start(bf16[160,1024]{1,0:T(8,128)(2,1)} %get-tuple-element.147), channel_id=1, source_target_pairs={{0,8},{4,12},{8,0},{12,4},{1,9},{5,13},{9,1},{13,5},{2,10},{6,14},... | collective-permute-start | bytes 983048 | tf_op jit(solution)/shard_map/ppermute | solution.py:548
  18.2 30.4 %collective-permute-start = (bf16[160,1024]{1,0:T(8,128)(2,1)}, bf16[160,1024]{1,0:T(8,128)(2,1)}, u32[]{:S(2)}, u32[]{:S(2)}) collective-permute-start(bf16[160,1024]{1,0:T(8,128)(2,1)} %get-tuple-element.144), channel_id=1, source_target_pairs={{0,1},{1,0},{2,3},{3,2},{4,5},{5,4},{6,7},{7,6},{8,9},{9,8},{10,11... | collective-permute-start | bytes 983048 | tf_op jit(solution)/shard_map/ppermute | solution.py:548
  19.7 28.8 %collective-permute-start.3 = (bf16[3,64,512]{1,2,0:T(8,128)(2,1)S(1)}, bf16[3,64,512]{1,2,0:T(8,128)(2,1)S(1)}, u32[]{:S(2)}, u32[]{:S(2)}) collective-permute-start(bf16[3,64,512]{1,2,0:T(8,128)(2,1)S(1)} %pad_maximum_fusion.9), channel_id=1, source_target_pairs={{0,2},{1,3},{2,0},{3,1},{4,6},{5,7},{6,4},{7,5},{8,10},{9,11},{10,... | collective-permute-start | bytes 589832 | tf_op jit(solution)/shard_map/ppermute | solution.py:548
  50.9 150.0 %all-gather.12.cloned.1.call-start = ((), (), s32[]{:S(2)}) async-start(), calls=%async_computation.4 | async-start | bytes 4718592 | tf_op jit(solution)/shard_map/all_gather | solution.py:698
  53.3 280.7 %reduce-scatter.2.cloned.1.call-start = ((), (), s32[]{:S(2)}) async-start(), calls=%async_computation.1 | async-start | bytes 4718592 | tf_op jit(solution)/shard_map/reduce_scatter | solution.py:841
  55.3 26.4 %collective-permute-start.8 = (bf16[512,512]{1,0:T(8,128)(2,1)S(1)}, bf16[512,512]{1,0:T(8,128)(2,1)S(1)}, u32[]{:S(2)}, u32[]{:S(2)}) collective-permute-start(bf16[512,512]{1,0:T(8,128)(2,1)S(1)} %pad_maximum_fusion.4.refs_4_.refs_16_.refs_0_), channel_id=1, source_target_pairs={{0,16},{16,0},{1,17},{17,1},{2,18},{18,2},{3,19},{19,3},{4,20},{20... | collective-permute-start | bytes 1572872 | tf_op jit(solution)/shard_map/ppermute | solution.py:548
  63.1 21.3 %collective-permute-start.9 = (bf16[4,160,1024]{2,1,0:T(8,128)(2,1)S(1)}, bf16[4,160,1024]{2,1,0:T(8,128)(2,1)}, u32[]{:S(2)}, u32[]{:S(2)}) collective-permute-start(bf16[4,160,1024]{2,1,0:T(8,128)(2,1)S(1)} %pad_maximum_fusion.1.refs_0_), channel_id=1, source_target_pairs={{0,4},{4,0},{8,12},{12,8},{1,5},{5,1},{9,13},{13,9},{2,6},{6,2},{1... | collective-permute-start | bytes 3932168 | tf_op jit(solution)/shard_map/ppermute | solution.py:548
  82.3 30.0 %collective-permute-start.14 = (bf16[2,128,1024]{2,1,0:T(8,128)(2,1)S(1)}, bf16[2,128,1024]{2,1,0:T(8,128)(2,1)S(1)}, u32[]{:S(2)}, u32[]{:S(2)}) collective-permute-start(bf16[2,128,1024]{2,1,0:T(8,128)(2,1)S(1)} %copy-done.28), channel_id=1, source_target_pairs={{0,8},{4,12},{8,0},{12,4},{1,9},{5,13},{9,1},{13,5},{2,10},{6,14},... | collective-permute-start | bytes 1572872 | tf_op jit(solution)/shard_map/ppermute | solution.py:548
  172.5 28.5 %collective-permute-start.30 = (bf16[2,128,1024]{2,1,0:T(8,128)(2,1)S(1)}, bf16[2,128,1024]{2,1,0:T(8,128)(2,1)S(1)}, u32[]{:S(2)}, u32[]{:S(2)}) collective-permute-start(bf16[2,128,1024]{2,1,0:T(8,128)(2,1)S(1)} %copy-done.63), channel_id=1, source_target_pairs={{0,4},{4,0},{8,12},{12,8},{1,5},{5,1},{9,13},{13,9},{2,6},{6,2},{1... | collective-permute-start | bytes 1572872 | tf_op jit(solution)/shard_map/ppermute | solution.py:548
  185.1 25.9 %collective-permute-start.27 = (bf16[2,128,1024]{2,1,0:T(8,128)(2,1)S(1)}, bf16[2,128,1024]{2,1,0:T(8,128)(2,1)}, u32[]{:S(2)}, u32[]{:S(2)}) collective-permute-start(bf16[2,128,1024]{2,1,0:T(8,128)(2,1)S(1)} %copy-done.28), channel_id=1, source_target_pairs={{0,4},{4,0},{8,12},{12,8},{1,5},{5,1},{9,13},{13,9},{2,6},{6,2},{1... | collective-permute-start | bytes 1572872 | tf_op jit(solution)/shard_map/ppermute | solution.py:548
  185.6 25.4 %collective-permute-start.26 = (bf16[2,128,1024]{2,1,0:T(8,128)(2,1)}, bf16[2,128,1024]{2,1,0:T(8,128)(2,1)}, u32[]{:S(2)}, u32[]{:S(2)}) collective-permute-start(bf16[2,128,1024]{2,1,0:T(8,128)(2,1)} %get-tuple-element.179.n_own.refs_0_), channel_id=1, source_target_pairs={{0,4},{4,0},{8,12},{12,8},{1,5},{5,1},{9,13},{13,9},{2,6},{6,2},{1... | collective-permute-start | bytes 1572872 | tf_op jit(solution)/shard_map/ppermute | solution.py:548
  235.9 152.6 %all-gather.14.cloned.1.call-start = ((), (), s32[]{:S(2)}) async-start(), calls=%async_computation.5 | async-start | bytes 2621440 | tf_op jit(solution)/shard_map/all_gather | solution.py:844
  260.5 44.0 %collective-permute-start.37 = (bf16[4,384,512]{2,1,0:T(8,128)(2,1)}, bf16[4,384,512]{2,1,0:T(8,128)(2,1)S(1)}, u32[]{:S(2)}, u32[]{:S(2)}) collective-permute-start(bf16[4,384,512]{2,1,0:T(8,128)(2,1)} %get-tuple-element.208), channel_id=1, source_target_pairs={{0,8},{4,12},{8,0},{12,4},{1,9},{5,13},{9,1},{13,5},{2,10},{6,14},... | collective-permute-start | bytes 4718600 | tf_op jit(solution)/shard_map/ppermute | solution.py:548
  279.8 23.1 %collective-permute-start.44 = (bf16[2,128,128]{2,1,0:T(8,128)(2,1)}, bf16[2,128,128]{2,1,0:T(8,128)(2,1)S(1)}, u32[]{:S(2)}, u32[]{:S(2)}) collective-permute-start(bf16[2,128,128]{2,1,0:T(8,128)(2,1)} %get-tuple-element.218), channel_id=1, source_target_pairs={{8,0},{9,1},{10,2},{11,3},{12,4},{13,5},{14,6},{15,7},{0,8},{1,9},... | collective-permute-start | bytes 196616 | tf_op jit(solution)/shard_map/ppermute | solution.py:572
  280.4 22.5 %collective-permute-start.45 = (bf16[2,128,128]{2,1,0:T(8,128)(2,1)}, bf16[2,128,128]{2,1,0:T(8,128)(2,1)S(1)}, u32[]{:S(2)}, u32[]{:S(2)}) collective-permute-start(bf16[2,128,128]{2,1,0:T(8,128)(2,1)} %get-tuple-element.219), channel_id=1, source_target_pairs={{9,0},{8,1},{11,2},{10,3},{13,4},{12,5},{15,6},{14,7},{1,8},{0,9},... | collective-permute-start | bytes 196616 | tf_op jit(solution)/shard_map/ppermute | solution.py:572
  302.9 28.9 %collective-permute-start.49 = (bf16[4,64,1024]{2,1,0:T(8,128)(2,1)}, bf16[4,64,1024]{2,1,0:T(8,128)(2,1)}, u32[]{:S(2)}, u32[]{:S(2)}) collective-permute-start(bf16[4,64,1024]{2,1,0:T(8,128)(2,1)} %get-tuple-element.232), channel_id=1, source_target_pairs={{0,8},{4,12},{8,0},{12,4},{1,9},{5,13},{9,1},{13,5},{2,10},{6,14},... | collective-permute-start | bytes 1572872 | tf_op jit(solution)/shard_map/ppermute | solution.py:548
  308.2 23.6 %collective-permute-start.48 = (bf16[4,2,64,512]{3,2,1,0:T(8,128)(2,1)S(1)}, bf16[4,2,64,512]{3,2,1,0:T(8,128)(2,1)S(1)}, u32[]{:S(2)}, u32[]{:S(2)}) collective-permute-start(bf16[4,2,64,512]{3,2,1,0:T(8,128)(2,1)S(1)} %fusion.2), channel_id=1, source_target_pairs={{0,16},{16,0},{1,17},{17,1},{2,18},{18,2},{3,19},{19,3},{4,20},{20... | collective-permute-start | bytes 1572872 | tf_op jit(solution)/shard_map/ppermute | solution.py:548
  334.0 84.4 %all-gather.8.cloned.1.call-start = ((), (), s32[]{:S(2)}) async-start(), calls=%async_computation.2 | async-start | bytes 1310720 | tf_op jit(solution)/shard_map/all_gather | solution.py:1028
  339.6 21.3 %collective-permute-start.57 = (bf16[256,512]{1,0:T(8,128)(2,1)S(1)}, bf16[256,512]{1,0:T(8,128)(2,1)S(1)}, u32[]{:S(2)}, u32[]{:S(2)}) collective-permute-start(bf16[256,512]{1,0:T(8,128)(2,1)S(1)} %get-tuple-element.342), channel_id=1, source_target_pairs={{0,2},{1,3},{2,0},{3,1},{4,6},{5,7},{6,4},{7,5},{8,10},{9,11},{10,... | collective-permute-start | bytes 786440 | tf_op jit(solution)/shard_map/ppermute | solution.py:548
  343.2 22.1 %collective-permute-start.53 = (bf16[2,128,1024]{2,1,0:T(8,128)(2,1)S(1)}, bf16[2,128,1024]{2,1,0:T(8,128)(2,1)S(1)}, u32[]{:S(2)}, u32[]{:S(2)}) collective-permute-start(bf16[2,128,1024]{2,1,0:T(8,128)(2,1)S(1)} %pad_maximum_fusion.8), channel_id=1, source_target_pairs={{0,8},{4,12},{8,0},{12,4},{1,9},{5,13},{9,1},{13,5},{2,10},{6,14},... | collective-permute-start | bytes 1572872 | tf_op jit(solution)/shard_map/ppermute | solution.py:548
  352.6 24.7 %collective-permute-start.51 = (bf16[2,128,1024]{2,1,0:T(8,128)(2,1)S(1)}, bf16[2,128,1024]{2,1,0:T(8,128)(2,1)S(1)}, u32[]{:S(2)}, u32[]{:S(2)}) collective-permute-start(bf16[2,128,1024]{2,1,0:T(8,128)(2,1)S(1)} %pad_maximum_fusion.7), channel_id=1, source_target_pairs={{0,8},{4,12},{8,0},{12,4},{1,9},{5,13},{9,1},{13,5},{2,10},{6,14},... | collective-permute-start | bytes 1572872 | tf_op jit(solution)/shard_map/ppermute | solution.py:548
  385.7 23.6 %collective-permute-start.52 = (bf16[128,1024]{1,0:T(8,128)(2,1)}, bf16[128,1024]{1,0:T(8,128)(2,1)}, u32[]{:S(2)}, u32[]{:S(2)}) collective-permute-start(bf16[128,1024]{1,0:T(8,128)(2,1)} %get-tuple-element.325), channel_id=1, source_target_pairs={{0,1},{1,0},{2,3},{3,2},{4,5},{5,4},{6,7},{7,6},{8,9},{9,8},{10,11... | collective-permute-start | bytes 786440 | tf_op jit(solution)/shard_map/ppermute | solution.py:548
  (137 other events, 1255.2 us)
Sparse Core Ops, SparseCore 0:
  51.0 74.9 all-gather.9
  128.7 72.2 all-gather.11
  235.3 86.3 reduce-scatter.1
  334.1 28.9 all-gather.13
  377.4 20.9 all-gather.7
